TPU v7x, 32 devices: a whole 2x2x4 slice. The times are simulated.
32 devices in a mesh: dp: 8 (over z, y), expert: 4 (over x, core).
Axes of the slice: x: 2, y: 2, z: 4, core: 2. Of those that a mesh axis runs over, the one named last changes fastest.
Arguments:
- hidden: bfloat16 [4, 1024, 8192], P('expert', None, 'dp'), may hold values from -6 to 6
- down_weight: bfloat16 [4, 8192, 6144], P('expert', 'dp'), may hold values from -0.0625 to 0.0625
- grad_out: bfloat16 [1024, 6144], P('dp', 'expert'), may hold values from -2 to 2
- routing: int32 [1024, 2], P('dp'), may hold values from 0 to 3, all different within a row; in each aligned block of 128 rows (0 to 127, 128 to 255, ...) at most 128 rows name the same one
- gates: float32 [1024, 2], P('dp'), may hold values from 0.25 to 1
Outputs:
- mixed_out: bfloat16 [1024, 6144], P('dp', 'expert')
- grad_hidden: bfloat16 [4, 1024, 8192], P('expert', None, 'dp')
- grad_weight: bfloat16 [4, 8192, 6144], P('expert', 'dp')
Inputs may be any that keep to these rules, and one draw needn't show every extreme that they name: `routing`: among the 128 tokens of one sequence shard (aligned blocks of rows), each expert is named by at most 128 tokens, a bound that some block reaches; a token names 2 different experts.
All inputs are finite; a program needn't handle non-finite values.
Results may differ from a plain program's by a relative error of at most 0.017.
Values may be sent and summed in bfloat16 or wider, within the bound.
No kernel may reach another device: no remote copies, remote signals or barrier semaphores. Data moves between devices by JAX's collectives and lax.ppermute only.
A program may use at most 128 MiB of HBM per device.

v0:
```python
import jax
import jax.numpy as jnp
from jax import lax
from jax.sharding import PartitionSpec as P


def dispatch_weights(routing, gates, experts, capacity):
    flattened = routing.reshape(-1)
    onehot = (flattened[:, None] == jnp.arange(experts, dtype=jnp.int32)[None, :]).astype(jnp.int32)
    position = jnp.sum((jnp.cumsum(onehot, axis=0) - onehot) * onehot, axis=1)
    target = flattened * capacity + position
    picked = (jnp.arange(experts * capacity, dtype=jnp.int32)[:, None] == target[None, :]).astype(
        jnp.float32
    )
    picked = picked * gates.reshape(-1)[None, :]
    return jnp.sum(picked.reshape(experts * capacity, routing.shape[0], routing.shape[1]), axis=2)


def body(hidden, down_weight, grad_out, routing, gates):
    highest = lax.Precision.HIGHEST
    groups = lax.axis_size("dp")
    owners = lax.axis_size("expert")
    experts = hidden.shape[0] * owners
    slot_total = hidden.shape[1]
    capacity = slot_total // groups
    dispatch = dispatch_weights(routing, gates, experts, capacity)
    hidden_rows = hidden[0]
    weight = down_weight[0]
    partial_value = jnp.dot(hidden_rows, weight, preferred_element_type=jnp.float32).astype(
        jnp.bfloat16
    )
    partial_value = partial_value.reshape(1, groups, capacity, partial_value.shape[-1])
    spread = lax.all_to_all(partial_value, "expert", split_axis=3, concat_axis=0, tiled=True)
    summed = lax.psum_scatter(spread, "dp", scatter_dimension=1, tiled=True).astype(jnp.float32)
    outputs = summed.astype(jnp.bfloat16)
    flat_outputs = outputs.reshape(experts * capacity, outputs.shape[-1]).astype(jnp.float32)
    mixed_out = lax.dot_general(dispatch, flat_outputs, (((0,), (0,)), ((), ())), precision=highest)
    mixed_out = mixed_out.astype(jnp.bfloat16)
    routed = jnp.dot(dispatch, grad_out.astype(jnp.float32), precision=highest).astype(jnp.bfloat16)
    routed = routed.reshape(experts, capacity, routed.shape[-1])
    shards = lax.all_gather(routed, "dp", axis=1, tiled=True)
    gathered = lax.all_to_all(shards, "expert", split_axis=0, concat_axis=2, tiled=True)
    grad_rows = gathered[0]
    hidden_acc = lax.dot_general(
        grad_rows, weight, (((1,), (1,)), ((), ())), preferred_element_type=jnp.float32
    )
    weight_acc = lax.dot_general(
        hidden_rows, grad_rows, (((0,), (0,)), ((), ())), preferred_element_type=jnp.float32
    )
    grad_hidden = hidden_acc.astype(jnp.bfloat16)[None]
    grad_weight = weight_acc.astype(jnp.bfloat16)[None]
    return (mixed_out, grad_hidden, grad_weight)


def solution(mesh):
    return jax.shard_map(
        body,
        mesh=mesh,
        in_specs=(
            P("expert", None, "dp"),
            P("expert", "dp", None),
            P("dp", "expert"),
            P("dp", None),
            P("dp", None),
        ),
        out_specs=(P("dp", "expert"), P("expert", None, "dp"), P("expert", "dp", None)),
        check_vma=False,
    )
```

profile of v0, /device:TPU:0, one launch (start us, length us, event | category | flops | bytes accessed | tf_op | source)
XLA Modules:
  0.0 426.2 jit_solution(15726662962249973861)
XLA Ops:
  7.2 0.0 copy-start
  7.2 0.0 all-gather.2.cloned.1.call-start
  7.2 0.9 copy.57
  8.2 0.1 eq.44
  8.3 0.1 eq.40
  8.4 1.2 reduce-window.6
  9.7 0.1 slice.8
  9.7 0.1 copy.59
  9.9 0.1 copy.60
  10.0 0.1 add_bitcast_fusion
  10.1 0.1 reduce_sum.21
  10.2 0.1 copy.61
  10.3 0.7 multiply_add_fusion
  11.0 0.8 select_reduce_fusion
  11.8 3.5 convolution_convert_fusion
  15.3 2.6 copy.65
  17.9 0.0 all-gather.2.cloned.1.call-update
  18.0 0.0 reduce-scatter.2.cloned.1.call-start
  18.0 0.0 copy-done
  18.0 20.0 %fusion.4 = bf16[1024,6144]{1,0:T(8,128)(2,1)} fusion(bf16[1,1024,6144]{2,1,0:T(8,128)(2,1)} %param.6, bf16[1,1024,1024]{2,1,0:T(8,128)(2,1)S(1)} %copy-done), kind=kOutput, calls=%fused_computation.5 | convolution fusion | flops 12891193344 | bytes 27262976 | tf_op jit(solution)/shard_map/dot_general | solution.py:29
  38.0 16.7 %copy.62 = bf16[1,8,128,6144]{2,1,0,3:T(8,128)(2,1)} copy(bf16[1,8,128,6144]{3,2,1,0:T(8,128)(2,1)} %bitcast.61) | data formatting | bytes 25165824 | tf_op jit(solution)/shard_map/reshape | solution.py:32
  54.7 143.1 %all_to_all.33 = bf16[1,8,128,6144]{2,1,0,3:T(8,128)(2,1)S(1)} all-to-all(bf16[1,8,128,6144]{2,1,0,3:T(8,128)(2,1)} %copy.62), channel_id=1, replica_groups=mesh['dp'=8,'expert'=4] {'expert'}, dimensions={3} | all-to-all | bytes 25165824 | tf_op jit(solution)/shard_map/all_to_all | solution.py:33
  197.8 7.4 %copy.63 = bf16[1,8,128,6144]{2,3,1,0:T(8,128)(2,1)} copy(bf16[1,8,128,6144]{2,1,0,3:T(8,128)(2,1)S(1)} %all_to_all.33) | data formatting | bytes 25165824 | tf_op jit(solution)/shard_map/all_to_all | solution.py:33
  205.1 0.0 reduce-scatter.2.cloned.1.call-update
  205.2 0.0 all-gather.2.cloned.1.call-done
  205.2 147.4 %all_to_all.34 = bf16[4,1024,1536]{1,2,0:T(8,128)(2,1)} all-to-all(bf16[4,1024,1536]{1,2,0:T(8,128)(2,1)} %all-gather.2.cloned.1.call-done), channel_id=1, replica_groups=mesh['dp'=8,'expert'=4] {'expert'}, dimensions={0} | all-to-all | bytes 25165824 | tf_op jit(solution)/shard_map/all_to_all | solution.py:42
  352.6 20.1 %convert_bitcast_fusion = bf16[1,1024,6144]{1,2,0:T(8,128)(2,1)} fusion(bf16[1024,6144]{0,1:T(8,128)(2,1)} %bitcast.59, bf16[1,1024,1024]{2,1,0:T(8,128)(2,1)S(1)} %copy-done), kind=kOutput, calls=%fused_computation.4 | convolution fusion | flops 12891193344 | bytes 27262976 | tf_op jit(solution)/shard_map/dot_general | solution.py:47
  372.7 16.6 %copy.66 = bf16[1,1024,6144]{2,1,0:T(8,128)(2,1)} copy(bf16[1,1024,6144]{1,2,0:T(8,128)(2,1)} %convert_bitcast_fusion) | data formatting | bytes 25165824
  389.4 19.0 %convert_bitcast_fusion.1 = bf16[1,1024,1024]{2,1,0:T(8,128)(2,1)} fusion(bf16[1024,6144]{0,1:T(8,128)(2,1)} %bitcast.60, bf16[1,1024,6144]{2,1,0:T(8,128)(2,1)} %param.6), kind=kOutput, calls=%fused_computation.10 | convolution fusion | flops 12885950464 | bytes 27262976 | tf_op jit(solution)/shard_map/dot_general | solution.py:44
  408.4 5.4 %reduce-scatter.2.cloned.1.call-done = bf16[4,1,128,1536]{2,3,0,1:T(8,128)(2,1)} async-done(((bf16[4,8,128,1536]{2,3,0,1:T(8,128)(2,1)}), bf16[4,1,128,1536]{2,3,0,1:T(8,128)(2,1)}) %reduce-scatter.2.cloned.1.call-update) | async-done | bytes 1572880 | tf_op jit(solution)/shard_map/reduce_scatter | solution.py:34
  413.8 2.6 copy.64
  416.4 3.0 convolution_convert_fusion.1
  (6 shorter events, 0.1 us)
Async XLA Ops:
  7.2 10.8 %copy-start = (bf16[1,1024,1024]{2,1,0:T(8,128)(2,1)S(1)}, bf16[1,1024,1024]{2,1,0:T(8,128)(2,1)}, u32[]{:S(2)}) copy-start(bf16[1,1024,1024]{2,1,0:T(8,128)(2,1)} %param.5) | copy-start | bytes 6291460
  7.2 198.0 %all-gather.2.cloned.1.call-start = ((), (), s32[]{:S(2)}) async-start(), calls=%async_computation.4 | async-start | bytes 14155776 | tf_op jit(solution)/shard_map/all_gather | solution.py:41
  18.0 395.8 %reduce-scatter.2.cloned.1.call-start = ((), (), s32[]{:S(2)}) async-start(), calls=%async_computation.3 | async-start | bytes 14155776 | tf_op jit(solution)/shard_map/reduce_scatter | solution.py:34
  389.4 30.0 %copy-start.1 = (bf16[1,1024,1024]{2,1,0:T(8,128)(2,1)S(1)}, bf16[1,1024,1024]{2,1,0:T(8,128)(2,1)}, u32[]{:S(2)}) copy-start(bf16[1,1024,1024]{2,1,0:T(8,128)(2,1)} %param.5) | copy-start | bytes 6291460
Sparse Core Ops, SparseCore 0:
  18.1 179.2 all-gather.1
  205.3 208.4 reduce-scatter.1
where the time goes:
time: 428 us; the launch traced here: 426 us
  blocking collectives  291 us (68%)
  matrix products  65.7 us (15%)
  local copies, waits for them, and re-layouts  47.6 us (11%)
  between operations  14.1 us (3%)
  waiting for transfers between devices  5.45 us (1%)
    all_to_all x1, blocking collectives, body(): lax.all_to_all(shards, 'expert', split_axis=0, concat_axis=2, tiled=True)  147 us
    all_to_all x1, blocking collectives, body(): lax.all_to_all(partial_value, 'expert', split_axis=3, concat_axis=0, tile...  143 us
    dot_general x1, matrix products, body(): lax.dot_general(hidden_rows, grad_rows, (((0,), (0,)), ((), ())), preferr...  20.1 us
    dot_general x1, matrix products, body(): jnp.dot(hidden_rows, weight, preferred_element_type=jnp.float32)  20 us
    dot_general x1, matrix products, body(): lax.dot_general(grad_rows, weight, (((1,), (1,)), ((), ())), preferred_el...  19 us
    unnamed x6, local copies, waits for them, and re-layouts  17.6 us
    reshape x1, local copies, waits for them, and re-layouts, body(): partial_value.reshape(1, groups, capacity, partial_value.shape[-1])  16.7 us
  transfers between devices with their start and end apart: 2, of which 1 were waited for; matrix products, arithmetic and copies ran while one was open for 23% of the time, Pallas kernels for 0%

commit v1 on v0

v1 whole, which is shorter than its diff:
```python
import functools
import jax
import jax.numpy as jnp
from jax import lax
from jax.experimental import pallas as pl
from jax.experimental.pallas import tpu as pltpu
from jax.sharding import PartitionSpec as P

BF16, F32 = jnp.bfloat16, jnp.float32


class Ring:
    def __init__(self, name, total, size, inner):
        self.name, self.size = name, size
        self.perm = []
        for i in range(total):
            here = (i // inner) % size
            self.perm.append((i, i + (((here + 1) % size) - here) * inner))
        self.place = (lax.axis_index(name) // inner) % size

    def shift(self, block):
        return lax.ppermute(block, self.name, self.perm)

    def gather(self, block):
        blocks = [block]
        for _ in range(self.size - 1):
            blocks.append(self.shift(blocks[-1]))
        return blocks

    def scatter(self, blocks):
        if self.size == 1:
            return blocks[0]
        total = blocks[1]
        for j in list(range(2, self.size)) + [0]:
            total = blocks[j] + self.shift(total)
        return total


def tile_of(width, most=512):
    tile = most
    while width % tile:
        tile -= 128
    return tile


def forward_kernel(quarter, rows, weight, *rest):
    out = rest[-1]
    acc = jnp.dot(rows[...], weight[...], preferred_element_type=F32)
    if len(rest) == 2:
        acc = acc + rest[0][0].astype(F32)
    out[0] = acc.astype(BF16)


def forward(rows, weight, quarters, extra=None):
    count = quarters.shape[0]
    tokens, depth = rows.shape
    width = weight.shape[1] // (lax.axis_size("expert"))
    tile = tile_of(width)
    per = width // tile
    specs = [
        pl.BlockSpec((tokens, depth), lambda i, j, q: (0, 0)),
        pl.BlockSpec((depth, tile), lambda i, j, q: (0, q[i] * per + j)),
    ]
    operands = [rows, weight]
    block = pl.BlockSpec((1, tokens, tile), lambda i, j, q: (i, 0, j))
    if extra is not None:
        specs.append(block)
        operands.append(extra)
    return pl.pallas_call(
        forward_kernel,
        grid_spec=pltpu.PrefetchScalarGridSpec(
            num_scalar_prefetch=1, grid=(count, per), in_specs=specs, out_specs=block
        ),
        out_shape=jax.ShapeDtypeStruct((count, tokens, width), BF16),
        compiler_params=pltpu.CompilerParams(vmem_limit_bytes=40 * 2**20),
        cost_estimate=pl.CostEstimate(
            flops=2 * tokens * depth * width * count,
            bytes_accessed=2 * (tokens * depth + count * width * (depth + tokens)),
            transcendentals=0,
        ),
        name="forward_rows",
    )(quarters, *operands)


def backward_kernel(steps, first, last, quarter, rows, grads, weight, *rest):
    rest = list(rest)
    gates = rest.pop(0) if last else None
    if not first:
        before, _ = rest.pop(0), rest.pop(0)
    weight_out, hidden_out, turned, total = rest
    step = pl.program_id(0) * pl.num_programs(1) + pl.program_id(1)

    @pl.when(step == 0)
    def _():
        turned[...] = rows[...].T
        total[...] = jnp.zeros_like(total) if first else before[...]

    block = grads[0]
    weight_out[...] = jnp.dot(turned[...], block, preferred_element_type=F32).astype(BF16)
    total[...] += lax.dot_general(
        block, weight[...], (((1,), (1,)), ((), ())), preferred_element_type=F32
    )

    @pl.when(step == steps - 1)
    def _():
        if last:
            hidden_out[...] = (total[...] * gates[...]).astype(BF16)
        else:
            hidden_out[...] = total[...]


def backward(rows, grads, weight, quarters, gates, before):
    count, tokens, width = grads.shape
    depth = rows.shape[1]
    tile = tile_of(width)
    per = width // tile
    first, last = before is None, gates is not None
    whole = lambda shape: pl.BlockSpec(shape, lambda i, j, q: (0, 0))
    specs = [
        whole((tokens, depth)),
        pl.BlockSpec((1, tokens, tile), lambda i, j, q: (i, 0, j)),
        pl.BlockSpec((depth, tile), lambda i, j, q: (0, q[i] * per + j)),
    ]
    operands = [rows, grads, weight]
    aliases = {}
    if last:
        specs.append(whole((tokens, 1)))
        operands.append(gates)
    if not first:
        specs += [whole((tokens, depth)), pl.BlockSpec(memory_space=pl.ANY)]
        operands += [before[1], before[0]]
        aliases = {len(operands): 0}
    return pl.pallas_call(
        functools.partial(backward_kernel, count * per, first, last),
        grid_spec=pltpu.PrefetchScalarGridSpec(
            num_scalar_prefetch=1,
            grid=(count, per),
            in_specs=specs,
            out_specs=[
                pl.BlockSpec((depth, tile), lambda i, j, q: (0, q[i] * per + j)),
                whole((tokens, depth)),
            ],
            scratch_shapes=[pltpu.VMEM((depth, tokens), BF16), pltpu.VMEM((tokens, depth), F32)],
        ),
        out_shape=[
            jax.ShapeDtypeStruct(weight.shape, BF16),
            jax.ShapeDtypeStruct((tokens, depth), BF16 if last else F32),
        ],
        input_output_aliases=aliases,
        compiler_params=pltpu.CompilerParams(vmem_limit_bytes=48 * 2**20),
        cost_estimate=pl.CostEstimate(
            flops=4 * tokens * depth * width * count,
            bytes_accessed=2 * (2 * tokens * depth + count * width * (2 * depth + tokens)),
            transcendentals=0,
        ),
        name="backward_rows",
    )(quarters, *operands)


def routes(routing, gates, experts):
    flattened = routing.reshape(-1)
    onehot = (flattened[:, None] == jnp.arange(experts, dtype=jnp.int32)[None, :]).astype(jnp.int32)
    before = jnp.cumsum(onehot, axis=0) - onehot
    slot = jnp.where(onehot > 0, before + 1, 0).reshape(routing.shape + (experts,)).sum(axis=1) - 1
    gate = (onehot.reshape(routing.shape + (experts,)) * gates[:, :, None]).sum(axis=1)
    return jnp.stack([slot.astype(F32).T, gate.T])


def body(hidden, down_weight, grad_out, routing, gates):
    groups, owners = lax.axis_size("dp"), lax.axis_size("expert")
    cores = 2 if owners % 2 == 0 else 1
    nx = owners // cores
    ny = nx if groups % nx == 0 else 1
    nz = groups // ny
    ring_c = Ring("expert", owners, cores, 1)
    ring_x = Ring("expert", owners, nx, cores)
    ring_y = Ring("dp", groups, ny, 1)
    ring_z = Ring("dp", groups, nz, ny)
    rows, width = grad_out.shape
    slots = hidden.shape[1]
    capacity = slots // groups
    experts = hidden.shape[0] * owners
    hidden_rows, weight = hidden[0], down_weight[0]
    third = rows // 4
    pair = (rows - third) // 2
    parts = {"a": (0, pair), "b": (pair, 2 * pair), "c": (2 * pair, rows)}

    late = list(range(1, nz)) + [0]
    turns = [late[: nz // 2], late[nz // 2 :]] if nz > 1 else [late]
    order = []
    starts = {}
    at = 0
    for part in "ab":
        for turn_at, turn in enumerate(turns):
            starts[part, turn_at] = at
            for jy in range(ny):
                for jz in turn:
                    order.append((part, jz, jy))
                    at += pair
    starts["c"] = at
    for jz in range(nz):
        for jy in range(ny):
            order.append(("c", jz, jy))

    have = {}
    c_x = jnp.stack(ring_x.gather(grad_out[2 * pair :]))
    c_y = jnp.stack(ring_y.gather(c_x))
    c_z = ring_z.gather(c_y)
    for jz in range(nz):
        for jy in range(ny):
            have["c", jz, jy] = [c_z[jz][jy, jx] for jx in range(nx)]
    ab = ring_z.gather(grad_out[: 2 * pair])
    early = list(range(nz))
    for turn in [early[: nz // 2], early[nz // 2 :]] if nz > 1 else [early]:
        a = jnp.stack([ab[jz][:pair] for jz in turn])
        b = jnp.stack([ab[jz][pair:] for jz in turn])
        a_xy = ring_x.gather(jnp.stack(ring_y.gather(a)))
        b_yx = ring_y.gather(jnp.stack(ring_x.gather(b)))
        for i, jz in enumerate(turn):
            for jy in range(ny):
                have["a", jz, jy] = [a_xy[jx][jy, i] for jx in range(nx)]
                have["b", jz, jy] = [b_yx[jy][jx, i] for jx in range(nx)]
    grads = jnp.stack([jnp.concatenate([have[key][jx] for key in order]) for jx in range(nx)])

    expert = lax.axis_index("expert")
    table = lax.all_gather(routes(routing, gates, experts), "dp")
    table = lax.dynamic_index_in_dim(table, expert, axis=2, keepdims=False)
    shard = jnp.arange(groups, dtype=F32)[:, None]
    slot = jnp.where(table[:, 0] >= 0, table[:, 0] + shard * capacity, -1.0)
    table = jnp.stack([slot, table[:, 1]])
    table = table.reshape(2, nz, ny, rows)
    back_z = (ring_z.place - jnp.arange(nz)) % nz
    back_y = (ring_y.place - jnp.arange(ny)) % ny
    table = table[:, back_z][:, :, back_y]
    table = jnp.concatenate(
        [table[:, jz, jy, parts[part][0] : parts[part][1]] for part, jz, jy in order], axis=1
    )
    slot_of, gate_of = table[0].astype(jnp.int32), table[1]
    chosen = slot_of[:, None] == jnp.arange(slots, dtype=jnp.int32)[None, :]
    chosen = chosen.astype(BF16)
    gate_column = gate_of[:, None]
    rows_in = jnp.dot(chosen, hidden_rows, preferred_element_type=F32)
    rows_in = (rows_in * gate_column).astype(BF16)

    back_x = (ring_x.place - jnp.arange(nx)) % nx * cores
    mine = (back_x + ring_c.place).astype(jnp.int32)
    theirs = [(back_x + (ring_c.place - jc) % cores).astype(jnp.int32) for jc in range(1, cores)]
    if cores > 1:
        partial = forward(rows_in, weight, theirs[0])
        partial = forward(rows_in, weight, mine, ring_c.shift(partial))
    else:
        partial = forward(rows_in, weight, mine)
    sums = {}
    for turn_at, turn in enumerate(turns):
        size = len(turn) * pair
        start = starts["a", turn_at]
        a = ring_x.scatter([partial[jx, start : start + ny * size] for jx in range(nx)])
        a = ring_y.scatter([a[jy * size : (jy + 1) * size] for jy in range(ny)])
        start = starts["b", turn_at]
        b = ring_y.scatter(
            [partial[:, start + jy * size : start + (jy + 1) * size] for jy in range(ny)]
        )
        b = ring_x.scatter([b[jx] for jx in range(nx)])
        for i, jz in enumerate(turn):
            span = slice(i * pair, (i + 1) * pair)
            sums[jz] = jnp.concatenate([a[span], b[span]])
    ab_sum = ring_z.scatter([sums[jz] for jz in range(nz)])
    size = ny * third
    start = starts["c"]
    c = ring_z.scatter([partial[:, start + jz * size : start + (jz + 1) * size] for jz in range(nz)])
    c = ring_y.scatter([c[:, jy * third : (jy + 1) * third] for jy in range(ny)])
    c = ring_x.scatter([c[jx] for jx in range(nx)])
    mixed_out = jnp.concatenate([ab_sum, c])

    if cores > 1:
        before = backward(rows_in, grads, weight, mine, None, None)
        grad_weight, back = backward(
            rows_in, ring_c.shift(grads), weight, theirs[0], gate_column, before
        )
    else:
        grad_weight, back = backward(rows_in, grads, weight, mine, gate_column, None)
    grad_hidden = lax.dot_general(
        chosen, back, (((0,), (0,)), ((), ())), preferred_element_type=F32
    ).astype(BF16)
    return (mixed_out, grad_hidden[None], grad_weight[None])


def solution(mesh):
    return jax.shard_map(
        body,
        mesh=mesh,
        in_specs=(
            P("expert", None, "dp"),
            P("expert", "dp", None),
            P("dp", "expert"),
            P("dp", None),
            P("dp", None),
        ),
        out_specs=(P("dp", "expert"), P("expert", None, "dp"), P("expert", "dp", None)),
        check_vma=False,
    )
```

time: 428 us -> 250 us (0.58)
  blocking collectives: 291 us -> 30.4 us
  waiting for transfers between devices: 5.45 us -> 111 us
  Pallas kernels: 0 us -> 62 us
  matrix products: 65.7 us -> 6.21 us
  local copies, waits for them, and re-layouts: 47.6 us -> 8.84 us
  starting transfers between devices: 0.08 us -> 21.3 us
  between operations: 14.1 us -> 1.46 us
  other arithmetic: 2.84 us -> 7.8 us
    all_to_all x2 -> x0, blocking collectives: 291 us -> none  [the longest x1 147 us: body(): lax.all_to_all(shards, 'expert', split_axis=0, concat_axis=2, tiled=True)]
    ppermute x0 -> x34, waiting for transfers between devices: none -> 111 us  [shift(): return lax.ppermute(block, self.name, self.perm)]
    pallas_call x0 -> x4, Pallas kernels: none -> 62 us  [the longest x2 39.9 us: backward(): pl.pallas_call(functools.partial(backward_kernel, count * per, first, las...]
    dot_general x5 -> x2, matrix products: 65.7 us -> 6.21 us  [the longest x1 3.83 us: body(): lax.dot_general(chosen, back, (((0,), (0,)), ((), ())), preferred_element...]
    all_gather x0 -> x1, blocking collectives: none -> 30.4 us  [body(): table = lax.all_gather(routes(routing, gates, experts), 'dp')]
    ppermute x0 -> x34, starting transfers between devices: none -> 21.3 us  [shift(): return lax.ppermute(block, self.name, self.perm)]
    reshape x2 -> x0, local copies, waits for them, and re-layouts: 19.3 us -> none  [the longest x1 16.7 us: body(): partial_value.reshape(1, groups, capacity, partial_value.shape[-1])]
    unnamed x6 -> x47, local copies, waits for them, and re-layouts: 17.6 us -> 3.94 us
  transfers between devices with their start and end apart: 2 -> 34, of which waited for: 1 -> 20; matrix products, arithmetic and copies ran while one was open for 23% -> 7% of each run, Pallas kernels for 0% -> 21%
where the time goes in v1:
time: 250 us; the launch traced here: 249 us
  waiting for transfers between devices  111 us (44%)
  Pallas kernels  62 us (25%)
  blocking collectives  30.4 us (12%)
  starting transfers between devices  21.3 us (9%)
  local copies, waits for them, and re-layouts  8.84 us (4%)
  other arithmetic  7.8 us (3%)
  matrix products  6.21 us (2%)
    ppermute x34, waiting for transfers between devices, shift(): return lax.ppermute(block, self.name, self.perm)  111 us
    pallas_call x2, Pallas kernels, backward(): pl.pallas_call(functools.partial(backward_kernel, count * per, first, las...  39.9 us
    all_gather x1, blocking collectives, body(): table = lax.all_gather(routes(routing, gates, experts), 'dp')  30.4 us
    pallas_call x2, Pallas kernels, forward(): pl.pallas_call(forward_kernel, grid_spec=pltpu.PrefetchScalarGridSpec(num...  22.2 us
    ppermute x34, starting transfers between devices, shift(): return lax.ppermute(block, self.name, self.perm)  21.3 us
  transfers between devices with their start and end apart: 34, of which 20 were waited for; matrix products, arithmetic and copies ran while one was open for 7% of the time, Pallas kernels for 21%

profile of v1, /device:TPU:0, one launch (start us, length us, event | category | flops | bytes accessed | tf_op | source)
XLA Modules:
  0.0 249.4 jit_solution(15751385829352695682)
XLA Ops:
  1.8 3.1 %collective-permute-start.17 = (bf16[96,1536]{1,0:T(8,128)(2,1)S(1)}, bf16[96,1536]{1,0:T(8,128)(2,1)S(1)}, u32[]{:S(2)}, u32[]{:S(2)}) collective-permute-start(bf16[96,1536]{1,0:T(8,128)(2,1)S(1)} %slice.426), channel_id=1, source_target_pairs={{0,8},{4,12},{8,16},{12,20},{16,24},{20,28},{24,0},{28,4},{1,9},{5... | collective-permute-start | bytes 884744 | tf_op jit(solution)/shard_map/ppermute | solution.py:22
  5.8 1.6 collective-permute-start.26
  11.3 30.4 %all-gather = f32[16,4,128]{2,1,0:T(4,128)S(1)} all-gather(f32[2,4,128]{2,1,0:T(4,128)S(1)} %pad_maximum_fusion.14), channel_id=2, replica_groups=mesh['dp'=8,'expert'=4] {'dp'}, dimensions={0}, use_global_device_ids=true | all-gather | bytes 36864 | tf_op jit(solution)/shard_map/all_gather | solution.py:226
  43.4 2.4 multiply_convert_fusion.rows
  45.8 11.5 %forward_rows.2 = bf16[2,1024,1536]{2,1,0:T(8,128)(2,1)} custom-call(s32[2]{0:T(128)S(1)} %broadcast_add_fusion.1.quarter, bf16[1024,1024]{1,0:T(8,128)(2,1)S(1)} %multiply_convert_fusion.rows, bf16[1024,6144]{1,0:T(8,128)(2,1)} %bitcast.321), custom_call_target="tpu_custom_call" | custom-call | flops 6442450944 | bytes 14680064 | tf_op jit(solution)/shard_map/forward_rows/pallas_call | solution.py:69
  58.2 1.6 collective-permute-start.20
  60.5 4.9 %collective-permute-done.27 = bf16[2,32,1536]{2,1,0:T(8,128)(2,1)S(1)} collective-permute-done((bf16[2,32,1536]{2,1,0:T(8,128)(2,1)S(1)}, bf16[2,32,1536]{2,1,0:T(8,128)(2,1)S(1)}, u32[]{:S(2)}, u32[]{:S(2)}) %collective-permute-start.27) | collective-permute-done | bytes 196640 | tf_op jit(solution)/shard_map/ppermute | solution.py:22
  65.5 5.8 %collective-permute-done.20 = bf16[2,48,1536]{2,1,0:T(8,128)(2,1)S(1)} collective-permute-done((bf16[2,48,1536]{2,1,0:T(8,128)(2,1)S(1)}, bf16[2,48,1536]{2,1,0:T(8,128)(2,1)S(1)}, u32[]{:S(2)}, u32[]{:S(2)}) %collective-permute-start.20) | collective-permute-done | bytes 294944 | tf_op jit(solution)/shard_map/ppermute | solution.py:22
  72.6 11.3 %collective-permute-done.18 = bf16[96,1536]{1,0:T(8,128)(2,1)S(1)} collective-permute-done((bf16[96,1536]{1,0:T(8,128)(2,1)S(1)}, bf16[96,1536]{1,0:T(8,128)(2,1)S(1)}, u32[]{:S(2)}, u32[]{:S(2)}) %collective-permute-start.18) | collective-permute-done | bytes 294944 | tf_op jit(solution)/shard_map/ppermute | solution.py:22
  84.0 11.6 %collective-permute-done.19 = bf16[96,1536]{1,0:T(8,128)(2,1)S(1)} collective-permute-done((bf16[96,1536]{1,0:T(8,128)(2,1)S(1)}, bf16[96,1536]{1,0:T(8,128)(2,1)S(1)}, u32[]{:S(2)}, u32[]{:S(2)}) %collective-permute-start.19) | collective-permute-done | bytes 294944 | tf_op jit(solution)/shard_map/ppermute | solution.py:22
  96.4 5.1 %collective-permute-done.29 = bf16[2,2,32,1536]{3,2,1,0:T(8,128)(2,1)S(1)} collective-permute-done((bf16[2,2,32,1536]{3,2,1,0:T(8,128)(2,1)S(1)}, bf16[2,2,32,1536]{3,2,1,0:T(8,128)(2,1)S(1)}, u32[]{:S(2)}, u32[]{:S(2)}) %collective-permute-start.29) | collective-permute-done | bytes 393248 | tf_op jit(solution)/shard_map/ppermute | solution.py:22
  102.7 6.5 %collective-permute-done.24 = bf16[2,48,1536]{2,1,0:T(8,128)(2,1)S(1)} collective-permute-done((bf16[2,48,1536]{2,1,0:T(8,128)(2,1)S(1)}, bf16[2,48,1536]{2,1,0:T(8,128)(2,1)S(1)}, u32[]{:S(2)}, u32[]{:S(2)}) %collective-permute-start.24) | collective-permute-done | bytes 294944 | tf_op jit(solution)/shard_map/ppermute | solution.py:22
  110.4 10.4 %collective-permute-done.32 = bf16[2,2,48,1536]{3,2,1,0:T(8,128)(2,1)S(1)} collective-permute-done((bf16[2,2,48,1536]{3,2,1,0:T(8,128)(2,1)S(1)}, bf16[2,2,48,1536]{3,2,1,0:T(8,128)(2,1)S(1)}, u32[]{:S(2)}, u32[]{:S(2)}) %collective-permute-start.32) | collective-permute-done | bytes 589856 | tf_op jit(solution)/shard_map/ppermute | solution.py:22
  121.4 3.2 %pad_maximum_fusion.grads = bf16[2,1024,1536]{2,1,0:T(8,128)(2,1)} fusion(bf16[1,1024,1536]{2,1,0:T(8,128)(2,1)S(1)} %bitcast.326, bf16[1,1024,1536]{2,1,0:T(8,128)(2,1)S(1)} %bitcast.325), kind=kLoop, calls=%fused_computation.2 | loop fusion | flops 3145728 | bytes 12582912 | tf_op jit(solution)/shard_map/stack | solution.py:223
  124.6 10.7 %forward_rows.3 = bf16[2,1024,1536]{2,1,0:T(8,128)(2,1)S(1)} custom-call(s32[2]{0:T(128)S(1)} %broadcast_add_fusion.2.quarter, bf16[1024,1024]{1,0:T(8,128)(2,1)S(1)} %copy-done.3, bf16[1024,6144]{1,0:T(8,128)(2,1)} %bitcast.322, bf16[2,1024,1536]{2,1,0:T(8,128)(2,1)} %collective-permute-done.rest_0_), custom_call_target="tpu_custom_call" | custom-call | flops 6442450944 | bytes 14680064 | tf_op jit(solution)/shard_map/forward_rows/pallas_call | solution.py:69
  136.1 1.5 collective-permute-start.5
  137.5 20.0 %backward_rows.2 = (bf16[1024,6144]{1,0:T(8,128)(2,1)}, f32[1024,1024]{1,0:T(8,128)}) custom-call(s32[2]{0:T(128)S(1)} %broadcast_add_fusion.2.quarter, bf16[1024,1024]{1,0:T(8,128)(2,1)S(1)} %copy-done.3, bf16[2,1024,1536]{2,1,0:T(8,128)(2,1)} %pad_maximum_fusion.grads, bf16[1024,6144]{1,0:T(8,128)(2,1)} %bitcast.323), custom_call_target="tpu_custom_call" | custom-call | flops 12884901888 | bytes 23068672 | tf_op jit(solution)/shard_map/backward_rows/pallas_call | solution.py:133
  160.2 13.6 %collective-permute-done.3 = bf16[2,96,1536]{2,1,0:T(8,128)(2,1)S(1)} collective-permute-done((bf16[2,96,1536]{2,1,0:T(8,128)(2,1)S(1)}, bf16[2,96,1536]{2,1,0:T(8,128)(2,1)S(1)}, u32[]{:S(2)}, u32[]{:S(2)}) %collective-permute-start.3) | collective-permute-done | bytes 589856 | tf_op jit(solution)/shard_map/ppermute | solution.py:22
  175.1 1.5 collective-permute-start.7
  176.7 3.4 %collective-permute-done.2 = bf16[96,1536]{1,0:T(8,128)(2,1)S(1)} collective-permute-done((bf16[96,1536]{1,0:T(8,128)(2,1)S(1)}, bf16[96,1536]{1,0:T(8,128)(2,1)S(1)}, u32[]{:S(2)}, u32[]{:S(2)}) %collective-permute-start.2) | collective-permute-done | bytes 294944 | tf_op jit(solution)/shard_map/ppermute | solution.py:22
  180.1 2.1 collective-permute-done.4
  182.3 4.1 %collective-permute-done.6 = bf16[96,1536]{1,0:T(8,128)(2,1)S(1)} collective-permute-done((bf16[96,1536]{1,0:T(8,128)(2,1)S(1)}, bf16[96,1536]{1,0:T(8,128)(2,1)S(1)}, u32[]{:S(2)}, u32[]{:S(2)}) %collective-permute-start.6) | collective-permute-done | bytes 294944 | tf_op jit(solution)/shard_map/ppermute | solution.py:22
  186.5 6.0 %collective-permute-done.14 = bf16[2,64,1536]{2,1,0:T(8,128)(2,1)S(1)} collective-permute-done((bf16[2,64,1536]{2,1,0:T(8,128)(2,1)S(1)}, bf16[2,64,1536]{2,1,0:T(8,128)(2,1)S(1)}, u32[]{:S(2)}, u32[]{:S(2)}) %collective-permute-start.14) | collective-permute-done | bytes 393248 | tf_op jit(solution)/shard_map/ppermute | solution.py:22
  193.2 5.9 %collective-permute-done.7 = bf16[2,96,1536]{2,1,0:T(8,128)(2,1)S(1)} collective-permute-done((bf16[2,96,1536]{2,1,0:T(8,128)(2,1)S(1)}, bf16[2,96,1536]{2,1,0:T(8,128)(2,1)S(1)}, u32[]{:S(2)}, u32[]{:S(2)}) %collective-permute-start.7) | collective-permute-done | bytes 589856 | tf_op jit(solution)/shard_map/ppermute | solution.py:22
  199.7 3.1 %collective-permute-done.15 = bf16[2,32,1536]{2,1,0:T(8,128)(2,1)S(1)} collective-permute-done((bf16[2,32,1536]{2,1,0:T(8,128)(2,1)S(1)}, bf16[2,32,1536]{2,1,0:T(8,128)(2,1)S(1)}, u32[]{:S(2)}, u32[]{:S(2)}) %collective-permute-start.15) | collective-permute-done | bytes 196640 | tf_op jit(solution)/shard_map/ppermute | solution.py:22
  203.5 5.0 %collective-permute-done.8 = bf16[96,1536]{1,0:T(8,128)(2,1)S(1)} collective-permute-done((bf16[96,1536]{1,0:T(8,128)(2,1)S(1)}, bf16[96,1536]{1,0:T(8,128)(2,1)S(1)}, u32[]{:S(2)}, u32[]{:S(2)}) %collective-permute-start.8) | collective-permute-done | bytes 294944 | tf_op jit(solution)/shard_map/ppermute | solution.py:22
  209.6 7.6 %collective-permute-done.9 = bf16[96,1536]{1,0:T(8,128)(2,1)S(1)} collective-permute-done((bf16[96,1536]{1,0:T(8,128)(2,1)S(1)}, bf16[96,1536]{1,0:T(8,128)(2,1)S(1)}, u32[]{:S(2)}, u32[]{:S(2)}) %collective-permute-start.9) | collective-permute-done | bytes 294944 | tf_op jit(solution)/shard_map/ppermute | solution.py:22
  217.3 2.6 %copy-done.5 = bf16[2,1024,1536]{2,1,0:T(8,128)(2,1)} copy-done((bf16[2,1024,1536]{2,1,0:T(8,128)(2,1)}, bf16[2,1024,1536]{2,1,0:T(8,128)(2,1)S(1)}, u32[]{:S(2)}) %copy-start.5) | copy-done | bytes 6291480
  220.0 19.9 %backward_rows.3 = (bf16[1024,6144]{1,0:T(8,128)(2,1)}, bf16[1024,1024]{1,0:T(8,128)(2,1)S(1)}) custom-call(s32[2]{0:T(128)S(1)} %broadcast_add_fusion.1.quarter, bf16[1024,1024]{1,0:T(8,128)(2,1)S(1)} %copy-done.3, bf16[2,1024,1536]{2,1,0:T(8,128)(2,1)} %copy-done.5, bf16[1024,6144]{1,0:T(8,128)(2,1)} %bitcast.324, ...), custom_call_target="tpu_custom_call", output_to_operand_aliasing={{0}: (6, {})} | custom-call | flops 12884901888 | bytes 23068672 | tf_op jit(solution)/shard_map/backward_rows/pallas_call | solution.py:133
  240.0 1.7 collective-permute-start.11
  241.7 3.8 %convert_bitcast_fusion = bf16[1,1024,1024]{2,1,0:T(8,128)(2,1)} fusion(bf16[1024,1024]{1,0:T(8,128)(2,1)S(1)} %get-tuple-element.9, s32[1024]{0:T(1024)S(1)} %bitcast.352), kind=kOutput, calls=%fused_computation.8 | convolution fusion | flops 2149580800 | bytes 4198400 | tf_op jit(solution)/shard_map/dot_general | solution.py:282
  245.5 3.1 %collective-permute-done.11 = bf16[96,1536]{1,0:T(8,128)(2,1)S(1)} collective-permute-done((bf16[96,1536]{1,0:T(8,128)(2,1)S(1)}, bf16[96,1536]{1,0:T(8,128)(2,1)S(1)}, u32[]{:S(2)}, u32[]{:S(2)}) %collective-permute-start.11) | collective-permute-done | bytes 294944 | tf_op jit(solution)/shard_map/ppermute | solution.py:22
  (175 shorter events, 23.2 us)
Async XLA Ops:
  1.8 56.4 %collective-permute-start.17 = (bf16[96,1536]{1,0:T(8,128)(2,1)S(1)}, bf16[96,1536]{1,0:T(8,128)(2,1)S(1)}, u32[]{:S(2)}, u32[]{:S(2)}) collective-permute-start(bf16[96,1536]{1,0:T(8,128)(2,1)S(1)} %slice.426), channel_id=1, source_target_pairs={{0,8},{4,12},{8,16},{12,20},{16,24},{20,28},{24,0},{28,4},{1,9},{5... | collective-permute-start | bytes 884744 | tf_op jit(solution)/shard_map/ppermute | solution.py:22
  5.8 51.8 %collective-permute-start.26 = (bf16[32,1536]{1,0:T(8,128)(2,1)S(1)}, bf16[32,1536]{1,0:T(8,128)(2,1)S(1)}, u32[]{:S(2)}, u32[]{:S(2)}) collective-permute-start(bf16[32,1536]{1,0:T(8,128)(2,1)S(1)} %get-tuple-element.38), channel_id=1, source_target_pairs={{0,2},{1,3},{2,0},{3,1},{4,6},{5,7},{6,4},{7,5},{8,10},{9,11},{10,... | collective-permute-start | bytes 294920 | tf_op jit(solution)/shard_map/ppermute | solution.py:22
  57.3 67.4 %collective-permute-start = (bf16[2,1024,1536]{2,1,0:T(8,128)(2,1)}, bf16[2,1024,1536]{2,1,0:T(8,128)(2,1)}, u32[]{:S(2)}, u32[]{:S(2)}) collective-permute-start(bf16[2,1024,1536]{2,1,0:T(8,128)(2,1)} %forward_rows.2), channel_id=1, source_target_pairs={{0,1},{1,0},{2,3},{3,2},{4,5},{5,4},{6,7},{7,6},{8,9},{9,8},{10,11... | collective-permute-start | bytes 18874376 | tf_op jit(solution)/shard_map/ppermute | solution.py:22
  57.6 7.8 %collective-permute-start.27 = (bf16[2,32,1536]{2,1,0:T(8,128)(2,1)S(1)}, bf16[2,32,1536]{2,1,0:T(8,128)(2,1)S(1)}, u32[]{:S(2)}, u32[]{:S(2)}) collective-permute-start(bf16[2,32,1536]{2,1,0:T(8,128)(2,1)S(1)} %get-tuple-element.67), channel_id=1, source_target_pairs={{0,4},{4,0},{8,12},{12,8},{16,20},{20,16},{24,28},{28,24},{1,5},{5... | collective-permute-start | bytes 589832 | tf_op jit(solution)/shard_map/ppermute | solution.py:22
  58.2 13.0 %collective-permute-start.20 = (bf16[2,48,1536]{2,1,0:T(8,128)(2,1)S(1)}, bf16[2,48,1536]{2,1,0:T(8,128)(2,1)S(1)}, u32[]{:S(2)}, u32[]{:S(2)}) collective-permute-start(bf16[2,48,1536]{2,1,0:T(8,128)(2,1)S(1)} %get-tuple-element.54), channel_id=1, source_target_pairs={{0,4},{4,0},{8,12},{12,8},{16,20},{20,16},{24,28},{28,24},{1,5},{5... | collective-permute-start | bytes 884744 | tf_op jit(solution)/shard_map/ppermute | solution.py:22
  59.9 12.1 %collective-permute-start.22 = (bf16[2,48,1536]{2,1,0:T(8,128)(2,1)S(1)}, bf16[2,48,1536]{2,1,0:T(8,128)(2,1)S(1)}, u32[]{:S(2)}, u32[]{:S(2)}) collective-permute-start(bf16[2,48,1536]{2,1,0:T(8,128)(2,1)S(1)} %get-tuple-element.44), channel_id=1, source_target_pairs={{0,2},{1,3},{2,0},{3,1},{4,6},{5,7},{6,4},{7,5},{8,10},{9,11},{10,... | collective-permute-start | bytes 884744 | tf_op jit(solution)/shard_map/ppermute | solution.py:22
  65.4 18.6 %collective-permute-start.28 = (bf16[2,2,32,1536]{3,2,1,0:T(8,128)(2,1)S(1)}, bf16[2,2,32,1536]{3,2,1,0:T(8,128)(2,1)S(1)}, u32[]{:S(2)}, u32[]{:S(2)}) collective-permute-start(bf16[2,2,32,1536]{3,2,1,0:T(8,128)(2,1)S(1)} %pad_maximum_fusion.6), channel_id=1, source_target_pairs={{0,8},{4,12},{8,16},{12,20},{16,24},{20,28},{24,0},{28,4},{1,9},{5... | collective-permute-start | bytes 1179656 | tf_op jit(solution)/shard_map/ppermute | solution.py:22
  65.5 18.5 %collective-permute-start.18 = (bf16[96,1536]{1,0:T(8,128)(2,1)S(1)}, bf16[96,1536]{1,0:T(8,128)(2,1)S(1)}, u32[]{:S(2)}, u32[]{:S(2)}) collective-permute-start(bf16[96,1536]{1,0:T(8,128)(2,1)S(1)} %collective-permute-done.17), channel_id=1, source_target_pairs={{0,8},{4,12},{8,16},{12,20},{16,24},{20,28},{24,0},{28,4},{1,9},{5... | collective-permute-start | bytes 884744 | tf_op jit(solution)/shard_map/ppermute | solution.py:22
  71.3 38.4 %collective-permute-start.31 = (bf16[2,2,48,1536]{3,2,1,0:T(8,128)(2,1)S(1)}, bf16[2,2,48,1536]{3,2,1,0:T(8,128)(2,1)S(1)}, u32[]{:S(2)}, u32[]{:S(2)}) collective-permute-start(bf16[2,2,48,1536]{3,2,1,0:T(8,128)(2,1)S(1)} %pad_maximum_fusion.3), channel_id=1, source_target_pairs={{0,2},{1,3},{2,0},{3,1},{4,6},{5,7},{6,4},{7,5},{8,10},{9,11},{10,... | collective-permute-start | bytes 1769480 | tf_op jit(solution)/shard_map/ppermute | solution.py:22
  72.0 49.0 %collective-permute-start.23 = (bf16[2,2,48,1536]{3,2,1,0:T(8,128)(2,1)S(1)}, bf16[2,2,48,1536]{3,2,1,0:T(8,128)(2,1)S(1)}, u32[]{:S(2)}, u32[]{:S(2)}) collective-permute-start(bf16[2,2,48,1536]{3,2,1,0:T(8,128)(2,1)S(1)} %pad_maximum_fusion.1), channel_id=1, source_target_pairs={{0,4},{4,0},{8,12},{12,8},{16,20},{20,16},{24,28},{28,24},{1,5},{5... | collective-permute-start | bytes 1769480 | tf_op jit(solution)/shard_map/ppermute | solution.py:22
  83.9 11.7 %collective-permute-start.19 = (bf16[96,1536]{1,0:T(8,128)(2,1)S(1)}, bf16[96,1536]{1,0:T(8,128)(2,1)S(1)}, u32[]{:S(2)}, u32[]{:S(2)}) collective-permute-start(bf16[96,1536]{1,0:T(8,128)(2,1)S(1)} %collective-permute-done.18), channel_id=1, source_target_pairs={{0,8},{4,12},{8,16},{12,20},{16,24},{20,28},{24,0},{28,4},{1,9},{5... | collective-permute-start | bytes 884744 | tf_op jit(solution)/shard_map/ppermute | solution.py:22
  84.0 17.5 %collective-permute-start.29 = (bf16[2,2,32,1536]{3,2,1,0:T(8,128)(2,1)S(1)}, bf16[2,2,32,1536]{3,2,1,0:T(8,128)(2,1)S(1)}, u32[]{:S(2)}, u32[]{:S(2)}) collective-permute-start(bf16[2,2,32,1536]{3,2,1,0:T(8,128)(2,1)S(1)} %collective-permute-done.28), channel_id=1, source_target_pairs={{0,8},{4,12},{8,16},{12,20},{16,24},{20,28},{24,0},{28,4},{1,9},{5... | collective-permute-start | bytes 1179656 | tf_op jit(solution)/shard_map/ppermute | solution.py:22
  101.5 7.7 %collective-permute-start.24 = (bf16[2,48,1536]{2,1,0:T(8,128)(2,1)S(1)}, bf16[2,48,1536]{2,1,0:T(8,128)(2,1)S(1)}, u32[]{:S(2)}, u32[]{:S(2)}) collective-permute-start(bf16[2,48,1536]{2,1,0:T(8,128)(2,1)S(1)} %get-tuple-element.42), channel_id=1, source_target_pairs={{0,2},{1,3},{2,0},{3,1},{4,6},{5,7},{6,4},{7,5},{8,10},{9,11},{10,... | collective-permute-start | bytes 884744 | tf_op jit(solution)/shard_map/ppermute | solution.py:22
  102.5 18.8 %collective-permute-start.30 = (bf16[2,2,32,1536]{3,2,1,0:T(8,128)(2,1)S(1)}, bf16[2,2,32,1536]{3,2,1,0:T(8,128)(2,1)S(1)}, u32[]{:S(2)}, u32[]{:S(2)}) collective-permute-start(bf16[2,2,32,1536]{3,2,1,0:T(8,128)(2,1)S(1)} %collective-permute-done.29), channel_id=1, source_target_pairs={{0,8},{4,12},{8,16},{12,20},{16,24},{20,28},{24,0},{28,4},{1,9},{5... | collective-permute-start | bytes 1179656 | tf_op jit(solution)/shard_map/ppermute | solution.py:22
  109.2 11.6 %collective-permute-start.32 = (bf16[2,2,48,1536]{3,2,1,0:T(8,128)(2,1)S(1)}, bf16[2,2,48,1536]{3,2,1,0:T(8,128)(2,1)S(1)}, u32[]{:S(2)}, u32[]{:S(2)}) collective-permute-start(bf16[2,2,48,1536]{3,2,1,0:T(8,128)(2,1)S(1)} %pad_maximum_fusion.4), channel_id=1, source_target_pairs={{0,2},{1,3},{2,0},{3,1},{4,6},{5,7},{6,4},{7,5},{8,10},{9,11},{10,... | collective-permute-start | bytes 1769480 | tf_op jit(solution)/shard_map/ppermute | solution.py:22
  109.8 11.2 %collective-permute-start.25 = (bf16[2,2,48,1536]{3,2,1,0:T(8,128)(2,1)S(1)}, bf16[2,2,48,1536]{3,2,1,0:T(8,128)(2,1)S(1)}, u32[]{:S(2)}, u32[]{:S(2)}) collective-permute-start(bf16[2,2,48,1536]{3,2,1,0:T(8,128)(2,1)S(1)} %pad_maximum_fusion.2), channel_id=1, source_target_pairs={{0,4},{4,0},{8,12},{12,8},{16,20},{20,16},{24,28},{28,24},{1,5},{5... | collective-permute-start | bytes 1769480 | tf_op jit(solution)/shard_map/ppermute | solution.py:22
  135.4 23.0 %collective-permute-start.1 = (bf16[192,1536]{1,0:T(8,128)(2,1)S(1)}, bf16[192,1536]{1,0:T(8,128)(2,1)S(1)}, u32[]{:S(2)}, u32[]{:S(2)}) collective-permute-start(bf16[192,1536]{1,0:T(8,128)(2,1)S(1)} %get-tuple-element.13), channel_id=1, source_target_pairs={{0,2},{1,3},{2,0},{3,1},{4,6},{5,7},{6,4},{7,5},{8,10},{9,11},{10,... | collective-permute-start | bytes 1769480 | tf_op jit(solution)/shard_map/ppermute | solution.py:22
  136.1 22.8 %collective-permute-start.5 = (bf16[192,1536]{1,0:T(8,128)(2,1)S(1)}, bf16[192,1536]{1,0:T(8,128)(2,1)S(1)}, u32[]{:S(2)}, u32[]{:S(2)}) collective-permute-start(bf16[192,1536]{1,0:T(8,128)(2,1)S(1)} %get-tuple-element.14), channel_id=1, source_target_pairs={{0,2},{1,3},{2,0},{3,1},{4,6},{5,7},{6,4},{7,5},{8,10},{9,11},{10,... | collective-permute-start | bytes 1769480 | tf_op jit(solution)/shard_map/ppermute | solution.py:22
  137.5 20.6 %collective-permute-start.12 = (bf16[2,64,1536]{2,1,0:T(8,128)(2,1)S(1)}, bf16[2,64,1536]{2,1,0:T(8,128)(2,1)S(1)}, u32[]{:S(2)}, u32[]{:S(2)}) collective-permute-start(bf16[2,64,1536]{2,1,0:T(8,128)(2,1)S(1)} %slice.543), channel_id=1, source_target_pairs={{0,8},{4,12},{8,16},{12,20},{16,24},{20,28},{24,0},{28,4},{1,9},{5... | collective-permute-start | bytes 1179656 | tf_op jit(solution)/shard_map/ppermute | solution.py:22
  157.5 59.8 %collective-permute-start.33 = (bf16[2,1024,1536]{2,1,0:T(8,128)(2,1)}, bf16[2,1024,1536]{2,1,0:T(8,128)(2,1)S(1)}, u32[]{:S(2)}, u32[]{:S(2)}) collective-permute-start(bf16[2,1024,1536]{2,1,0:T(8,128)(2,1)} %pad_maximum_fusion.grads), channel_id=1, source_target_pairs={{0,1},{1,0},{2,3},{3,2},{4,5},{5,4},{6,7},{7,6},{8,9},{9,8},{10,11... | collective-permute-start | bytes 18874376 | tf_op jit(solution)/shard_map/ppermute | solution.py:22
  157.6 16.2 %collective-permute-start.3 = (bf16[2,96,1536]{2,1,0:T(8,128)(2,1)S(1)}, bf16[2,96,1536]{2,1,0:T(8,128)(2,1)S(1)}, u32[]{:S(2)}, u32[]{:S(2)}) collective-permute-start(bf16[2,96,1536]{2,1,0:T(8,128)(2,1)S(1)} %slice.522), channel_id=1, source_target_pairs={{0,4},{4,0},{8,12},{12,8},{16,20},{20,16},{24,28},{28,24},{1,5},{5... | collective-permute-start | bytes 1769480 | tf_op jit(solution)/shard_map/ppermute | solution.py:22
  158.2 17.0 %collective-permute-start.13 = (bf16[2,64,1536]{2,1,0:T(8,128)(2,1)S(1)}, bf16[2,64,1536]{2,1,0:T(8,128)(2,1)S(1)}, u32[]{:S(2)}, u32[]{:S(2)}) collective-permute-start(bf16[2,64,1536]{2,1,0:T(8,128)(2,1)S(1)} %slice_add_fusion.2), channel_id=1, source_target_pairs={{0,8},{4,12},{8,16},{12,20},{16,24},{20,28},{24,0},{28,4},{1,9},{5... | collective-permute-start | bytes 1179656 | tf_op jit(solution)/shard_map/ppermute | solution.py:22
  159.0 21.0 %collective-permute-start.2 = (bf16[96,1536]{1,0:T(8,128)(2,1)S(1)}, bf16[96,1536]{1,0:T(8,128)(2,1)S(1)}, u32[]{:S(2)}, u32[]{:S(2)}) collective-permute-start(bf16[96,1536]{1,0:T(8,128)(2,1)S(1)} %slice.519), channel_id=1, source_target_pairs={{0,4},{4,0},{8,12},{12,8},{16,20},{20,16},{24,28},{28,24},{1,5},{5... | collective-permute-start | bytes 884744 | tf_op jit(solution)/shard_map/ppermute | solution.py:22
  173.9 8.3 %collective-permute-start.4 = (bf16[96,1536]{1,0:T(8,128)(2,1)S(1)}, bf16[96,1536]{1,0:T(8,128)(2,1)S(1)}, u32[]{:S(2)}, u32[]{:S(2)}) collective-permute-start(bf16[96,1536]{1,0:T(8,128)(2,1)S(1)} %slice_bitcast_fusion.6), channel_id=1, source_target_pairs={{0,2},{1,3},{2,0},{3,1},{4,6},{5,7},{6,4},{7,5},{8,10},{9,11},{10,... | collective-permute-start | bytes 884744 | tf_op jit(solution)/shard_map/ppermute | solution.py:22
  174.5 11.8 %collective-permute-start.6 = (bf16[96,1536]{1,0:T(8,128)(2,1)S(1)}, bf16[96,1536]{1,0:T(8,128)(2,1)S(1)}, u32[]{:S(2)}, u32[]{:S(2)}) collective-permute-start(bf16[96,1536]{1,0:T(8,128)(2,1)S(1)} %slice.531), channel_id=1, source_target_pairs={{0,4},{4,0},{8,12},{12,8},{16,20},{20,16},{24,28},{28,24},{1,5},{5... | collective-permute-start | bytes 884744 | tf_op jit(solution)/shard_map/ppermute | solution.py:22
  175.1 23.9 %collective-permute-start.7 = (bf16[2,96,1536]{2,1,0:T(8,128)(2,1)S(1)}, bf16[2,96,1536]{2,1,0:T(8,128)(2,1)S(1)}, u32[]{:S(2)}, u32[]{:S(2)}) collective-permute-start(bf16[2,96,1536]{2,1,0:T(8,128)(2,1)S(1)} %get-tuple-element.16), channel_id=1, source_target_pairs={{0,4},{4,0},{8,12},{12,8},{16,20},{20,16},{24,28},{28,24},{1,5},{5... | collective-permute-start | bytes 1769480 | tf_op jit(solution)/shard_map/ppermute | solution.py:22
  180.1 12.4 %collective-permute-start.14 = (bf16[2,64,1536]{2,1,0:T(8,128)(2,1)S(1)}, bf16[2,64,1536]{2,1,0:T(8,128)(2,1)S(1)}, u32[]{:S(2)}, u32[]{:S(2)}) collective-permute-start(bf16[2,64,1536]{2,1,0:T(8,128)(2,1)S(1)} %slice_add_fusion.3), channel_id=1, source_target_pairs={{0,8},{4,12},{8,16},{12,20},{16,24},{20,28},{24,0},{28,4},{1,9},{5... | collective-permute-start | bytes 1179656 | tf_op jit(solution)/shard_map/ppermute | solution.py:22
  192.6 10.3 %collective-permute-start.15 = (bf16[2,32,1536]{2,1,0:T(8,128)(2,1)S(1)}, bf16[2,32,1536]{2,1,0:T(8,128)(2,1)S(1)}, u32[]{:S(2)}, u32[]{:S(2)}) collective-permute-start(bf16[2,32,1536]{2,1,0:T(8,128)(2,1)S(1)} %slice.545), channel_id=1, source_target_pairs={{0,4},{4,0},{8,12},{12,8},{16,20},{20,16},{24,28},{28,24},{1,5},{5... | collective-permute-start | bytes 589832 | tf_op jit(solution)/shard_map/ppermute | solution.py:22
  199.1 9.4 %collective-permute-start.8 = (bf16[96,1536]{1,0:T(8,128)(2,1)S(1)}, bf16[96,1536]{1,0:T(8,128)(2,1)S(1)}, u32[]{:S(2)}, u32[]{:S(2)}) collective-permute-start(bf16[96,1536]{1,0:T(8,128)(2,1)S(1)} %slice_bitcast_fusion.4), channel_id=1, source_target_pairs={{0,2},{1,3},{2,0},{3,1},{4,6},{5,7},{6,4},{7,5},{8,10},{9,11},{10,... | collective-permute-start | bytes 884744 | tf_op jit(solution)/shard_map/ppermute | solution.py:22
  208.6 8.6 %collective-permute-start.9 = (bf16[96,1536]{1,0:T(8,128)(2,1)S(1)}, bf16[96,1536]{1,0:T(8,128)(2,1)S(1)}, u32[]{:S(2)}, u32[]{:S(2)}) collective-permute-start(bf16[96,1536]{1,0:T(8,128)(2,1)S(1)} %pad_maximum_fusion.7), channel_id=1, source_target_pairs={{0,8},{4,12},{8,16},{12,20},{16,24},{20,28},{24,0},{28,4},{1,9},{5... | collective-permute-start | bytes 884744 | tf_op jit(solution)/shard_map/ppermute | solution.py:22
  217.2 22.6 %collective-permute-start.10 = (bf16[96,1536]{1,0:T(8,128)(2,1)S(1)}, bf16[96,1536]{1,0:T(8,128)(2,1)S(1)}, u32[]{:S(2)}, u32[]{:S(2)}) collective-permute-start(bf16[96,1536]{1,0:T(8,128)(2,1)S(1)} %maximum_add_fusion.2), channel_id=1, source_target_pairs={{0,8},{4,12},{8,16},{12,20},{16,24},{20,28},{24,0},{28,4},{1,9},{5... | collective-permute-start | bytes 884744 | tf_op jit(solution)/shard_map/ppermute | solution.py:22
  240.0 8.6 %collective-permute-start.11 = (bf16[96,1536]{1,0:T(8,128)(2,1)S(1)}, bf16[96,1536]{1,0:T(8,128)(2,1)S(1)}, u32[]{:S(2)}, u32[]{:S(2)}) collective-permute-start(bf16[96,1536]{1,0:T(8,128)(2,1)S(1)} %maximum_add_fusion.1), channel_id=1, source_target_pairs={{0,8},{4,12},{8,16},{12,20},{16,24},{20,28},{24,0},{28,4},{1,9},{5... | collective-permute-start | bytes 884744 | tf_op jit(solution)/shard_map/ppermute | solution.py:22
  (8 other events, 92.7 us)

commit v2 on v0

v2 whole, which is shorter than its diff:
```python
import functools
import jax
import jax.numpy as jnp
from jax import lax
from jax.experimental import pallas as pl
from jax.experimental.pallas import tpu as pltpu
from jax.sharding import PartitionSpec as P

BF16, F32 = jnp.bfloat16, jnp.float32
ALL = ("dp", "expert")
VMEM = 44 * 2**20


class Ring:
    def __init__(self, size, perm):
        self.size, self.perm = size, perm

    def shift(self, block):
        return lax.ppermute(block, ALL, self.perm)

    def gather(self, block):
        blocks = [block]
        for _ in range(self.size - 1):
            blocks.append(self.shift(blocks[-1]))
        return blocks

    def scatter(self, blocks):
        if self.size == 1:
            return blocks[0]
        total = blocks[1]
        for j in list(range(2, self.size)) + [0]:
            total = blocks[j] + self.shift(total)
        return total


class Layout:
    def __init__(self):
        self.groups, self.owners = lax.axis_size("dp"), lax.axis_size("expert")
        self.nc = 2 if self.owners % 2 == 0 else 1
        self.nx = self.owners // self.nc
        self.ny = self.nx if self.groups % self.nx == 0 else 1
        self.nz = self.groups // self.ny
        dp, expert = lax.axis_index("dp"), lax.axis_index("expert")
        self.z, self.y = dp // self.ny, dp % self.ny
        self.x, self.core = expert // self.nc, expert % self.nc
        self.mixed = self.nx == self.ny and self.nc == 2
        step = {
            "x": lambda z, y, x, c: (z, y, (x + 1) % self.nx, c),
            "y": lambda z, y, x, c: (z, (y + 1) % self.ny, x, c),
            "c": lambda z, y, x, c: (z, y, x, (c + 1) % self.nc),
        }
        swapped = lambda c: self.mixed and c == 1
        self.far_z = [
            self.ring(self.nz, lambda z, y, x, c, k=k: ((z + k) % self.nz, y, x, c))
            for k in range(self.nz)
        ]
        self.ring_y = self.ring(self.ny, step["y"])
        self.ring_c = self.ring(self.nc, step["c"])
        self.ring_1 = self.ring(
            self.ny, lambda z, y, x, c: step["x" if swapped(c) else "y"](z, y, x, c)
        )
        self.ring_2 = self.ring(
            self.nx, lambda z, y, x, c: step["y" if swapped(c) else "x"](z, y, x, c)
        )

    def ring(self, size, onward):
        flat = lambda z, y, x, c: ((z * self.ny + y) * self.nx + x) * self.nc + c
        perm = []
        for z in range(self.nz):
            for y in range(self.ny):
                for x in range(self.nx):
                    for c in range(self.nc):
                        perm.append((flat(z, y, x, c), flat(*onward(z, y, x, c))))
        return Ring(size, perm)


def tile_of(width, most):
    tile = most
    while width % tile:
        tile -= 128
    return tile


def send_kernel(quarter, rows, weight, out):
    out[...] = jnp.dot(rows[...], weight[...], preferred_element_type=F32).astype(BF16)


def forward_sent(rows, weight, quarter):
    tokens, depth = rows.shape
    width = weight.shape[1] // lax.axis_size("expert")
    tile = tile_of(width, 768)
    per = width // tile
    return pl.pallas_call(
        send_kernel,
        grid_spec=pltpu.PrefetchScalarGridSpec(
            num_scalar_prefetch=1,
            grid=(per,),
            in_specs=[
                pl.BlockSpec((tokens, depth), lambda j, q: (0, 0)),
                pl.BlockSpec((depth, tile), lambda j, q: (0, q[0] * per + j)),
            ],
            out_specs=pl.BlockSpec((tokens, tile), lambda j, q: (0, j)),
        ),
        out_shape=jax.ShapeDtypeStruct((tokens, width), BF16),
        compiler_params=pltpu.CompilerParams(vmem_limit_bytes=VMEM),
        cost_estimate=pl.CostEstimate(
            flops=2 * tokens * depth * width,
            bytes_accessed=2 * (tokens * depth + width * (depth + tokens)),
            transcendentals=0,
        ),
        name="forward_sent",
    )(quarter, rows, weight)


def place_kernel(jx, ny, plan, mixed, has_extra, table, rows, weight, *rest):
    rest = list(rest)
    extra = rest.pop(0) if has_extra else None
    stage, sems = rest[-2:]
    outs = rest[-2 - sum(len(group[3]) for group in plan) : -2]
    step, steps = pl.program_id(0), pl.num_programs(0)
    tile = weight.shape[1]
    acc = jnp.dot(rows[...], weight[...], preferred_element_type=F32)
    if has_extra:
        acc = acc + extra[...].astype(F32)
    stage[step] = acc.astype(BF16)

    def copies(at, act):
        columns = pl.ds(pl.multiple_of(at * tile, 128), tile)
        for g, (first, stride, size, numbers) in enumerate(plan):
            for jy in range(ny):

                def copy(k1, k2, first=first + jy * stride, size=size, numbers=numbers, g=g, jy=jy):
                    act(
                        pltpu.make_async_copy(
                            stage.at[at, pl.ds(first, size), :],
                            outs[numbers[k1]].at[k2, :, columns],
                            sems.at[at, g * ny + jy],
                        )
                    )

                if not mixed or jx == jy:
                    copy(jx, jy)
                else:
                    pl.when(table[1] == 0)(functools.partial(copy, jx, jy))
                    pl.when(table[1] != 0)(functools.partial(copy, jy, jx))

    copies(step, lambda copy: copy.start())

    @pl.when(step == steps - 1)
    def _():
        for at in range(stage.shape[0]):
            copies(at, lambda copy: copy.wait())


def forward_placed(rows, weight, quarter, extra, jx, swapped, places, size, at, before):
    tokens, depth = rows.shape
    width = weight.shape[1] // at.owners
    tile = tile_of(width, 768)
    per = width // tile
    plan, shapes = [], []
    for first, stride in places:
        plan.append((first, stride, size, [len(shapes) + k for k in range(at.nx)]))
        shapes += [jax.ShapeDtypeStruct((at.ny, size, width), BF16)] * at.nx
    specs = [
        pl.BlockSpec((tokens, depth), lambda j, t: (0, 0)),
        pl.BlockSpec((depth, tile), lambda j, t: (0, t[0] * per + j)),
    ]
    operands = [rows, weight]
    if extra is not None:
        specs.append(pl.BlockSpec((tokens, tile), lambda j, t: (0, j)))
        operands.append(extra)
    aliases = {}
    if before is not None:
        aliases = {1 + len(operands) + i: i for i in range(len(shapes))}
        specs += [pl.BlockSpec(memory_space=pltpu.HBM)] * len(shapes)
        operands += list(before)
    return pl.pallas_call(
        functools.partial(place_kernel, jx, at.ny, plan, at.mixed, extra is not None),
        grid_spec=pltpu.PrefetchScalarGridSpec(
            num_scalar_prefetch=1,
            grid=(per,),
            in_specs=specs,
            out_specs=[pl.BlockSpec(memory_space=pltpu.HBM)] * len(shapes),
            scratch_shapes=[
                pltpu.VMEM((per, tokens, tile), BF16),
                pltpu.SemaphoreType.DMA((per, len(places) * at.ny)),
            ],
        ),
        out_shape=shapes,
        input_output_aliases=aliases,
        compiler_params=pltpu.CompilerParams(vmem_limit_bytes=VMEM),
        cost_estimate=pl.CostEstimate(
            flops=2 * tokens * depth * width,
            bytes_accessed=2 * (tokens * depth + width * (depth + 2 * tokens)),
            transcendentals=0,
        ),
        name="forward_placed",
    )(jnp.concatenate([quarter, swapped]), *operands)


def gather_kernel(plan, swapped, *rest):
    sources = max(item[0] for item in plan) + 1
    blocks, (out, stage, loads, stores) = rest[:sources], rest[-4:]
    copies, done = [], 0
    for i, (number, index, (j1, j2), first, stride, size) in enumerate(plan):
        jy = jnp.where(swapped[0] == 0, j1, j2)
        jx = jnp.where(swapped[0] == 0, j2, j1)
        place = stage.at[pl.ds(done, size)]
        done += size
        row = pl.multiple_of(first + jy * stride, 128)
        copies.append(
            (
                pltpu.make_async_copy(blocks[number].at[index], place, loads.at[i]),
                pltpu.make_async_copy(place, out.at[jx, pl.ds(row, size)], stores.at[i]),
            )
        )
    for load, _ in copies:
        load.start()
    for load, store in copies:
        load.wait()
        store.start()
    for _, store in copies:
        store.wait()


def put_together(plan, blocks, swapped, shape):
    operands = list(blocks)
    return pl.pallas_call(
        functools.partial(gather_kernel, plan),
        grid_spec=pltpu.PrefetchScalarGridSpec(
            num_scalar_prefetch=1,
            grid=(1,),
            in_specs=[pl.BlockSpec(memory_space=pl.ANY)] * len(operands),
            out_specs=pl.BlockSpec(memory_space=pltpu.HBM),
            scratch_shapes=[
                pltpu.VMEM((sum(item[5] for item in plan), shape[-1]), BF16),
                pltpu.SemaphoreType.DMA((len(plan),)),
                pltpu.SemaphoreType.DMA((len(plan),)),
            ],
        ),
        out_shape=jax.ShapeDtypeStruct(shape, BF16),
        compiler_params=pltpu.CompilerParams(vmem_limit_bytes=VMEM),
        cost_estimate=pl.CostEstimate(
            flops=0, bytes_accessed=4 * sum(b.size for b in blocks), transcendentals=0
        ),
        name="put_together",
    )(swapped, *operands)


def weight_kernel(sources, quarters, turned, *rest):
    total, first = None, 0
    for block in rest[:sources]:
        size = block.shape[1]
        part = jnp.dot(turned[:, first : first + size], block[0], preferred_element_type=F32)
        total = part if total is None else total + part
        first += size
    rest[-1][...] = total.astype(BF16)


def weight_gradient(turned, grads, jx, quarter, shape, before):
    depth, tokens = turned.shape
    width = grads[0].shape[2]
    tile = tile_of(width, 768)
    per = width // tile
    specs = [pl.BlockSpec((depth, tokens), lambda j, q: (0, 0))]
    for block in grads:
        specs.append(pl.BlockSpec((1, block.shape[1], tile), lambda j, q: (jx, 0, j)))
    operands = [turned] + list(grads)
    aliases = {}
    if before is not None:
        specs.append(pl.BlockSpec(memory_space=pltpu.HBM))
        aliases = {len(operands) + 1: 0}
        operands.append(before)
    return pl.pallas_call(
        functools.partial(weight_kernel, len(grads)),
        grid_spec=pltpu.PrefetchScalarGridSpec(
            num_scalar_prefetch=1,
            grid=(per,),
            in_specs=specs,
            out_specs=pl.BlockSpec((depth, tile), lambda j, q: (0, q[0] * per + j)),
        ),
        out_shape=jax.ShapeDtypeStruct(shape, BF16),
        input_output_aliases=aliases,
        compiler_params=pltpu.CompilerParams(vmem_limit_bytes=VMEM),
        cost_estimate=pl.CostEstimate(
            flops=2 * tokens * depth * width,
            bytes_accessed=2 * (tokens * depth + width * (depth + tokens)),
            transcendentals=0,
        ),
        name="weight_gradient",
    )(quarter, *operands)


def hidden_kernel(steps, each, last, table, gates, weight, *rest):
    out, total = rest[-2:]
    sources = steps // each
    step = pl.program_id(0)

    @pl.when(step == 0)
    def _():
        total[...] = jnp.zeros_like(total)

    for i, block in enumerate(rest[:sources]):

        @pl.when(step // each == i)
        def _(block=block):
            total[...] += lax.dot_general(
                block[0], weight[...], (((1,), (1,)), ((), ())), preferred_element_type=F32
            )

    @pl.when(step == steps - 1)
    def _():
        back = (total[...] * gates[...]).astype(BF16)
        if last:
            chosen, before = rest[sources : sources + 2]
            size = before.shape[0]
            picked = jnp.dot(chosen[:, :size], before[...], preferred_element_type=F32)
            picked += jnp.dot(chosen[:, size:], back, preferred_element_type=F32)
            out[...] = picked.astype(BF16)
        else:
            out[...] = back


def hidden_gradient(gates, grads, weight, quarters, chosen=None, before=None):
    count, tokens, width = grads[0].shape
    depth = weight.shape[0]
    tile = tile_of(width, 1536)
    per = width // tile
    each = per * count
    steps = each * len(grads)
    last = chosen is not None
    height = chosen.shape[0] if last else tokens
    specs = [
        pl.BlockSpec((tokens, 1), lambda s, t: (0, 0)),
        pl.BlockSpec((depth, tile), lambda s, t: (0, t[s // per] * per + s % per)),
    ]
    for i in range(len(grads)):

        def place(s, t, i=i):
            s = jnp.clip(s - i * each, 0, each - 1)
            return (s // per, 0, s % per)

        specs.append(pl.BlockSpec((1, tokens, tile), place))
    operands = [gates, weight] + list(grads)
    flops = 2 * tokens * depth * width * count * len(grads)
    if last:
        specs.append(pl.BlockSpec(chosen.shape, lambda s, t: (0, 0)))
        specs.append(pl.BlockSpec(before.shape, lambda s, t: (0, 0)))
        operands += [chosen, before]
        flops += 2 * chosen.shape[0] * chosen.shape[1] * depth
    return pl.pallas_call(
        functools.partial(hidden_kernel, steps, each, last),
        grid_spec=pltpu.PrefetchScalarGridSpec(
            num_scalar_prefetch=1,
            grid=(steps,),
            in_specs=specs,
            out_specs=pl.BlockSpec((height, depth), lambda s, t: (0, 0)),
            scratch_shapes=[pltpu.VMEM((tokens, depth), F32)],
        ),
        out_shape=jax.ShapeDtypeStruct((height, depth), BF16),
        compiler_params=pltpu.CompilerParams(vmem_limit_bytes=VMEM),
        cost_estimate=pl.CostEstimate(
            flops=flops,
            bytes_accessed=2 * len(grads) * count * width * (depth + tokens),
            transcendentals=0,
        ),
        name="hidden_gradient",
    )(quarters, *operands)


def tie(value, *others):
    return lax.optimization_barrier((value, others))[0]


def body(hidden, down_weight, grad_out, routing, gates):
    at = Layout()
    nx, ny, nz = at.nx, at.ny, at.nz
    rows, width = grad_out.shape
    top = routing.shape[1]
    slots = hidden.shape[1]
    capacity = slots // at.groups
    hidden_rows, weight = hidden[0], down_weight[0]

    turns = [list(range(nz // 2)), list(range(nz // 2, nz))]
    order = [(jz, jy) for turn in turns for jy in range(ny) for jz in turn]
    half = len(turns[0]) * ny * rows
    places = [
        (base + i * rows, len(turn) * rows)
        for base, turn in zip((0, half), turns)
        for i in range(len(turn))
    ]
    swapped = ((at.core == 1) if at.mixed else (at.core < 0)).astype(jnp.int32)[None]
    back_x = (at.x - jnp.arange(nx)) % nx * at.nc
    mine = (back_x + at.core).astype(jnp.int32)
    theirs = (back_x + (at.core + at.nc - 1) % at.nc).astype(jnp.int32)
    two = at.nc > 1
    quarters = jnp.concatenate([mine, theirs]) if two else mine

    def share(block, name):
        with jax.named_scope(name):
            return at.ring_c.shift(block) if two else block

    def gathered(ring, block, name):
        with jax.named_scope(name):
            return ring.gather(block)

    def shifted(k, block, name):
        with jax.named_scope(name):
            return at.far_z[k % nz].shift(block)

    packed = jnp.concatenate([routing.astype(F32).T, gates.T])
    packed = jnp.stack(gathered(at.ring_y, packed, "routes_y"))
    plane = [grad_out]
    first = [gathered(at.ring_1, grad_out, "own_first")]
    tables = [packed] + [shifted(jz, packed, "routes_z") for jz in range(1, nz)]
    plane.append(shifted(1, tie(grad_out, packed), "plane_1"))
    second = [gathered(at.ring_2, jnp.stack(first[0]), "own_second")]
    packed = jnp.stack([tables[jz][jy] for jz, jy in order])

    hits = packed[:, :top] == lax.axis_index("expert").astype(F32)
    hit = hits.astype(F32).sum(axis=1)
    gate = jnp.where(hits, packed[:, top:], 0.0).sum(axis=1)
    earlier = (jnp.arange(rows)[:, None] < jnp.arange(rows)[None, :]).astype(BF16)
    place = jnp.dot(hit.astype(BF16), earlier, preferred_element_type=F32).astype(jnp.int32)
    shards = jnp.stack([(at.z - jz) % nz * ny + (at.y - jy) % ny for jz, jy in order])
    slot_of = jnp.where(hit > 0, place + shards[:, None] * capacity, -1).reshape(-1)
    numbers = jnp.arange(slots, dtype=jnp.int32)
    chosen = (slot_of[:, None] == numbers[None, :]).astype(BF16)
    chosen_turned = (numbers[:, None] == slot_of[None, :]).astype(BF16)
    gate_column = gate.reshape(-1)[:, None]
    rows_in = jnp.dot(chosen, hidden_rows, preferred_element_type=F32)
    rows_in = (rows_in * gate_column).astype(BF16)

    plane.append(shifted(1, plane[1], "plane_2"))
    first.append(gathered(at.ring_1, plane[1], "plane_1_first"))
    ask = tie(theirs, plane[1], first[0])
    sent = []
    if two:
        sent = [forward_sent(rows_in, weight, ask[:1])]
    plane[2], first[1] = tie((plane[2], first[1]), sent)
    plane.append(shifted(1, plane[2], "plane_3"))
    first.append(gathered(at.ring_1, plane[2], "plane_2_first"))
    first[1] = jnp.stack(first[1])
    second.append(gathered(at.ring_2, first[1], "plane_1_second"))
    ask = tie(theirs, first[1], plane[2])
    if two:
        sent += [forward_sent(rows_in, weight, ask[jx : jx + 1]) for jx in range(1, nx)]
    extras = [share(block, "forward_core") for block in sent] if two else [None] * nx
    first[2] = jnp.stack(tie(first[2], sent[1:]))
    second.append(gathered(at.ring_2, first[2], "plane_2_second"))
    ask = tie(mine, first[2])
    placed = forward_placed(
        rows_in, weight, ask[:1], extras[0], 0, swapped, places, rows, at, None
    )
    plane[3], placed = tie((plane[3], placed), placed)
    first.append(gathered(at.ring_1, plane[3], "plane_3_first"))
    ask = tie(mine, plane[3])
    for jx in range(1, nx):
        placed = forward_placed(
            rows_in, weight, ask[jx : jx + 1], extras[jx], jx, swapped, places, rows, at, placed
        )
    first[3], second[0], second[1] = tie((first[3], second[0], second[1]), placed)
    first[3] = jnp.stack(first[3])
    second.append(gathered(at.ring_2, first[3], "plane_3_second"))

    def assembled(turn):
        plan, blocks = [], []
        for i, jz in enumerate(turn):
            for j2 in range(nx):
                for j1 in range(ny):
                    item = (len(blocks), j1, (j1, j2), i * rows, len(turn) * rows, rows)
                    plan.append(item)
                blocks.append(second[jz][j2])
        return put_together(plan, blocks, swapped, (nx, half, width))

    class Sum:
        def __init__(self, jz):
            self.name = "sum_%d" % jz
            self.terms = list(placed[jz * nx : (jz + 1) * nx])

        def start(self, ring, after=()):
            with jax.named_scope(self.name):
                self.terms = tie(self.terms, after)
                total = self.terms[1]
                for j in range(2, ring.size):
                    total = self.terms[j] + ring.shift(total)
                self.sent = total
                self.got = ring.shift(total)

        def finish(self, after):
            self.terms = self.terms[0] + tie(self.got, after)

        def second(self):
            self.terms = [self.terms[j] for j in range(ny)]
            self.start(at.ring_1)

    sums = [Sum(jz) for jz in range(nz)]
    sums[2].start(at.ring_2)
    grads_1 = assembled(turns[0])
    others_1 = [grads_1, share(grads_1, "gradients_core")] if two else [grads_1]
    sums[3].start(at.ring_2, grads_1)
    ask = tie(quarters, first[3], sums[3].sent)
    back = hidden_gradient(gate_column[:half], others_1, weight, ask)

    second[2], second[3] = tie((second[2], second[3]), back)
    grads_2 = assembled(turns[1])
    others_2 = [grads_2, share(grads_2, "gradients_core")] if two else [grads_2]
    sums[1].start(at.ring_2, grads_2)
    turned = rows_in.T
    ask = tie(mine, sums[1].sent)
    pair = [grads_1, grads_2]
    grad_weight = weight_gradient(turned, pair, 0, ask[:1], weight.shape, None)
    sums[2].finish(grad_weight)
    sums[2].second()
    ask = tie(quarters, sums[2].sent)
    grad_hidden = hidden_gradient(
        gate_column[half:], others_2, weight, ask, chosen_turned, back
    )

    received = {}
    sums[2].finish(grad_hidden)
    received[2] = shifted(nz - 2, sums[2].terms, "sum_2_z")
    sums[3].finish(grad_hidden)
    sums[3].second()
    sums[0].start(at.ring_2, grad_hidden)
    ask = tie(mine, sums[3].sent, sums[2].terms, sums[0].sent)
    for jx in range(1, nx):
        grad_weight = weight_gradient(
            turned, pair, jx, ask[jx : jx + 1], weight.shape, grad_weight
        )
    sums[3].finish(grad_weight)
    received[3] = shifted(nz - 3, sums[3].terms, "sum_3_z")
    sums[1].finish(grad_weight)
    sums[1].second()
    ask = tie(theirs, sums[3].terms, sums[1].sent)
    pair = [others_1[-1], others_2[-1]]
    for jx in range(nx if two else 0):
        grad_weight = weight_gradient(
            turned, pair, jx, ask[jx : jx + 1], weight.shape, grad_weight
        )
        if jx == 0:
            sums[1].finish(grad_weight)
            received[1] = shifted(nz - 1, sums[1].terms, "sum_1_z")
            sums[0].finish(grad_weight)
            sums[0].second()
            ask = tie(theirs, sums[1].terms, sums[0].sent)
    if not two:
        sums[1].finish(grad_weight)
        received[1] = shifted(nz - 1, sums[1].terms, "sum_1_z")
        sums[0].finish(grad_weight)
        sums[0].second()
    sums[0].finish(grad_weight)
    mixed_out = sums[0].terms.astype(F32)
    for jz in range(1, nz):
        mixed_out = mixed_out + tie(received[jz], grad_weight).astype(F32)
    return (mixed_out.astype(BF16), grad_hidden[None], grad_weight[None])


def solution(mesh):
    return jax.shard_map(
        body,
        mesh=mesh,
        in_specs=(
            P("expert", None, "dp"),
            P("expert", "dp", None),
            P("dp", "expert"),
            P("dp", None),
            P("dp", None),
        ),
        out_specs=(P("dp", "expert"), P("expert", None, "dp"), P("expert", "dp", None)),
        check_vma=False,
    )
```

time: 428 us -> 187 us (0.44)
  blocking collectives: 291 us -> 0 us
  Pallas kernels: 0 us -> 87 us
  matrix products: 65.7 us -> 3.96 us
  local copies, waits for them, and re-layouts: 47.6 us -> 12.2 us
  starting transfers between devices: 0.08 us -> 33 us
  waiting for transfers between devices: 5.45 us -> 38 us
  between operations: 14.1 us -> 0.95 us
  other arithmetic: 2.84 us -> 11.4 us
    all_to_all x2 -> x0, blocking collectives: 291 us -> none  [the longest x1 147 us: body(): lax.all_to_all(shards, 'expert', split_axis=0, concat_axis=2, tiled=True)]
    pallas_call x0 -> x12, Pallas kernels: none -> 87 us  [the longest x2 27 us: hidden_gradient(): pl.pallas_call(functools.partial(hidden_kernel, steps, each, last), grid_...]
    dot_general x5 -> x2, matrix products: 65.7 us -> 3.96 us  [the longest x1 3.86 us: body(): rows_in = jnp.dot(chosen, hidden_rows, preferred_element_type=F32)]
    ppermute x0 -> x30, waiting for transfers between devices: none -> 38 us  [shift(): return lax.ppermute(block, ALL, self.perm)]
    ppermute x0 -> x30, starting transfers between devices: none -> 33 us  [shift(): return lax.ppermute(block, ALL, self.perm)]
    reshape x2 -> x0, local copies, waits for them, and re-layouts: 19.3 us -> none  [the longest x1 16.7 us: body(): partial_value.reshape(1, groups, capacity, partial_value.shape[-1])]
    unnamed x6 -> x40, local copies, waits for them, and re-layouts: 17.6 us -> 6.43 us
    all_to_all x1 -> x0, local copies, waits for them, and re-layouts: 7.36 us -> none  [body(): lax.all_to_all(partial_value, 'expert', split_axis=3, concat_axis=0, tile...]
  transfers between devices with their start and end apart: 2 -> 30, of which waited for: 1 -> 10; matrix products, arithmetic and copies ran while one was open for 23% -> 10% of each run, Pallas kernels for 0% -> 43%
where the time goes in v2:
time: 187 us; the launch traced here: 186 us
  Pallas kernels  87 us (47%)
  waiting for transfers between devices  38 us (20%)
  starting transfers between devices  33 us (18%)
  local copies, waits for them, and re-layouts  12.2 us (7%)
  other arithmetic  11.4 us (6%)
  matrix products  3.96 us (2%)
    ppermute x30, waiting for transfers between devices, shift(): return lax.ppermute(block, ALL, self.perm)  38 us
    ppermute x30, starting transfers between devices, shift(): return lax.ppermute(block, ALL, self.perm)  33 us
    pallas_call x2, Pallas kernels, hidden_gradient(): pl.pallas_call(functools.partial(hidden_kernel, steps, each, last), grid_...  27 us
    pallas_call x4, Pallas kernels, weight_gradient(): pl.pallas_call(functools.partial(weight_kernel, len(grads)), grid_spec=pl...  26.3 us
    pallas_call x2, Pallas kernels, forward_placed(): pl.pallas_call(functools.partial(place_kernel, jx, at.ny, plan, at.mixed,...  14.2 us
    pallas_call x2, Pallas kernels, forward_sent(): pl.pallas_call(send_kernel, grid_spec=pltpu.PrefetchScalarGridSpec(num_sc...  13.2 us
    unnamed x40, local copies, waits for them, and re-layouts  6.43 us
    pallas_call x2, Pallas kernels, put_together(): pl.pallas_call(functools.partial(gather_kernel, plan), grid_spec=pltpu.Pr...  6.25 us
  transfers between devices with their start and end apart: 30, of which 10 were waited for; matrix products, arithmetic and copies ran while one was open for 10% of the time, Pallas kernels for 43%

profile of v2, /device:TPU:0, one launch (start us, length us, event | category | flops | bytes accessed | tf_op | source)
XLA Modules:
  0.0 186.5 jit_solution(18117821855187489969)
XLA Ops:
  2.2 3.0 %collective-permute-start = (f32[4,128]{1,0:T(4,128)S(1)}, f32[4,128]{1,0:T(4,128)S(1)}, u32[]{:S(2)}, u32[]{:S(2)}) collective-permute-start(f32[4,128]{1,0:T(4,128)S(1)} %get-tuple-element.172), channel_id=1, source_target_pairs={{0,4},{1,5},{2,6},{3,7},{4,0},{5,1},{6,2},{7,3},{8,12},{9,13},{10,... | collective-permute-start | bytes 6152 | tf_op jit(solution)/shard_map/routes_y/ppermute | solution.py:19
  6.7 2.1 %collective-permute-start.5 = (f32[2,4,128]{2,1,0:T(4,128)S(1)}, f32[2,4,128]{2,1,0:T(4,128)S(1)}, u32[]{:S(2)}, u32[]{:S(2)}) collective-permute-start(f32[2,4,128]{2,1,0:T(4,128)S(1)} %pad_maximum_fusion.4), channel_id=1, source_target_pairs={{0,8},{1,9},{2,10},{3,11},{4,12},{5,13},{6,14},{7,15},{8,16},{9,17... | collective-permute-start | bytes 12296 | tf_op jit(solution)/shard_map/routes_z/ppermute | solution.py:19
  8.8 2.1 %collective-permute-start.7 = (f32[2,4,128]{2,1,0:T(4,128)S(1)}, f32[2,4,128]{2,1,0:T(4,128)S(1)}, u32[]{:S(2)}, u32[]{:S(2)}) collective-permute-start(f32[2,4,128]{2,1,0:T(4,128)S(1)} %pad_maximum_fusion.4), channel_id=1, source_target_pairs={{0,24},{1,25},{2,26},{3,27},{4,28},{5,29},{6,30},{7,31},{8,0},{9,1... | collective-permute-start | bytes 12296 | tf_op jit(solution)/shard_map/routes_z/ppermute | solution.py:19
  11.9 1.6 collective-permute-start.1
  13.5 2.3 %collective-permute-done.6 = f32[2,4,128]{2,1,0:T(4,128)S(1)} collective-permute-done((f32[2,4,128]{2,1,0:T(4,128)S(1)}, f32[2,4,128]{2,1,0:T(4,128)S(1)}, u32[]{:S(2)}, u32[]{:S(2)}) %collective-permute-start.6) | collective-permute-done | bytes 4128 | tf_op jit(solution)/shard_map/routes_z/ppermute | solution.py:19
  16.0 7.7 %collective-permute-done.1 = bf16[128,1536]{1,0:T(8,128)(2,1)S(1)} collective-permute-done((bf16[128,1536]{1,0:T(8,128)(2,1)}, bf16[128,1536]{1,0:T(8,128)(2,1)S(1)}, u32[]{:S(2)}, u32[]{:S(2)}) %collective-permute-start.1) | collective-permute-done | bytes 393248 | tf_op jit(solution)/shard_map/plane_1/ppermute | solution.py:19
  24.4 3.9 %multiply_convert_fusion = bf16[1024,1024]{0,1:T(8,128)(2,1)} fusion(f32[1024]{0:T(1024)S(1)} %bitcast.80, bf16[1,1024,1024]{2,1,0:T(8,128)(2,1)S(1)} %copy-done, s32[1024]{0:T(1024)S(1)} %fusion.8), kind=kOutput, calls=%fused_computation.1 | convolution fusion | flops 2150629376 | bytes 4202496 | tf_op jit(solution)/shard_map/dot_general | solution.py:431
  28.3 2.9 %copy.25.rows = bf16[1024,1024]{1,0:T(8,128)(2,1)S(1)} copy(bf16[1024,1024]{0,1:T(8,128)(2,1)} %multiply_convert_fusion) | data formatting | bytes 4194304 | tf_op jit(solution)/shard_map/convert_element_type | solution.py:432
  31.1 6.3 %forward_sent.2 = bf16[1024,1536]{1,0:T(8,128)(2,1)} custom-call(s32[1]{0:T(128)S(1)} %bitcast.63, bf16[1024,1024]{1,0:T(8,128)(2,1)S(1)} %copy.25.rows, bf16[1024,6144]{1,0:T(8,128)(2,1)} %bitcast.67), custom_call_target="tpu_custom_call" | custom-call | flops 3221225472 | bytes 8388608 | tf_op jit(solution)/shard_map/forward_sent/pallas_call | solution.py:93
  37.5 1.9 %pad_maximum_fusion.rest_2_ = bf16[2,128,1536]{2,1,0:T(8,128)(2,1)} fusion(bf16[1,128,1536]{2,1,0:T(8,128)(2,1)} %bitcast.17, bf16[1,128,1536]{2,1,0:T(8,128)(2,1)S(1)} %bitcast.78), kind=kLoop, calls=%fused_computation.11 | loop fusion | flops 393216 | bytes 1572864 | tf_op jit(solution)/shard_map/stack | solution.py:443
  40.0 6.9 %forward_sent.3 = bf16[1024,1536]{1,0:T(8,128)(2,1)} custom-call(s32[1]{0:T(128)} %slice.93.quarter, bf16[1024,1024]{1,0:T(8,128)(2,1)S(1)} %copy.25.rows, bf16[1024,6144]{1,0:T(8,128)(2,1)} %bitcast.68), custom_call_target="tpu_custom_call" | custom-call | flops 3221225472 | bytes 8388608 | tf_op jit(solution)/shard_map/forward_sent/pallas_call | solution.py:93
  50.5 8.6 %collective-permute-done.9 = bf16[128,1536]{1,0:T(8,128)(2,1)} collective-permute-done((bf16[128,1536]{1,0:T(8,128)(2,1)S(1)}, bf16[128,1536]{1,0:T(8,128)(2,1)}, u32[]{:S(2)}, u32[]{:S(2)}) %collective-permute-start.9) | collective-permute-done | bytes 393248 | tf_op jit(solution)/shard_map/plane_2_first/ppermute | solution.py:19
  59.1 1.8 collective-permute-start.16
  62.1 6.7 %forward_placed.2 = (bf16[2,128,1536]{2,1,0:T(8,128)(2,1)S(1)}, bf16[2,128,1536]{2,1,0:T(8,128)(2,1)S(1)}, bf16[2,128,1536]{2,1,0:T(8,128)(2,1)S(1)}, bf16[2,128...) custom-call(s32[2]{0:T(128)S(1)} %pad_add_fusion.table, ...), custom_call_target="tpu_custom_call" | custom-call | flops 3221225472 | bytes 11534336 | tf_op jit(solution)/shard_map/forward_placed/pallas_call | solution.py:177
  70.5 7.5 %forward_placed.3 = (bf16[2,128,1536]{2,1,0:T(8,128)(2,1)S(1)}, bf16[2,128,1536]{2,1,0:T(8,128)(2,1)S(1)}, bf16[2,128,1536]{2,1,0:T(8,128)(2,1)S(1)}, bf16[2,128...) custom-call(s32[2]{0:T(128)S(1)} %pad_add_fusion.1.table, ...), custom_call_target="tpu_custom_call", output_to_operand_aliasing={{0}: (4, {}), {1}: (5, {}), {2}: (6, {}), {3}: (7, {}), {4}... | custom-call | flops 3221225472 | bytes 11534336 | tf_op jit(solution)/shard_map/forward_placed/pallas_call | solution.py:177
  81.6 3.0 %put_together.2.rest_0_ = bf16[2,512,1536]{2,1,0:T(8,128)(2,1)} custom-call(s32[1]{0:T(128)} %bitcast.20.swapped, bf16[2,128,1536]{2,1,0:T(8,128)(2,1)S(1)} %pad_maximum_fusion.2.rest_0_, bf16[2,128,1536]{2,1,0:T(8,128)(2,1)S(1)} %collective-permute-done.15.rest_1_, bf16[2,128,1536]{2,1,0:T(8,128)(2,1)} %pad_maximum_fusion.rest_2_, ...), custom_call_target="tpu_custom_call" | custom-call | bytes 6291456 | tf_op jit(solution)/shard_map/put_together/pallas_call | solution.py:228
  87.9 2.8 %collective-permute-done.18.rest_1_.rest_0_ = bf16[2,512,1536]{2,1,0:T(8,128)(2,1)} collective-permute-done((bf16[2,512,1536]{2,1,0:T(8,128)(2,1)}, bf16[2,512,1536]{2,1,0:T(8,128)(2,1)}, u32[]{:S(2)}, u32[]{:S(2)}) %collective-permute-start.18) | collective-permute-done | bytes 3145760 | tf_op jit(solution)/shard_map/gradients_core/ppermute | solution.py:19
  90.7 11.6 %hidden_gradient.2.rest_3_ = bf16[512,1024]{1,0:T(8,128)(2,1)S(1)} custom-call(s32[4]{0:T(128)S(1)} %pad_add_fusion.2.table, f32[512,1]{1,0:T(8,128)S(1)} %copy.29.gates, bf16[1024,6144]{1,0:T(8,128)(2,1)} %bitcast.71, bf16[2,512,1536]{2,1,0:T(8,128)(2,1)} %put_together.2.rest_0_, bf16[2,512,1536]{2,1,0:T(8,128)(2,1)} %collective-permute-done.18.rest_1_.rest_0_), custom_call_target="tpu_custom_call" | custom-call | flops 6442450944 | bytes 18874368 | tf_op jit(solution)/shard_map/hidden_gradient/pallas_call | solution.py:351
  103.3 2.0 %collective-permute-done.17.rest_3_ = bf16[2,128,1536]{2,1,0:T(8,128)(2,1)} collective-permute-done((bf16[2,128,1536]{2,1,0:T(8,128)(2,1)}, bf16[2,128,1536]{2,1,0:T(8,128)(2,1)}, u32[]{:S(2)}, u32[]{:S(2)}) %collective-permute-start.17) | collective-permute-done | bytes 786464 | tf_op jit(solution)/shard_map/plane_3_second/ppermute | solution.py:19
  105.3 3.2 %put_together.3.rest_1_.rest_0_ = bf16[2,512,1536]{2,1,0:T(8,128)(2,1)} custom-call(s32[1]{0:T(128)} %bitcast.20.swapped, bf16[2,128,1536]{2,1,0:T(8,128)(2,1)S(1)} %pad_maximum_fusion.1.rest_0_, bf16[2,128,1536]{2,1,0:T(8,128)(2,1)} %collective-permute-done.13.rest_1_, bf16[2,128,1536]{2,1,0:T(8,128)(2,1)} %pad_maximum_fusion.3.rest_2_, ...), custom_call_target="tpu_custom_call" | custom-call | bytes 6291456 | tf_op jit(solution)/shard_map/put_together/pallas_call | solution.py:228
  108.6 1.5 collective-permute-start.12
  113.3 1.6 copy-done.2
  114.9 6.2 %weight_gradient.4.rest_2_ = bf16[1024,6144]{1,0:T(8,128)(2,1)} custom-call(s32[1]{0:T(128)S(1)} %bitcast.66, bf16[1024,1024]{1,0:T(8,128)(2,1)S(1)} %bitcast.59, bf16[2,512,1536]{2,1,0:T(8,128)(2,1)} %put_together.2.rest_0_, bf16[2,512,1536]{2,1,0:T(8,128)(2,1)} %put_together.3.rest_1_.rest_0_), custom_call_target="tpu_custom_call" | custom-call | flops 3221225472 | bytes 8388608 | tf_op jit(solution)/shard_map/weight_gradient/pallas_call | solution.py:274
  122.6 1.5 collective-permute-start.23
  124.2 15.4 %hidden_gradient.3 = bf16[1024,1024]{1,0:T(8,128)(2,1)} custom-call(s32[4]{0:T(128)S(1)} %pad_add_fusion.2.table, f32[512,1]{1,0:T(8,128)S(1)} %copy.30.gates, bf16[1024,6144]{1,0:T(8,128)(2,1)} %bitcast.72, bf16[2,512,1536]{2,1,0:T(8,128)(2,1)} %put_together.3.rest_1_.rest_0_, bf16[2,512,1536]{2,1,0:T(8,128)(2,1)} %collective-permute-done.19.rest_1_, ...), custom_call_target="tpu_custom_call" | custom-call | flops 8589934592 | bytes 18874368 | tf_op jit(solution)/shard_map/hidden_gradient/pallas_call | solution.py:351
  142.4 6.9 %weight_gradient.5.rest_2_ = bf16[1024,6144]{1,0:T(8,128)(2,1)} custom-call(s32[1]{0:T(128)} %slice.105.quarters, bf16[1024,1024]{1,0:T(8,128)(2,1)S(1)} %bitcast.60, bf16[2,512,1536]{2,1,0:T(8,128)(2,1)} %put_together.2.rest_0_, bf16[2,512,1536]{2,1,0:T(8,128)(2,1)} %put_together.3.rest_1_.rest_0_, ...), custom_call_target="tpu_custom_call", output_to_operand_aliasing={{}: (4, {})} | custom-call | flops 3221225472 | bytes 8388608 | tf_op jit(solution)/shard_map/weight_gradient/pallas_call | solution.py:274
  152.0 3.1 %collective-permute-start.29 = (bf16[128,1536]{1,0:T(8,128)(2,1)S(1)}, bf16[128,1536]{1,0:T(8,128)(2,1)S(1)}, u32[]{:S(2)}, u32[]{:S(2)}) collective-permute-start(bf16[128,1536]{1,0:T(8,128)(2,1)S(1)} %add.158), channel_id=1, source_target_pairs={{0,8},{1,9},{2,10},{3,11},{4,12},{5,13},{6,14},{7,15},{8,16},{9,17... | collective-permute-start | bytes 1179656 | tf_op jit(solution)/shard_map/sum_3_z/ppermute | solution.py:19
  155.2 6.3 %weight_gradient.6.rest_2_ = bf16[1024,6144]{1,0:T(8,128)(2,1)} custom-call(s32[1]{0:T(128)S(1)} %bitcast.64, bf16[1024,1024]{1,0:T(8,128)(2,1)S(1)} %bitcast.61, bf16[2,512,1536]{2,1,0:T(8,128)(2,1)} %collective-permute-done.18.rest_1_.rest_0_, bf16[2,512,1536]{2,1,0:T(8,128)(2,1)} %collective-permute-done.19.rest_1_, ...), custom_call_target="tpu_custom_call", output_to_operand_aliasing={{}: (4, {})} | custom-call | flops 3221225472 | bytes 8388608 | tf_op jit(solution)/shard_map/weight_gradient/pallas_call | solution.py:274
  161.5 1.7 collective-permute-start.27
  165.3 7.0 %weight_gradient.7 = bf16[1024,6144]{1,0:T(8,128)(2,1)} custom-call(s32[1]{0:T(128)} %slice.111.quarters, bf16[1024,1024]{1,0:T(8,128)(2,1)S(1)} %bitcast.62, bf16[2,512,1536]{2,1,0:T(8,128)(2,1)} %collective-permute-done.18.rest_1_.rest_0_, bf16[2,512,1536]{2,1,0:T(8,128)(2,1)} %collective-permute-done.19.rest_1_, ...), custom_call_target="tpu_custom_call", output_to_operand_aliasing={{}: (4, {})} | custom-call | flops 3221225472 | bytes 8388608 | tf_op jit(solution)/shard_map/weight_gradient/pallas_call | solution.py:274
  173.0 6.5 %collective-permute-done.28 = bf16[128,1536]{1,0:T(8,128)(2,1)S(1)} collective-permute-done((bf16[128,1536]{1,0:T(8,128)(2,1)S(1)}, bf16[128,1536]{1,0:T(8,128)(2,1)S(1)}, u32[]{:S(2)}, u32[]{:S(2)}) %collective-permute-start.28) | collective-permute-done | bytes 393248 | tf_op jit(solution)/shard_map/sum_2_z/ppermute | solution.py:19
  179.5 6.0 %collective-permute-done.27 = bf16[128,1536]{1,0:T(8,128)(2,1)S(1)} collective-permute-done((bf16[128,1536]{1,0:T(8,128)(2,1)S(1)}, bf16[128,1536]{1,0:T(8,128)(2,1)S(1)}, u32[]{:S(2)}, u32[]{:S(2)}) %collective-permute-start.27) | collective-permute-done | bytes 393248 | tf_op jit(solution)/shard_map/sum_1_z/ppermute | solution.py:19
  (120 shorter events, 34.1 us)
Async XLA Ops:
  0.6 23.8 %copy-start = (bf16[1,1024,1024]{2,1,0:T(8,128)(2,1)S(1)}, bf16[1,1024,1024]{2,1,0:T(8,128)(2,1)}, u32[]{:S(2)}) copy-start(bf16[1,1024,1024]{2,1,0:T(8,128)(2,1)} %param.5) | copy-start | bytes 6291460
  2.2 4.5 %collective-permute-start = (f32[4,128]{1,0:T(4,128)S(1)}, f32[4,128]{1,0:T(4,128)S(1)}, u32[]{:S(2)}, u32[]{:S(2)}) collective-permute-start(f32[4,128]{1,0:T(4,128)S(1)} %get-tuple-element.172), channel_id=1, source_target_pairs={{0,4},{1,5},{2,6},{3,7},{4,0},{5,1},{6,2},{7,3},{8,12},{9,13},{10,... | collective-permute-start | bytes 6152 | tf_op jit(solution)/shard_map/routes_y/ppermute | solution.py:19
  5.1 26.0 %collective-permute-start.4 = (bf16[128,1536]{1,0:T(8,128)(2,1)}, bf16[128,1536]{1,0:T(8,128)(2,1)S(1)}, u32[]{:S(2)}, u32[]{:S(2)}) collective-permute-start(bf16[128,1536]{1,0:T(8,128)(2,1)} %param.7), channel_id=1, source_target_pairs={{0,4},{1,3},{2,6},{3,1},{4,0},{5,7},{6,2},{7,5},{8,12},{9,11},{10,... | collective-permute-start | bytes 1179656 | tf_op jit(solution)/shard_map/own_first/ppermute | solution.py:19
  6.7 6.8 %collective-permute-start.5 = (f32[2,4,128]{2,1,0:T(4,128)S(1)}, f32[2,4,128]{2,1,0:T(4,128)S(1)}, u32[]{:S(2)}, u32[]{:S(2)}) collective-permute-start(f32[2,4,128]{2,1,0:T(4,128)S(1)} %pad_maximum_fusion.4), channel_id=1, source_target_pairs={{0,8},{1,9},{2,10},{3,11},{4,12},{5,13},{6,14},{7,15},{8,16},{9,17... | collective-permute-start | bytes 12296 | tf_op jit(solution)/shard_map/routes_z/ppermute | solution.py:19
  8.8 7.0 %collective-permute-start.7 = (f32[2,4,128]{2,1,0:T(4,128)S(1)}, f32[2,4,128]{2,1,0:T(4,128)S(1)}, u32[]{:S(2)}, u32[]{:S(2)}) collective-permute-start(f32[2,4,128]{2,1,0:T(4,128)S(1)} %pad_maximum_fusion.4), channel_id=1, source_target_pairs={{0,24},{1,25},{2,26},{3,27},{4,28},{5,29},{6,30},{7,31},{8,0},{9,1... | collective-permute-start | bytes 12296 | tf_op jit(solution)/shard_map/routes_z/ppermute | solution.py:19
  10.9 4.9 %collective-permute-start.6 = (f32[2,4,128]{2,1,0:T(4,128)S(1)}, f32[2,4,128]{2,1,0:T(4,128)S(1)}, u32[]{:S(2)}, u32[]{:S(2)}) collective-permute-start(f32[2,4,128]{2,1,0:T(4,128)S(1)} %pad_maximum_fusion.4), channel_id=1, source_target_pairs={{0,16},{1,17},{2,18},{3,19},{4,20},{5,21},{6,22},{7,23},{8,24},{9,... | collective-permute-start | bytes 12296 | tf_op jit(solution)/shard_map/routes_z/ppermute | solution.py:19
  11.9 11.8 %collective-permute-start.1 = (bf16[128,1536]{1,0:T(8,128)(2,1)}, bf16[128,1536]{1,0:T(8,128)(2,1)S(1)}, u32[]{:S(2)}, u32[]{:S(2)}) collective-permute-start(bf16[128,1536]{1,0:T(8,128)(2,1)} %param.7), channel_id=1, source_target_pairs={{0,8},{1,9},{2,10},{3,11},{4,12},{5,13},{6,14},{7,15},{8,16},{9,17... | collective-permute-start | bytes 1179656 | tf_op jit(solution)/shard_map/plane_1/ppermute | solution.py:19
  23.7 13.8 %collective-permute-start.3 = (bf16[128,1536]{1,0:T(8,128)(2,1)S(1)}, bf16[128,1536]{1,0:T(8,128)(2,1)}, u32[]{:S(2)}, u32[]{:S(2)}) collective-permute-start(bf16[128,1536]{1,0:T(8,128)(2,1)S(1)} %collective-permute-done.1), channel_id=1, source_target_pairs={{0,4},{1,3},{2,6},{3,1},{4,0},{5,7},{6,2},{7,5},{8,12},{9,11},{10,... | collective-permute-start | bytes 1179656 | tf_op jit(solution)/shard_map/plane_1_first/ppermute | solution.py:19
  24.4 13.1 %collective-permute-start.2 = (bf16[128,1536]{1,0:T(8,128)(2,1)S(1)}, bf16[128,1536]{1,0:T(8,128)(2,1)S(1)}, u32[]{:S(2)}, u32[]{:S(2)}) collective-permute-start(bf16[128,1536]{1,0:T(8,128)(2,1)S(1)} %collective-permute-done.1), channel_id=1, source_target_pairs={{0,8},{1,9},{2,10},{3,11},{4,12},{5,13},{6,14},{7,15},{8,16},{9,17... | collective-permute-start | bytes 1179656 | tf_op jit(solution)/shard_map/plane_2/ppermute | solution.py:19
  37.4 24.6 %collective-permute-start.10 = (bf16[1024,1536]{1,0:T(8,128)(2,1)}, bf16[1024,1536]{1,0:T(8,128)(2,1)}, u32[]{:S(2)}, u32[]{:S(2)}) collective-permute-start(bf16[1024,1536]{1,0:T(8,128)(2,1)} %forward_sent.2), channel_id=1, source_target_pairs={{0,1},{1,0},{2,3},{3,2},{4,5},{5,4},{6,7},{7,6},{8,9},{9,8},{10,11... | collective-permute-start | bytes 9437192 | tf_op jit(solution)/shard_map/forward_core/ppermute | solution.py:19
  46.9 23.7 %collective-permute-start.11 = (bf16[1024,1536]{1,0:T(8,128)(2,1)}, bf16[1024,1536]{1,0:T(8,128)(2,1)}, u32[]{:S(2)}, u32[]{:S(2)}) collective-permute-start(bf16[1024,1536]{1,0:T(8,128)(2,1)} %forward_sent.3), channel_id=1, source_target_pairs={{0,1},{1,0},{2,3},{3,2},{4,5},{5,4},{6,7},{7,6},{8,9},{9,8},{10,11... | collective-permute-start | bytes 9437192 | tf_op jit(solution)/shard_map/forward_core/ppermute | solution.py:19
  47.4 11.8 %collective-permute-start.9 = (bf16[128,1536]{1,0:T(8,128)(2,1)S(1)}, bf16[128,1536]{1,0:T(8,128)(2,1)}, u32[]{:S(2)}, u32[]{:S(2)}) collective-permute-start(bf16[128,1536]{1,0:T(8,128)(2,1)S(1)} %collective-permute-done.2), channel_id=1, source_target_pairs={{0,4},{1,3},{2,6},{3,1},{4,0},{5,7},{6,2},{7,5},{8,12},{9,11},{10,... | collective-permute-start | bytes 1179656 | tf_op jit(solution)/shard_map/plane_2_first/ppermute | solution.py:19
  48.8 32.8 %collective-permute-start.15 = (bf16[2,128,1536]{2,1,0:T(8,128)(2,1)S(1)}, bf16[2,128,1536]{2,1,0:T(8,128)(2,1)S(1)}, u32[]{:S(2)}, u32[]{:S(2)}) collective-permute-start(bf16[2,128,1536]{2,1,0:T(8,128)(2,1)S(1)} %pad_maximum_fusion.2.rest_0_), channel_id=1, source_target_pairs={{0,2},{1,5},{2,0},{3,7},{4,6},{5,1},{6,4},{7,3},{8,10},{9,13},{10,... | collective-permute-start | bytes 2359304 | tf_op jit(solution)/shard_map/own_second/ppermute | solution.py:19
  49.5 19.3 %collective-permute-start.8 = (bf16[128,1536]{1,0:T(8,128)(2,1)S(1)}, bf16[128,1536]{1,0:T(8,128)(2,1)S(1)}, u32[]{:S(2)}, u32[]{:S(2)}) collective-permute-start(bf16[128,1536]{1,0:T(8,128)(2,1)S(1)} %collective-permute-done.2), channel_id=1, source_target_pairs={{0,8},{1,9},{2,10},{3,11},{4,12},{5,13},{6,14},{7,15},{8,16},{9,17... | collective-permute-start | bytes 1179656 | tf_op jit(solution)/shard_map/plane_3/ppermute | solution.py:19
  59.1 22.5 %collective-permute-start.16 = (bf16[2,128,1536]{2,1,0:T(8,128)(2,1)}, bf16[2,128,1536]{2,1,0:T(8,128)(2,1)S(1)}, u32[]{:S(2)}, u32[]{:S(2)}) collective-permute-start(bf16[2,128,1536]{2,1,0:T(8,128)(2,1)} %pad_maximum_fusion.rest_2_), channel_id=1, source_target_pairs={{0,2},{1,5},{2,0},{3,7},{4,6},{5,1},{6,4},{7,3},{8,10},{9,13},{10,... | collective-permute-start | bytes 2359304 | tf_op jit(solution)/shard_map/plane_1_second/ppermute | solution.py:19
  68.8 12.8 %collective-permute-start.14 = (bf16[128,1536]{1,0:T(8,128)(2,1)S(1)}, bf16[128,1536]{1,0:T(8,128)(2,1)S(1)}, u32[]{:S(2)}, u32[]{:S(2)}) collective-permute-start(bf16[128,1536]{1,0:T(8,128)(2,1)S(1)} %collective-permute-done.8), channel_id=1, source_target_pairs={{0,4},{1,3},{2,6},{3,1},{4,0},{5,7},{6,2},{7,5},{8,12},{9,11},{10,... | collective-permute-start | bytes 1179656 | tf_op jit(solution)/shard_map/plane_3_first/ppermute | solution.py:19
  84.6 6.1 %collective-permute-start.18 = (bf16[2,512,1536]{2,1,0:T(8,128)(2,1)}, bf16[2,512,1536]{2,1,0:T(8,128)(2,1)}, u32[]{:S(2)}, u32[]{:S(2)}) collective-permute-start(bf16[2,512,1536]{2,1,0:T(8,128)(2,1)} %put_together.2.rest_0_), channel_id=1, source_target_pairs={{0,1},{1,0},{2,3},{3,2},{4,5},{5,4},{6,7},{7,6},{8,9},{9,8},{10,11... | collective-permute-start | bytes 9437192 | tf_op jit(solution)/shard_map/gradients_core/ppermute | solution.py:19
  84.8 18.5 %collective-permute-start.13 = (bf16[2,128,1536]{2,1,0:T(8,128)(2,1)S(1)}, bf16[2,128,1536]{2,1,0:T(8,128)(2,1)}, u32[]{:S(2)}, u32[]{:S(2)}) collective-permute-start(bf16[2,128,1536]{2,1,0:T(8,128)(2,1)S(1)} %pad_maximum_fusion.1.rest_0_), channel_id=1, source_target_pairs={{0,2},{1,5},{2,0},{3,7},{4,6},{5,1},{6,4},{7,3},{8,10},{9,13},{10,... | collective-permute-start | bytes 2359304 | tf_op jit(solution)/shard_map/plane_2_second/ppermute | solution.py:19
  87.2 18.1 %collective-permute-start.17 = (bf16[2,128,1536]{2,1,0:T(8,128)(2,1)}, bf16[2,128,1536]{2,1,0:T(8,128)(2,1)}, u32[]{:S(2)}, u32[]{:S(2)}) collective-permute-start(bf16[2,128,1536]{2,1,0:T(8,128)(2,1)} %pad_maximum_fusion.3.rest_2_), channel_id=1, source_target_pairs={{0,2},{1,5},{2,0},{3,7},{4,6},{5,1},{6,4},{7,3},{8,10},{9,13},{10,... | collective-permute-start | bytes 2359304 | tf_op jit(solution)/shard_map/plane_3_second/ppermute | solution.py:19
  108.6 15.6 %collective-permute-start.19 = (bf16[2,512,1536]{2,1,0:T(8,128)(2,1)}, bf16[2,512,1536]{2,1,0:T(8,128)(2,1)}, u32[]{:S(2)}, u32[]{:S(2)}) collective-permute-start(bf16[2,512,1536]{2,1,0:T(8,128)(2,1)} %put_together.3.rest_1_.rest_0_), channel_id=1, source_target_pairs={{0,1},{1,0},{2,3},{3,2},{4,5},{5,4},{6,7},{7,6},{8,9},{9,8},{10,11... | collective-permute-start | bytes 9437192 | tf_op jit(solution)/shard_map/gradients_core/ppermute | solution.py:19
  108.6 12.5 %collective-permute-start.12 = (bf16[2,128,1536]{2,1,0:T(8,128)(2,1)}, bf16[2,128,1536]{2,1,0:T(8,128)(2,1)}, u32[]{:S(2)}, u32[]{:S(2)}) collective-permute-start(bf16[2,128,1536]{2,1,0:T(8,128)(2,1)} %get-tuple-element.113), channel_id=1, source_target_pairs={{0,2},{1,5},{2,0},{3,7},{4,6},{5,1},{6,4},{7,3},{8,10},{9,13},{10,... | collective-permute-start | bytes 2359304 | tf_op jit(solution)/shard_map/sum_2/ppermute | solution.py:19
  111.2 28.4 %collective-permute-start.21 = (bf16[2,128,1536]{2,1,0:T(8,128)(2,1)}, bf16[2,128,1536]{2,1,0:T(8,128)(2,1)S(1)}, u32[]{:S(2)}, u32[]{:S(2)}) collective-permute-start(bf16[2,128,1536]{2,1,0:T(8,128)(2,1)} %get-tuple-element.124), channel_id=1, source_target_pairs={{0,2},{1,5},{2,0},{3,7},{4,6},{5,1},{6,4},{7,3},{8,10},{9,13},{10,... | collective-permute-start | bytes 2359304 | tf_op jit(solution)/shard_map/sum_3/ppermute | solution.py:19
  111.8 37.4 %collective-permute-start.24 = (bf16[2,128,1536]{2,1,0:T(8,128)(2,1)}, bf16[2,128,1536]{2,1,0:T(8,128)(2,1)S(1)}, u32[]{:S(2)}, u32[]{:S(2)}) collective-permute-start(bf16[2,128,1536]{2,1,0:T(8,128)(2,1)} %get-tuple-element.130), channel_id=1, source_target_pairs={{0,2},{1,5},{2,0},{3,7},{4,6},{5,1},{6,4},{7,3},{8,10},{9,13},{10,... | collective-permute-start | bytes 2359304 | tf_op jit(solution)/shard_map/sum_1/ppermute | solution.py:19
  122.6 17.8 %collective-permute-start.23 = (bf16[128,1536]{1,0:T(8,128)(2,1)S(1)}, bf16[128,1536]{1,0:T(8,128)(2,1)S(1)}, u32[]{:S(2)}, u32[]{:S(2)}) collective-permute-start(bf16[128,1536]{1,0:T(8,128)(2,1)S(1)} %get-tuple-element.133), channel_id=1, source_target_pairs={{0,4},{1,3},{2,6},{3,1},{4,0},{5,7},{6,2},{7,5},{8,12},{9,11},{10,... | collective-permute-start | bytes 1179656 | tf_op jit(solution)/shard_map/sum_2/ppermute | solution.py:19
  139.8 12.1 %collective-permute-start.22 = (bf16[128,1536]{1,0:T(8,128)(2,1)S(1)}, bf16[128,1536]{1,0:T(8,128)(2,1)S(1)}, u32[]{:S(2)}, u32[]{:S(2)}) collective-permute-start(bf16[128,1536]{1,0:T(8,128)(2,1)S(1)} %get-tuple-element.140), channel_id=1, source_target_pairs={{0,4},{1,3},{2,6},{3,1},{4,0},{5,7},{6,2},{7,5},{8,12},{9,11},{10,... | collective-permute-start | bytes 1179656 | tf_op jit(solution)/shard_map/sum_3/ppermute | solution.py:19
  140.7 22.5 %collective-permute-start.20 = (bf16[2,128,1536]{2,1,0:T(8,128)(2,1)S(1)}, bf16[2,128,1536]{2,1,0:T(8,128)(2,1)S(1)}, u32[]{:S(2)}, u32[]{:S(2)}) collective-permute-start(bf16[2,128,1536]{2,1,0:T(8,128)(2,1)S(1)} %copy-done.13), channel_id=1, source_target_pairs={{0,2},{1,5},{2,0},{3,7},{4,6},{5,1},{6,4},{7,3},{8,10},{9,13},{10,... | collective-permute-start | bytes 2359304 | tf_op jit(solution)/shard_map/sum_0/ppermute | solution.py:19
  149.5 11.9 %collective-permute-start.26 = (bf16[128,1536]{1,0:T(8,128)(2,1)S(1)}, bf16[128,1536]{1,0:T(8,128)(2,1)S(1)}, u32[]{:S(2)}, u32[]{:S(2)}) collective-permute-start(bf16[128,1536]{1,0:T(8,128)(2,1)S(1)} %get-tuple-element.147), channel_id=1, source_target_pairs={{0,4},{1,3},{2,6},{3,1},{4,0},{5,7},{6,2},{7,5},{8,12},{9,11},{10,... | collective-permute-start | bytes 1179656 | tf_op jit(solution)/shard_map/sum_1/ppermute | solution.py:19
  150.6 28.9 %collective-permute-start.28 = (bf16[128,1536]{1,0:T(8,128)(2,1)S(1)}, bf16[128,1536]{1,0:T(8,128)(2,1)S(1)}, u32[]{:S(2)}, u32[]{:S(2)}) collective-permute-start(bf16[128,1536]{1,0:T(8,128)(2,1)S(1)} %add.157), channel_id=1, source_target_pairs={{0,16},{1,17},{2,18},{3,19},{4,20},{5,21},{6,22},{7,23},{8,24},{9,... | collective-permute-start | bytes 1179656 | tf_op jit(solution)/shard_map/sum_2_z/ppermute | solution.py:19
  152.0 21.0 %collective-permute-start.29 = (bf16[128,1536]{1,0:T(8,128)(2,1)S(1)}, bf16[128,1536]{1,0:T(8,128)(2,1)S(1)}, u32[]{:S(2)}, u32[]{:S(2)}) collective-permute-start(bf16[128,1536]{1,0:T(8,128)(2,1)S(1)} %add.158), channel_id=1, source_target_pairs={{0,8},{1,9},{2,10},{3,11},{4,12},{5,13},{6,14},{7,15},{8,16},{9,17... | collective-permute-start | bytes 1179656 | tf_op jit(solution)/shard_map/sum_3_z/ppermute | solution.py:19
  161.5 23.9 %collective-permute-start.27 = (bf16[128,1536]{1,0:T(8,128)(2,1)S(1)}, bf16[128,1536]{1,0:T(8,128)(2,1)S(1)}, u32[]{:S(2)}, u32[]{:S(2)}) collective-permute-start(bf16[128,1536]{1,0:T(8,128)(2,1)S(1)} %add.161), channel_id=1, source_target_pairs={{0,24},{1,25},{2,26},{3,27},{4,28},{5,29},{6,30},{7,31},{8,0},{9,1... | collective-permute-start | bytes 1179656 | tf_op jit(solution)/shard_map/sum_1_z/ppermute | solution.py:19
  163.4 22.0 %collective-permute-start.25 = (bf16[128,1536]{1,0:T(8,128)(2,1)S(1)}, bf16[128,1536]{1,0:T(8,128)(2,1)S(1)}, u32[]{:S(2)}, u32[]{:S(2)}) collective-permute-start(bf16[128,1536]{1,0:T(8,128)(2,1)S(1)} %get-tuple-element.151), channel_id=1, source_target_pairs={{0,4},{1,3},{2,6},{3,1},{4,0},{5,7},{6,2},{7,5},{8,12},{9,11},{10,... | collective-permute-start | bytes 1179656 | tf_op jit(solution)/shard_map/sum_0/ppermute | solution.py:19
  165.3 21.2 %copy-start.1 = (bf16[1,1024,1024]{2,1,0:T(8,128)(2,1)S(1)}, bf16[1,1024,1024]{2,1,0:T(8,128)(2,1)}, u32[]{:S(2)}) copy-start(bf16[1,1024,1024]{2,1,0:T(8,128)(2,1)} %param.5) | copy-start | bytes 6291460
  (15 other events, 63.0 us)

commit v3 on v2

v3 whole, which is shorter than its diff:
```python
import functools
import jax
import jax.numpy as jnp
from jax import lax
from jax.experimental import pallas as pl
from jax.experimental.pallas import tpu as pltpu
from jax.sharding import PartitionSpec as P

BF16, F32 = jnp.bfloat16, jnp.float32
ALL = ("dp", "expert")
VMEM = 44 * 2**20


def cost(flops, moved):
    return pl.CostEstimate(flops=flops, bytes_accessed=moved, transcendentals=0)


class Ring:
    def __init__(self, size, perm):
        self.size, self.perm = size, perm

    def shift(self, block):
        return lax.ppermute(block, ALL, self.perm)

    def gather(self, block):
        blocks = [block]
        for _ in range(self.size - 1):
            blocks.append(self.shift(blocks[-1]))
        return blocks

    def scatter(self, blocks):
        if self.size == 1:
            return blocks[0]
        total = blocks[1]
        for j in list(range(2, self.size)) + [0]:
            total = blocks[j] + self.shift(total)
        return total


class Layout:
    def __init__(self):
        self.groups, self.owners = lax.axis_size("dp"), lax.axis_size("expert")
        self.nc = 2 if self.owners % 2 == 0 else 1
        self.nx = self.owners // self.nc
        self.ny = self.nx if self.groups % self.nx == 0 else 1
        self.nz = self.groups // self.ny
        dp, expert = lax.axis_index("dp"), lax.axis_index("expert")
        self.z, self.y = dp // self.ny, dp % self.ny
        self.x, self.core = expert // self.nc, expert % self.nc
        self.mixed = self.nx == self.ny and self.nc == 2
        step = {
            "x": lambda z, y, x, c: (z, y, (x + 1) % self.nx, c),
            "y": lambda z, y, x, c: (z, (y + 1) % self.ny, x, c),
            "c": lambda z, y, x, c: (z, y, x, (c + 1) % self.nc),
        }
        swapped = lambda c: self.mixed and c == 1
        self.far_z = [
            self.ring(self.nz, lambda z, y, x, c, k=k: ((z + k) % self.nz, y, x, c))
            for k in range(self.nz)
        ]
        self.ring_y = self.ring(self.ny, step["y"])
        self.ring_c = self.ring(self.nc, step["c"])
        self.ring_1 = self.ring(
            self.ny, lambda z, y, x, c: step["x" if swapped(c) else "y"](z, y, x, c)
        )
        self.ring_2 = self.ring(
            self.nx, lambda z, y, x, c: step["y" if swapped(c) else "x"](z, y, x, c)
        )

    def ring(self, size, onward):
        flat = lambda z, y, x, c: ((z * self.ny + y) * self.nx + x) * self.nc + c
        perm = []
        for z in range(self.nz):
            for y in range(self.ny):
                for x in range(self.nx):
                    for c in range(self.nc):
                        perm.append((flat(z, y, x, c), flat(*onward(z, y, x, c))))
        return Ring(size, perm)


def tile_of(width, most):
    tile = most
    while width % tile:
        tile -= 128
    return tile


def rows_kernel(size, shards, slots, gates, *rest):
    hidden, (out, turned) = rest[:-2], rest[-2:]
    count = shards.shape[0]
    capacity = hidden[0].shape[0] // count
    numbers = lax.broadcasted_iota(jnp.int32, (size, capacity), 1)
    for e, source in enumerate(hidden):
        slot_columns, gate_columns = slots[e].T, gates[e].T
        for i in range(count):
            block = source[pl.ds(pl.multiple_of(shards[i] * capacity, capacity), capacity), :]
            chosen = (slot_columns[:, i : i + 1] == numbers).astype(F32).astype(BF16)
            picked = jnp.dot(chosen, block, preferred_element_type=F32)
            picked = (picked * gate_columns[:, i : i + 1]).astype(BF16)
            out[e, pl.ds(i * size, size), :] = picked
            if e == 0:
                turned[:, pl.ds(i * size, size)] = picked.T


def token_rows(slot_of, gates, hidden, shards):
    experts, count, size = gates.shape
    tokens = count * size
    slots, depth = hidden[0].shape
    tile = tile_of(depth, 512)
    narrow = pl.BlockSpec((experts, count, size), lambda j, t: (0, 0, 0))
    return pl.pallas_call(
        functools.partial(rows_kernel, size),
        grid_spec=pltpu.PrefetchScalarGridSpec(
            num_scalar_prefetch=1,
            grid=(depth // tile,),
            in_specs=[narrow, narrow]
            + [pl.BlockSpec((slots, tile), lambda j, t: (0, j)) for _ in hidden],
            out_specs=[
                pl.BlockSpec((experts, tokens, tile), lambda j, t: (0, 0, j)),
                pl.BlockSpec((tile, tokens), lambda j, t: (j, 0)),
            ],
        ),
        out_shape=[
            jax.ShapeDtypeStruct((experts, tokens, depth), BF16),
            jax.ShapeDtypeStruct((depth, tokens), BF16),
        ],
        compiler_params=pltpu.CompilerParams(vmem_limit_bytes=VMEM),
        cost_estimate=cost(2 * tokens * slots * depth, 4 * experts * tokens * depth),
        name="token_rows",
    )(shards, slot_of, gates, *hidden)


def place_kernel(jx, first_tile, ny, plan, mixed, experts, table, rows, *rest):
    weights = rest[:experts]
    stage, sems = rest[-2:]
    outs = rest[-2 - sum(len(group[3]) for group in plan) : -2]
    step, steps = pl.program_id(0), pl.num_programs(0)
    tile = weights[0].shape[1]
    acc = jnp.dot(rows[0], weights[0][...], preferred_element_type=F32)
    for e in range(1, experts):
        acc = acc + jnp.dot(rows[e], weights[e][...], preferred_element_type=F32)
    stage[step] = acc.astype(BF16)

    def copies(at, act):
        columns = pl.ds(pl.multiple_of((first_tile + at) * tile, 128), tile)
        for g, (first, stride, size, numbers) in enumerate(plan):
            for jy in range(ny):

                def copy(k1, k2, first=first + jy * stride, size=size, numbers=numbers, g=g, jy=jy):
                    act(
                        pltpu.make_async_copy(
                            stage.at[at, pl.ds(first, size), :],
                            outs[numbers[k1]].at[k2, :, columns],
                            sems.at[at, g * ny + jy],
                        )
                    )

                if not mixed or jx == jy:
                    copy(jx, jy)
                else:
                    pl.when(table[1] == 0)(functools.partial(copy, jx, jy))
                    pl.when(table[1] != 0)(functools.partial(copy, jy, jx))

    copies(step, lambda copy: copy.start())

    @pl.when(step == steps - 1)
    def _():
        for at in range(stage.shape[0]):
            copies(at, lambda copy: copy.wait())


def forward_placed(rows, weights, table, jx, part, parts, places, size, at, before):
    experts, tokens, depth = rows.shape
    width = weights[0].shape[1] // at.owners
    tile = tile_of(width // parts, 384)
    per = width // parts // tile
    plan, shapes = [], []
    for first, stride in places:
        plan.append((first, stride, size, [len(shapes) + k for k in range(at.nx)]))
        shapes += [jax.ShapeDtypeStruct((at.ny, size, width), BF16)] * at.nx
    block = pl.BlockSpec((depth, tile), lambda j, t: (0, (t[0] * parts + part) * per + j))
    specs = [pl.BlockSpec((experts, tokens, depth), lambda j, t: (0, 0, 0))] + [block] * experts
    operands = [rows] + list(weights)
    aliases = {}
    if before is not None:
        aliases = {1 + len(operands) + i: i for i in range(len(shapes))}
        specs += [pl.BlockSpec(memory_space=pltpu.HBM)] * len(shapes)
        operands += list(before)
    return pl.pallas_call(
        functools.partial(place_kernel, jx, part * per, at.ny, plan, at.mixed, experts),
        grid_spec=pltpu.PrefetchScalarGridSpec(
            num_scalar_prefetch=1,
            grid=(per,),
            in_specs=specs,
            out_specs=[pl.BlockSpec(memory_space=pltpu.HBM)] * len(shapes),
            scratch_shapes=[
                pltpu.VMEM((per, tokens, tile), BF16),
                pltpu.SemaphoreType.DMA((per, len(places) * at.ny)),
            ],
        ),
        out_shape=shapes,
        input_output_aliases=aliases,
        compiler_params=pltpu.CompilerParams(vmem_limit_bytes=VMEM),
        cost_estimate=cost(
            2 * experts * tokens * depth * tile * per, 2 * tile * per * (2 * depth + 2 * tokens)
        ),
        name="forward_placed",
    )(table, *operands)


def gather_kernel(plan, outputs, swapped, *rest):
    sources = max(item[0] for item in plan) + 1
    blocks, outs, (stage, loads, stores) = rest[:sources], rest[-3 - outputs : -3], rest[-3:]
    places, done = [], 0
    for i, (number, index, _, _, _, size) in enumerate(plan):
        places.append(stage.at[pl.ds(done, size)])
        done += size
        pltpu.make_async_copy(blocks[number].at[index], places[i], loads.at[i]).start()

    def store(i, act):
        _, _, (j1, j2), first, stride, size = plan[i]

        def copy(jy, jx):
            target = outs[jx].at[pl.ds(first + jy * stride, size)]
            act(pltpu.make_async_copy(places[i], target, stores.at[i]))

        if j1 == j2:
            copy(j1, j2)
        else:
            pl.when(swapped[0] == 0)(functools.partial(copy, j1, j2))
            if max(j1, j2) < outputs:
                pl.when(swapped[0] != 0)(functools.partial(copy, j2, j1))

    for i, (number, index, _, _, _, size) in enumerate(plan):
        pltpu.make_async_copy(blocks[number].at[index], places[i], loads.at[i]).wait()
        store(i, lambda copy: copy.start())
    for i in range(len(plan)):
        store(i, lambda copy: copy.wait())


def put_together(plan, blocks, swapped, count, shape):
    return pl.pallas_call(
        functools.partial(gather_kernel, plan, count),
        grid_spec=pltpu.PrefetchScalarGridSpec(
            num_scalar_prefetch=1,
            grid=(1,),
            in_specs=[pl.BlockSpec(memory_space=pl.ANY)] * len(blocks),
            out_specs=[pl.BlockSpec(memory_space=pltpu.HBM)] * count,
            scratch_shapes=[
                pltpu.VMEM((sum(item[5] for item in plan), shape[-1]), BF16),
                pltpu.SemaphoreType.DMA((len(plan),)),
                pltpu.SemaphoreType.DMA((len(plan),)),
            ],
        ),
        out_shape=[jax.ShapeDtypeStruct(shape, BF16)] * count,
        compiler_params=pltpu.CompilerParams(vmem_limit_bytes=VMEM),
        cost_estimate=cost(0, 4 * sum(b.size for b in blocks)),
        name="put_together",
    )(swapped, *blocks)


def weight_kernel(count, per, quarters, turned, *rest):
    sources = (len(rest) - 1) // count
    step = pl.program_id(0)
    for i in range(count):

        @pl.when(step // per == i)
        def _(i=i):
            total, first = None, 0
            for block in rest[i * sources : (i + 1) * sources]:
                size = block.shape[0]
                part = jnp.dot(
                    turned[:, first : first + size], block[...], preferred_element_type=F32
                )
                total = part if total is None else total + part
                first += size
            rest[-1][...] = total.astype(BF16)


def weight_gradient(turned, grads, quarters, shape, before):
    depth, tokens = turned.shape
    count = len(grads)
    width = grads[0][0].shape[1]
    tile = tile_of(width, 768)
    per = width // tile
    specs = [pl.BlockSpec((depth, tokens), lambda j, q: (0, 0))]
    operands = [turned]
    for i in range(count):
        for block in grads[i]:
            specs.append(
                pl.BlockSpec(
                    (block.shape[0], tile), lambda j, q, i=i: (0, jnp.clip(j - i * per, 0, per - 1))
                )
            )
            operands.append(block)
    aliases, extra = {}, []
    kernel = functools.partial(weight_kernel, count, per)
    if before is not None:
        specs.append(pl.BlockSpec(memory_space=pltpu.HBM))
        aliases = {len(operands) + 1: 0}
        operands.append(before)
        inner = kernel
        kernel = lambda quarters, turned, *rest: inner(quarters, turned, *rest[:-2], rest[-1])
    return pl.pallas_call(
        kernel,
        grid_spec=pltpu.PrefetchScalarGridSpec(
            num_scalar_prefetch=1,
            grid=(count * per,),
            in_specs=specs,
            out_specs=pl.BlockSpec((depth, tile), lambda j, q: (0, q[j // per] * per + j % per)),
        ),
        out_shape=jax.ShapeDtypeStruct(shape, BF16),
        input_output_aliases=aliases,
        compiler_params=pltpu.CompilerParams(vmem_limit_bytes=VMEM),
        cost_estimate=cost(
            2 * tokens * depth * width * count, 2 * count * width * (depth + tokens)
        ),
        name="weight_gradient",
    )(quarters, *operands)


def hidden_kernel(steps, each, count, last, table, gates, slots, weight, *rest):
    out, total = rest[-2:]
    sources = steps // each
    step = pl.program_id(0)
    size = total.shape[0] // count

    @pl.when(step == 0)
    def _():
        total[...] = jnp.zeros_like(total)

    for i, block in enumerate(rest[:sources]):

        @pl.when(step // each == i)
        def _(block=block):
            total[...] += lax.dot_general(
                block[...], weight[...], (((1,), (1,)), ((), ())), preferred_element_type=F32
            )

    @pl.when(step == steps - 1)
    def _():
        capacity = out.shape[0] // (2 * count if last else count)
        numbers = lax.broadcasted_iota(jnp.int32, (capacity, size), 0)
        gate_columns = gates[...].T
        for i in range(count):
            span = pl.ds(i * size, size)
            back = (total[span, :] * gate_columns[:, i : i + 1]).astype(BF16)
            chosen = (slots[pl.ds(i, 1), :] == numbers).astype(F32).astype(BF16)
            picked = jnp.dot(chosen, back, preferred_element_type=F32).astype(BF16)
            if last:
                before = rest[sources]
                place = table[steps + count + i] * capacity
                out[pl.ds(pl.multiple_of(place, capacity), capacity), :] = picked
                place = table[steps + i] * capacity
                old = before[pl.ds(i * capacity, capacity), :]
                out[pl.ds(pl.multiple_of(place, capacity), capacity), :] = old
            else:
                out[pl.ds(i * capacity, capacity), :] = picked


def hidden_gradient(gates, slots, grads, weight, quarters, capacity, shards=None, before=None):
    tokens, width = grads[0].shape
    depth = weight.shape[0]
    tile = tile_of(width, 1536)
    per = width // tile
    steps = per * len(grads)
    last = before is not None
    number = slots.shape[0]
    height = capacity * number * (2 if last else 1)
    table = jnp.repeat(quarters, per) if per > 1 else quarters
    if last:
        table = jnp.concatenate([table, shards])
    specs = [
        pl.BlockSpec(gates.shape, lambda s, t: (0, 0)),
        pl.BlockSpec(slots.shape, lambda s, t: (0, 0)),
        pl.BlockSpec((depth, tile), lambda s, t: (0, t[s] * per + s % per)),
    ]
    for i in range(len(grads)):

        def place(s, t, i=i):
            return (0, jnp.clip(s - i * per, 0, per - 1))

        specs.append(pl.BlockSpec((tokens, tile), place))
    operands = [gates, slots, weight] + list(grads)
    if last:
        specs.append(pl.BlockSpec(before.shape, lambda s, t: (0, 0)))
        operands.append(before)
    return pl.pallas_call(
        functools.partial(hidden_kernel, steps, per, number, last),
        grid_spec=pltpu.PrefetchScalarGridSpec(
            num_scalar_prefetch=1,
            grid=(steps,),
            in_specs=specs,
            out_specs=pl.BlockSpec((height, depth), lambda s, t: (0, 0)),
            scratch_shapes=[pltpu.VMEM((tokens, depth), F32)],
        ),
        out_shape=jax.ShapeDtypeStruct((height, depth), BF16),
        compiler_params=pltpu.CompilerParams(vmem_limit_bytes=VMEM),
        cost_estimate=cost(2 * steps * tile * tokens * depth, 2 * steps * tile * (depth + tokens)),
        name="hidden_gradient",
    )(table, *operands)


def tie(value, *others):
    return lax.optimization_barrier((value, others))[0]


def body(hidden, down_weight, grad_out, routing, gates):
    at = Layout()
    nx, ny, nz = at.nx, at.ny, at.nz
    rows, width = grad_out.shape
    top = routing.shape[1]
    slots = hidden.shape[1]
    capacity = slots // at.groups
    hidden_rows, weight = hidden[0], down_weight[0]

    turns = [list(range(nz // 2)), list(range(nz // 2, nz))]
    order = [(jz, jy) for turn in turns for jy in range(ny) for jz in turn]
    size = len(turns[0]) * rows
    half = ny * size
    places = [(0, size), (half, size)]
    swapped = ((at.core == 1) if at.mixed else (at.core < 0)).astype(jnp.int32)[None]
    back_x = (at.x - jnp.arange(nx)) % nx * at.nc
    mine = (back_x + at.core).astype(jnp.int32)
    theirs = (back_x + (at.core + at.nc - 1) % at.nc).astype(jnp.int32)
    two = at.nc > 1
    quarters = jnp.concatenate([mine, theirs]) if two else mine

    def both(block, name):
        with jax.named_scope(name):
            return [block, at.ring_c.shift(block)] if two else [block]

    def gathered(ring, block, name):
        with jax.named_scope(name):
            return ring.gather(block)

    def shifted(k, block, name):
        with jax.named_scope(name):
            return at.far_z[k % nz].shift(block)

    packed = jnp.concatenate([routing.astype(F32).T, gates.T])
    packed = jnp.stack(gathered(at.ring_y, packed, "routes_y"))
    hiddens = both(hidden_rows, "hidden_core")
    plane = [grad_out]
    first = [gathered(at.ring_1, grad_out, "own_first")]
    tables = [packed] + [shifted(jz, packed, "routes_z") for jz in range(1, nz)]
    plane.append(shifted(1, tie(grad_out, packed), "plane_1"))
    first[0] = jnp.stack(first[0])
    weights = both(tie(weight, packed, hiddens), "weight_core")
    second = [gathered(at.ring_2, first[0], "own_second")]
    packed = jnp.stack([tables[jz][jy] for jz, jy in order])

    expert = lax.axis_index("expert")
    ours = [expert, expert - at.core + 1 - at.core] if two else [expert]
    ours = jnp.stack(ours).astype(F32)[:, None, None, None]
    hits = packed[None, :, :top] == ours
    hit = hits.astype(F32).sum(axis=2)
    gate = jnp.where(hits, packed[None, :, top:], 0.0).sum(axis=2)
    earlier = (jnp.arange(rows)[:, None] < jnp.arange(rows)[None, :]).astype(BF16)
    place = jnp.dot(hit.astype(BF16), earlier, preferred_element_type=F32).astype(jnp.int32)
    shards = jnp.stack([(at.z - jz) % nz * ny + (at.y - jy) % ny for jz, jy in order])
    shards = shards.astype(jnp.int32)
    slot_of = jnp.where(hit > 0, place, -1)
    rows_in, turned = token_rows(slot_of, gate, hiddens, shards)
    slot_of, gate = slot_of[0], gate[0]
    plane[1], first[0] = tie((plane[1], first[0]), rows_in)
    plane.append(shifted(1, plane[1], "plane_2"))
    plane.append(shifted(nz - 1, tie(grad_out, plane[1]), "plane_3"))
    first.append(gathered(at.ring_1, plane[1], "plane_1_first"))

    calls = [(jx, 0, 1) for jx in range(nx - 1)] + [(nx - 1, 0, 2), (nx - 1, 1, 2)]
    forward_tables = [jnp.concatenate([mine[jx : jx + 1], swapped]) for jx in range(nx)]

    def forward(call, placed, *after):
        jx, part, parts = call
        table = tie(forward_tables[jx], *after)
        return forward_placed(rows_in, weights, table, jx, part, parts, places, size, at, placed)

    first[1] = jnp.stack(first[1])
    second.append(gathered(at.ring_2, first[1], "plane_1_second"))
    done = None
    for call in calls[:-2]:
        done = forward(call, done, plane[1], first[1])
    pair = jnp.stack(tie(plane[2:], done))
    first.append(gathered(at.ring_1, pair, "pair_first"))

    def assembled(blocks, turn):
        plan = []
        for i in range(len(blocks) // nx):
            for j2 in range(nx):
                for j1 in range(ny):
                    number = i * nx + j2
                    plan.append((number, j1, (j1, j2), i * rows, size, blocks[number].shape[1]))
        return list(put_together(plan, blocks, swapped, nx, (half, width)))

    done = forward(calls[-2], done, pair, first[1])
    first[2] = jnp.stack(tie(first[2], done)).reshape(ny, size, width)
    second.append(gathered(at.ring_2, first[2], "pair_second"))
    grads_1 = assembled(tie(second[0] + second[1], done), turns[0])
    others_1 = [both(block, "gradients_core")[-1] for block in grads_1] if two else []
    placed = forward(calls[-1], done, first[2], grads_1)

    class Sum:
        def __init__(self, turn):
            self.name = "sum_%d" % turn
            self.terms = list(placed[turn * nx : (turn + 1) * nx])

        def start(self, ring, after=()):
            with jax.named_scope(self.name):
                self.terms = tie(self.terms, after)
                total = self.terms[1]
                for j in range(2, ring.size):
                    total = self.terms[j] + ring.shift(total)
                self.sent = total
                self.got = ring.shift(total)

        def finish(self, after):
            self.terms = self.terms[0] + tie(self.got, after)

        def second(self):
            self.terms = [self.terms[j] for j in range(ny)]
            self.start(at.ring_1)

    near, far = Sum(0), Sum(1)
    far.start(at.ring_2)
    ask = tie(quarters, far.sent)
    count = len(order) // 2
    back = hidden_gradient(gate[:count], slot_of[:count], grads_1 + others_1, weight, ask, capacity)

    grads_2 = assembled(tie(second[2], back), turns[1])
    others_2 = [both(block, "gradients_core")[-1] for block in grads_2] if two else []
    ask = tie(mine, grads_2)
    grad_weight = weight_gradient(turned, list(zip(grads_1, grads_2)), ask, weight.shape, None)
    far.finish(grad_weight)
    far.second()
    near.start(at.ring_2)
    ask = tie(quarters, far.sent, near.sent)
    grad_hidden = hidden_gradient(
        gate[count:],
        slot_of[count:],
        grads_2 + others_2,
        weight,
        ask,
        capacity,
        shards,
        back,
    )
    far.finish(grad_hidden)
    near.finish(grad_hidden)
    near.second()
    last = shifted(nz - 3, far.terms[rows:], "sum_3_z")
    onward = shifted(nz - 1, far.terms[:rows], "sum_2_z")
    ask = tie(theirs, far.terms, near.sent)
    if two:
        grad_weight = weight_gradient(
            turned, list(zip(others_1, others_2)), ask, weight.shape, grad_weight
        )
    near.finish(grad_weight)
    onward = tie(onward, grad_weight) + near.terms[rows:]
    onward = shifted(nz - 1, onward, "sum_1_z")
    mixed_out = near.terms[:rows].astype(F32) + last.astype(F32) + onward.astype(F32)
    return (mixed_out.astype(BF16), grad_hidden[None], grad_weight[None])


def solution(mesh):
    return jax.shard_map(
        body,
        mesh=mesh,
        in_specs=(
            P("expert", None, "dp"),
            P("expert", "dp", None),
            P("dp", "expert"),
            P("dp", None),
            P("dp", None),
        ),
        out_specs=(P("dp", "expert"), P("expert", None, "dp"), P("expert", "dp", None)),
        check_vma=False,
    )
```

time: 187 us -> 169 us (0.904)
  waiting for transfers between devices: 38 us -> 25.3 us
  matrix products: 3.96 us -> 0.14 us
  local copies, waits for them, and re-layouts: 12.2 us -> 8.6 us
    ppermute x30 -> x26, waiting for transfers between devices: 38 us -> 25.3 us  [shift(): return lax.ppermute(block, ALL, self.perm)]
    dot_general x1 -> x0, matrix products: 3.86 us -> none  [body(): rows_in = jnp.dot(chosen, hidden_rows, preferred_element_type=F32)]
    convert_element_type x1 -> x0, local copies, waits for them, and re-layouts: 2.85 us -> none  [body(): rows_in = (rows_in * gate_column).astype(BF16)]
    add x7 -> x4, other arithmetic: 2.26 us -> 5.1 us  [finish(): self.terms = self.terms[0] + tie(self.got, after)]
    slice x7, local copies, waits for them, and re-layouts: 2.62 us -> 0.66 us  [the longest x1 0.58 us: body(): mine[jx:jx + 1]]
    pallas_call x12 -> x10, Pallas kernels: 87 us -> 88.5 us  [the longest x3 30.2 us: forward_placed(): pl.pallas_call(functools.partial(place_kernel, jx, part * per, at.ny, pla...]
    ppermute x30 -> x26, starting transfers between devices: 33 us -> 32 us  [shift(): return lax.ppermute(block, ALL, self.perm)]
    unnamed x40 -> x28, local copies, waits for them, and re-layouts: 6.43 us -> 6.33 us
  transfers between devices with their start and end apart: 30 -> 26, of which waited for: 10 -> 7; matrix products, arithmetic and copies ran while one was open for 10% -> 9% of each run, Pallas kernels for 43% -> 53%
where the time goes in v3:
time: 169 us; the launch traced here: 168 us
  Pallas kernels  88.5 us (52%)
  starting transfers between devices  32 us (19%)
  waiting for transfers between devices  25.3 us (15%)
  other arithmetic  13 us (8%)
  local copies, waits for them, and re-layouts  8.6 us (5%)
    ppermute x26, starting transfers between devices, shift(): return lax.ppermute(block, ALL, self.perm)  32 us
    pallas_call x3, Pallas kernels, forward_placed(): pl.pallas_call(functools.partial(place_kernel, jx, part * per, at.ny, pla...  30.2 us
    ppermute x26, waiting for transfers between devices, shift(): return lax.ppermute(block, ALL, self.perm)  25.3 us
    pallas_call x2, Pallas kernels, hidden_gradient(): pl.pallas_call(functools.partial(hidden_kernel, steps, per, number, last)...  24.7 us
    pallas_call x2, Pallas kernels, weight_gradient(): pl.pallas_call(kernel, grid_spec=pltpu.PrefetchScalarGridSpec(num_scalar_...  22.1 us
    pallas_call x1, Pallas kernels, token_rows(): pl.pallas_call(functools.partial(rows_kernel, size), grid_spec=pltpu.Pref...  6.59 us
    unnamed x28, local copies, waits for them, and re-layouts  6.33 us
    add x4, other arithmetic, finish(): self.terms = self.terms[0] + tie(self.got, after)  5.1 us
  transfers between devices with their start and end apart: 26, of which 7 were waited for; matrix products, arithmetic and copies ran while one was open for 9% of the time, Pallas kernels for 53%

profile of v3, /device:TPU:0, one launch (start us, length us, event | category | flops | bytes accessed | tf_op | source)
XLA Modules:
  0.0 168.5 jit_solution(13581932795818101185)
XLA Ops:
  2.5 2.5 %collective-permute-start = (f32[4,128]{1,0:T(4,128)S(1)}, f32[4,128]{1,0:T(4,128)S(1)}, u32[]{:S(2)}, u32[]{:S(2)}) collective-permute-start(f32[4,128]{1,0:T(4,128)S(1)} %get-tuple-element.122), channel_id=1, source_target_pairs={{0,4},{1,5},{2,6},{3,7},{4,0},{5,1},{6,2},{7,3},{8,12},{9,13},{10,... | collective-permute-start | bytes 6152 | tf_op jit(solution)/shard_map/routes_y/ppermute | solution.py:23
  5.0 1.6 collective-permute-done
  6.7 2.1 %collective-permute-start.2 = (bf16[128,1536]{1,0:T(8,128)(2,1)}, bf16[128,1536]{1,0:T(8,128)(2,1)S(1)}, u32[]{:S(2)}, u32[]{:S(2)}) collective-permute-start(bf16[128,1536]{1,0:T(8,128)(2,1)} %param.7), channel_id=1, source_target_pairs={{0,4},{1,3},{2,6},{3,1},{4,0},{5,7},{6,2},{7,5},{8,12},{9,11},{10,... | collective-permute-start | bytes 1179656 | tf_op jit(solution)/shard_map/own_first/ppermute | solution.py:23
  9.5 1.6 collective-permute-start.3
  11.2 2.2 %collective-permute-start.5 = (f32[2,4,128]{2,1,0:T(4,128)S(1)}, f32[2,4,128]{2,1,0:T(4,128)S(1)}, u32[]{:S(2)}, u32[]{:S(2)}) collective-permute-start(f32[2,4,128]{2,1,0:T(4,128)S(1)} %pad_maximum_fusion.4), channel_id=1, source_target_pairs={{0,24},{1,25},{2,26},{3,27},{4,28},{5,29},{6,30},{7,31},{8,0},{9,1... | collective-permute-start | bytes 12296 | tf_op jit(solution)/shard_map/routes_z/ppermute | solution.py:23
  15.9 2.1 %collective-permute-done.4 = f32[2,4,128]{2,1,0:T(4,128)S(1)} collective-permute-done((f32[2,4,128]{2,1,0:T(4,128)S(1)}, f32[2,4,128]{2,1,0:T(4,128)S(1)}, u32[]{:S(2)}, u32[]{:S(2)}) %collective-permute-start.4) | collective-permute-done | bytes 4128 | tf_op jit(solution)/shard_map/routes_z/ppermute | solution.py:23
  18.3 2.0 %pad_maximum_fusion.1.rest_0_ = bf16[2,128,1536]{2,1,0:T(8,128)(2,1)} fusion(bf16[1,128,1536]{2,1,0:T(8,128)(2,1)S(1)} %bitcast.61, bf16[1,128,1536]{2,1,0:T(8,128)(2,1)} %bitcast.5), kind=kLoop, calls=%fused_computation.7 | loop fusion | flops 393216 | bytes 1572864 | tf_op jit(solution)/shard_map/stack | solution.py:448
  20.2 1.6 copy-done.7
  21.8 6.6 %token_rows.1 = (bf16[2,1024,1024]{2,1,0:T(8,128)(2,1)}, bf16[1024,1024]{1,0:T(8,128)(2,1)S(1)}) custom-call(s32[8]{0:T(128)S(1)} %stack.98.shards, s32[2,8,128]{2,1,0:T(8,128)S(1)} %fusion.slots, f32[2,8,128]{2,1,0:T(8,128)S(1)} %get-tuple-element.107.gates, bf16[1024,1024]{1,0:T(8,128)(2,1)S(1)} %bitcast.51, ...), custom_call_target="tpu_custom_call" | custom-call | flops 2147483648 | bytes 8388608 | tf_op jit(solution)/shard_map/token_rows/pallas_call | solution.py:111
  31.4 1.6 collective-permute-start.12
  33.0 3.8 %collective-permute-start.8 = (bf16[128,1536]{1,0:T(8,128)(2,1)}, bf16[128,1536]{1,0:T(8,128)(2,1)S(1)}, u32[]{:S(2)}, u32[]{:S(2)}) collective-permute-start(bf16[128,1536]{1,0:T(8,128)(2,1)} %param.7), channel_id=1, source_target_pairs={{0,24},{1,25},{2,26},{3,27},{4,28},{5,29},{6,30},{7,31},{8,0},{9,1... | collective-permute-start | bytes 1179656 | tf_op jit(solution)/shard_map/plane_3/ppermute | solution.py:23
  36.9 5.0 %collective-permute-done.9 = bf16[128,1536]{1,0:T(8,128)(2,1)S(1)} collective-permute-done((bf16[128,1536]{1,0:T(8,128)(2,1)}, bf16[128,1536]{1,0:T(8,128)(2,1)S(1)}, u32[]{:S(2)}, u32[]{:S(2)}) %collective-permute-start.9) | collective-permute-done | bytes 393248 | tf_op jit(solution)/shard_map/plane_1_first/ppermute | solution.py:23
  43.0 2.0 %collective-permute-start.13 = (bf16[2,128,1536]{2,1,0:T(8,128)(2,1)S(1)}, bf16[2,128,1536]{2,1,0:T(8,128)(2,1)S(1)}, u32[]{:S(2)}, u32[]{:S(2)}) collective-permute-start(bf16[2,128,1536]{2,1,0:T(8,128)(2,1)S(1)} %pad_maximum_fusion.2.rest_2_), channel_id=1, source_target_pairs={{0,2},{1,5},{2,0},{3,7},{4,6},{5,1},{6,4},{7,3},{8,10},{9,13},{10,... | collective-permute-start | bytes 2359304 | tf_op jit(solution)/shard_map/plane_1_second/ppermute | solution.py:23
  45.0 13.6 %forward_placed.3 = (bf16[2,256,1536]{2,1,0:T(8,128)(2,1)S(1)}, bf16[2,256,1536]{2,1,0:T(8,128)(2,1)S(1)}, bf16[2,256,1536]{2,1,0:T(8,128)(2,1)S(1)}, bf16[2,256,1536]{2,1,0:T(8,128)(2,1)S(1)}) custom-call(s32[2]{0:T(128)S(1)} %pad_add_fusion.1.table, bf16[2,1024,1024]{2,1,0:T(8,128)(2,1)} %get-tuple-element.56.rows, bf16[1024,6144]{1,0:T(8,128)(2,1)} %bitcast.53, ...), custom_call_target="tpu_custom_call" | custom-call | flops 6442450944 | bytes 12582912 | tf_op jit(solution)/shard_map/forward_placed/pallas_call | solution.py:189
  59.4 8.3 %forward_placed.4 = (bf16[2,256,1536]{2,1,0:T(8,128)(2,1)S(1)}, bf16[2,256,1536]{2,1,0:T(8,128)(2,1)S(1)}, bf16[2,256,1536]{2,1,0:T(8,128)(2,1)S(1)}, bf16[2,256,1536]{2,1,0:T(8,128)(2,1)S(1)}) custom-call(s32[2]{0:T(128)S(1)} %pad_add_fusion.table, ...), custom_call_target="tpu_custom_call", output_to_operand_aliasing={{0}: (4, {}), {1}: (5, {}), {2}: (6, {}), {3}: (7, {})} | custom-call | flops 3221225472 | bytes 6291456 | tf_op jit(solution)/shard_map/forward_placed/pallas_call | solution.py:189
  67.8 2.9 %put_together.2 = (bf16[512,1536]{1,0:T(8,128)(2,1)}, bf16[512,1536]{1,0:T(8,128)(2,1)}) custom-call(s32[1]{0:T(128)} %bitcast.swapped, bf16[2,128,1536]{2,1,0:T(8,128)(2,1)} %pad_maximum_fusion.1.rest_0_, bf16[2,128,1536]{2,1,0:T(8,128)(2,1)S(1)} %collective-permute-done.12.rest_1_, bf16[2,128,1536]{2,1,0:T(8,128)(2,1)S(1)} %pad_maximum_fusion.2.rest_2_, ...), custom_call_target="tpu_custom_call" | custom-call | bytes 6291456 | tf_op jit(solution)/shard_map/put_together/pallas_call | solution.py:242
  71.8 8.3 %forward_placed.5 = (bf16[2,256,1536]{2,1,0:T(8,128)(2,1)S(1)}, bf16[2,256,1536]{2,1,0:T(8,128)(2,1)S(1)}, bf16[2,256,1536]{2,1,0:T(8,128)(2,1)S(1)}, bf16[2,256,1536]{2,1,0:T(8,128)(2,1)S(1)}) custom-call(s32[2]{0:T(128)S(1)} %pad_add_fusion.table, ...), custom_call_target="tpu_custom_call", output_to_operand_aliasing={{0}: (4, {}), {1}: (5, {}), {2}: (6, {}), {3}: (7, {})} | custom-call | flops 3221225472 | bytes 6291456 | tf_op jit(solution)/shard_map/forward_placed/pallas_call | solution.py:189
  80.1 1.9 %collective-permute-start.15 = (bf16[2,256,1536]{2,1,0:T(8,128)(2,1)S(1)}, bf16[2,256,1536]{2,1,0:T(8,128)(2,1)}, u32[]{:S(2)}, u32[]{:S(2)}) collective-permute-start(bf16[2,256,1536]{2,1,0:T(8,128)(2,1)S(1)} %get-tuple-element.88), channel_id=1, source_target_pairs={{0,2},{1,5},{2,0},{3,7},{4,6},{5,1},{6,4},{7,3},{8,10},{9,13},{10,... | collective-permute-start | bytes 4718600 | tf_op jit(solution)/shard_map/sum_1/ppermute | solution.py:23
  82.0 11.2 %hidden_gradient.2.rest_4_ = bf16[512,1024]{1,0:T(8,128)(2,1)S(1)} custom-call(s32[4]{0:T(128)S(1)} %pad_add_fusion.2.table, f32[4,128]{1,0:T(4,128)S(1)} %get-tuple-element.120.gates, s32[4,128]{1,0:T(4,128)S(1)} %get-tuple-element.118.slots, bf16[1024,6144]{1,0:T(8,128)(2,1)} %bitcast.56, bf16[512,1536]{1,0:T(8,128)(2,1)} %get-tuple-element.78.rest_0_, ...), custom_call_target="tpu_custom_call" | custom-call | flops 6442450944 | bytes 18874368 | tf_op jit(solution)/shard_map/hidden_gradient/pallas_call | solution.py:388
  95.4 2.0 %put_together.3 = (bf16[512,1536]{1,0:T(8,128)(2,1)}, bf16[512,1536]{1,0:T(8,128)(2,1)}) custom-call(s32[1]{0:T(128)} %bitcast.swapped, bf16[2,256,1536]{2,1,0:T(8,128)(2,1)S(1)} %pad_maximum_fusion.rest_0_, bf16[2,256,1536]{2,1,0:T(8,128)(2,1)S(1)} %collective-permute-done.16.rest_1_), custom_call_target="tpu_custom_call" | custom-call | bytes 6291456 | tf_op jit(solution)/shard_map/put_together/pallas_call | solution.py:242
  98.2 11.2 %weight_gradient.2.rest_4_ = bf16[1024,6144]{1,0:T(8,128)(2,1)} custom-call(s32[2]{0:T(128)S(1)} %get-tuple-element.94.quarters, bf16[1024,1024]{1,0:T(8,128)(2,1)S(1)} %copy-done.1, bf16[512,1536]{1,0:T(8,128)(2,1)} %get-tuple-element.78.rest_0_, bf16[512,1536]{1,0:T(8,128)(2,1)} %get-tuple-element.92.rest_1_.rest_0_, ...), custom_call_target="tpu_custom_call" | custom-call | flops 6442450944 | bytes 12582912 | tf_op jit(solution)/shard_map/weight_gradient/pallas_call | solution.py:304
  109.4 1.8 %add.137 = bf16[2,256,1536]{2,1,0:T(8,128)(2,1)S(1)} add(bf16[2,256,1536]{2,1,0:T(8,128)(2,1)S(1)} %get-tuple-element.87, bf16[2,256,1536]{2,1,0:T(8,128)(2,1)} %collective-permute-done.15) | non-fusion elementwise | flops 786432 | bytes 4718592 | tf_op jit(solution)/shard_map/add | solution.py:518
  112.6 1.9 %collective-permute-start.22 = (bf16[256,1536]{1,0:T(8,128)(2,1)}, bf16[256,1536]{1,0:T(8,128)(2,1)}, u32[]{:S(2)}, u32[]{:S(2)}) collective-permute-start(bf16[256,1536]{1,0:T(8,128)(2,1)} %get-tuple-element.97), channel_id=1, source_target_pairs={{0,4},{1,3},{2,6},{3,1},{4,0},{5,7},{6,2},{7,5},{8,12},{9,11},{10,... | collective-permute-start | bytes 2359304 | tf_op jit(solution)/shard_map/sum_1/ppermute | solution.py:23
  115.8 13.4 %hidden_gradient.3 = bf16[1024,1024]{1,0:T(8,128)(2,1)} custom-call(s32[12]{0:T(128)S(1)} %concatenate.25.table, f32[4,128]{1,0:T(4,128)S(1)} %get-tuple-element.119.gates, s32[4,128]{1,0:T(4,128)S(1)} %get-tuple-element.117.slots, bf16[1024,6144]{1,0:T(8,128)(2,1)} %bitcast.57, bf16[512,1536]{1,0:T(8,128)(2,1)} %get-tuple-element.92.rest_1_.rest_0_, ...), custom_call_target="tpu_custom_call" | custom-call | flops 6442450944 | bytes 18874368 | tf_op jit(solution)/shard_map/hidden_gradient/pallas_call | solution.py:388
  129.2 4.9 %collective-permute-done.14 = bf16[2,256,1536]{2,1,0:T(8,128)(2,1)} collective-permute-done((bf16[2,256,1536]{2,1,0:T(8,128)(2,1)S(1)}, bf16[2,256,1536]{2,1,0:T(8,128)(2,1)}, u32[]{:S(2)}, u32[]{:S(2)}) %collective-permute-start.14) | collective-permute-done | bytes 1572896 | tf_op jit(solution)/shard_map/sum_0/ppermute | solution.py:23
  134.2 1.8 %add.138 = bf16[2,256,1536]{2,1,0:T(8,128)(2,1)S(1)} add(bf16[2,256,1536]{2,1,0:T(8,128)(2,1)S(1)} %get-tuple-element.83, bf16[2,256,1536]{2,1,0:T(8,128)(2,1)} %collective-permute-done.14) | non-fusion elementwise | flops 786432 | bytes 4718592 | tf_op jit(solution)/shard_map/add | solution.py:518
  136.1 2.1 %collective-permute-start.21 = (bf16[256,1536]{1,0:T(8,128)(2,1)S(1)}, bf16[256,1536]{1,0:T(8,128)(2,1)S(1)}, u32[]{:S(2)}, u32[]{:S(2)}) collective-permute-start(bf16[256,1536]{1,0:T(8,128)(2,1)S(1)} %get-tuple-element.101), channel_id=1, source_target_pairs={{0,4},{1,3},{2,6},{3,1},{4,0},{5,7},{6,2},{7,5},{8,12},{9,11},{10,... | collective-permute-start | bytes 2359304 | tf_op jit(solution)/shard_map/sum_0/ppermute | solution.py:23
  139.6 3.8 %collective-permute-start.24 = (bf16[128,1536]{1,0:T(8,128)(2,1)S(1)}, bf16[128,1536]{1,0:T(8,128)(2,1)S(1)}, u32[]{:S(2)}, u32[]{:S(2)}) collective-permute-start(bf16[128,1536]{1,0:T(8,128)(2,1)S(1)} %get-tuple-element.114), channel_id=1, source_target_pairs={{0,24},{1,25},{2,26},{3,27},{4,28},{5,29},{6,30},{7,31},{8,0},{9,1... | collective-permute-start | bytes 1179656 | tf_op jit(solution)/shard_map/sum_2_z/ppermute | solution.py:23
  143.5 10.9 %weight_gradient.3 = bf16[1024,6144]{1,0:T(8,128)(2,1)} custom-call(s32[2]{0:T(128)S(1)} %get-tuple-element.104.quarters, bf16[1024,1024]{1,0:T(8,128)(2,1)S(1)} %copy-done.2, bf16[512,1536]{1,0:T(8,128)(2,1)S(1)} %copy-done.4, bf16[512,1536]{1,0:T(8,128)(2,1)} %collective-permute-done.19.rest_2_.rest_1_, ...), custom_call_target="tpu_custom_call", output_to_operand_aliasing={{}: (6, {})} | custom-call | flops 6442450944 | bytes 12582912 | tf_op jit(solution)/shard_map/weight_gradient/pallas_call | solution.py:304
  154.3 3.7 %collective-permute-done.24 = bf16[128,1536]{1,0:T(8,128)(2,1)S(1)} collective-permute-done((bf16[128,1536]{1,0:T(8,128)(2,1)S(1)}, bf16[128,1536]{1,0:T(8,128)(2,1)S(1)}, u32[]{:S(2)}, u32[]{:S(2)}) %collective-permute-start.24) | collective-permute-done | bytes 393248 | tf_op jit(solution)/shard_map/sum_2_z/ppermute | solution.py:23
  158.3 2.1 %collective-permute-start.25 = (bf16[128,1536]{1,0:T(8,128)(2,1)S(1)}, bf16[128,1536]{1,0:T(8,128)(2,1)S(1)}, u32[]{:S(2)}, u32[]{:S(2)}) collective-permute-start(bf16[128,1536]{1,0:T(8,128)(2,1)S(1)} %slice_add_fusion), channel_id=1, source_target_pairs={{0,24},{1,25},{2,26},{3,27},{4,28},{5,29},{6,30},{7,31},{8,0},{9,1... | collective-permute-start | bytes 1179656 | tf_op jit(solution)/shard_map/sum_1_z/ppermute | solution.py:23
  160.4 7.2 %collective-permute-done.25 = bf16[128,1536]{1,0:T(8,128)(2,1)S(1)} collective-permute-done((bf16[128,1536]{1,0:T(8,128)(2,1)S(1)}, bf16[128,1536]{1,0:T(8,128)(2,1)S(1)}, u32[]{:S(2)}, u32[]{:S(2)}) %collective-permute-start.25) | collective-permute-done | bytes 393248 | tf_op jit(solution)/shard_map/sum_1_z/ppermute | solution.py:23
  (91 shorter events, 19.7 us)
Async XLA Ops:
  0.6 6.0 %collective-permute-start.6 = (bf16[1024,1024]{1,0:T(8,128)(2,1)}, bf16[1024,1024]{1,0:T(8,128)(2,1)S(1)}, u32[]{:S(2)}, u32[]{:S(2)}) collective-permute-start(bf16[1024,1024]{1,0:T(8,128)(2,1)} %bitcast.50), channel_id=1, source_target_pairs={{0,1},{1,0},{2,3},{3,2},{4,5},{5,4},{6,7},{7,6},{8,9},{9,8},{10,11... | collective-permute-start | bytes 6291464 | tf_op jit(solution)/shard_map/hidden_core/ppermute | solution.py:23
  2.5 4.1 %collective-permute-start = (f32[4,128]{1,0:T(4,128)S(1)}, f32[4,128]{1,0:T(4,128)S(1)}, u32[]{:S(2)}, u32[]{:S(2)}) collective-permute-start(f32[4,128]{1,0:T(4,128)S(1)} %get-tuple-element.122), channel_id=1, source_target_pairs={{0,4},{1,5},{2,6},{3,7},{4,0},{5,1},{6,2},{7,3},{8,12},{9,13},{10,... | collective-permute-start | bytes 6152 | tf_op jit(solution)/shard_map/routes_y/ppermute | solution.py:23
  6.6 38.4 %collective-permute-start.10 = (bf16[1024,6144]{1,0:T(8,128)(2,1)}, bf16[1024,6144]{1,0:T(8,128)(2,1)}, u32[]{:S(2)}, u32[]{:S(2)}) collective-permute-start(bf16[1024,6144]{1,0:T(8,128)(2,1)} %bitcast.52), channel_id=1, source_target_pairs={{0,1},{1,0},{2,3},{3,2},{4,5},{5,4},{6,7},{7,6},{8,9},{9,8},{10,11... | collective-permute-start | bytes 37748744 | tf_op jit(solution)/shard_map/weight_core/ppermute | solution.py:23
  6.7 11.6 %collective-permute-start.2 = (bf16[128,1536]{1,0:T(8,128)(2,1)}, bf16[128,1536]{1,0:T(8,128)(2,1)S(1)}, u32[]{:S(2)}, u32[]{:S(2)}) collective-permute-start(bf16[128,1536]{1,0:T(8,128)(2,1)} %param.7), channel_id=1, source_target_pairs={{0,4},{1,3},{2,6},{3,1},{4,0},{5,7},{6,2},{7,5},{8,12},{9,11},{10,... | collective-permute-start | bytes 1179656 | tf_op jit(solution)/shard_map/own_first/ppermute | solution.py:23
  9.5 5.4 %collective-permute-start.3 = (f32[2,4,128]{2,1,0:T(4,128)S(1)}, f32[2,4,128]{2,1,0:T(4,128)S(1)}, u32[]{:S(2)}, u32[]{:S(2)}) collective-permute-start(f32[2,4,128]{2,1,0:T(4,128)S(1)} %pad_maximum_fusion.4), channel_id=1, source_target_pairs={{0,8},{1,9},{2,10},{3,11},{4,12},{5,13},{6,14},{7,15},{8,16},{9,17... | collective-permute-start | bytes 12296 | tf_op jit(solution)/shard_map/routes_z/ppermute | solution.py:23
  11.2 6.8 %collective-permute-start.5 = (f32[2,4,128]{2,1,0:T(4,128)S(1)}, f32[2,4,128]{2,1,0:T(4,128)S(1)}, u32[]{:S(2)}, u32[]{:S(2)}) collective-permute-start(f32[2,4,128]{2,1,0:T(4,128)S(1)} %pad_maximum_fusion.4), channel_id=1, source_target_pairs={{0,24},{1,25},{2,26},{3,27},{4,28},{5,29},{6,30},{7,31},{8,0},{9,1... | collective-permute-start | bytes 12296 | tf_op jit(solution)/shard_map/routes_z/ppermute | solution.py:23
  13.5 4.5 %collective-permute-start.4 = (f32[2,4,128]{2,1,0:T(4,128)S(1)}, f32[2,4,128]{2,1,0:T(4,128)S(1)}, u32[]{:S(2)}, u32[]{:S(2)}) collective-permute-start(f32[2,4,128]{2,1,0:T(4,128)S(1)} %pad_maximum_fusion.4), channel_id=1, source_target_pairs={{0,16},{1,17},{2,18},{3,19},{4,20},{5,21},{6,22},{7,23},{8,24},{9,... | collective-permute-start | bytes 12296 | tf_op jit(solution)/shard_map/routes_z/ppermute | solution.py:23
  15.0 14.8 %collective-permute-start.1 = (bf16[128,1536]{1,0:T(8,128)(2,1)}, bf16[128,1536]{1,0:T(8,128)(2,1)}, u32[]{:S(2)}, u32[]{:S(2)}) collective-permute-start(bf16[128,1536]{1,0:T(8,128)(2,1)} %param.7), channel_id=1, source_target_pairs={{0,8},{1,9},{2,10},{3,11},{4,12},{5,13},{6,14},{7,15},{8,16},{9,17... | collective-permute-start | bytes 1179656 | tf_op jit(solution)/shard_map/plane_1/ppermute | solution.py:23
  29.7 12.2 %collective-permute-start.9 = (bf16[128,1536]{1,0:T(8,128)(2,1)}, bf16[128,1536]{1,0:T(8,128)(2,1)S(1)}, u32[]{:S(2)}, u32[]{:S(2)}) collective-permute-start(bf16[128,1536]{1,0:T(8,128)(2,1)} %collective-permute-done.1), channel_id=1, source_target_pairs={{0,4},{1,3},{2,6},{3,1},{4,0},{5,7},{6,2},{7,5},{8,12},{9,11},{10,... | collective-permute-start | bytes 1179656 | tf_op jit(solution)/shard_map/plane_1_first/ppermute | solution.py:23
  31.4 36.3 %collective-permute-start.12 = (bf16[2,128,1536]{2,1,0:T(8,128)(2,1)}, bf16[2,128,1536]{2,1,0:T(8,128)(2,1)S(1)}, u32[]{:S(2)}, u32[]{:S(2)}) collective-permute-start(bf16[2,128,1536]{2,1,0:T(8,128)(2,1)} %pad_maximum_fusion.1.rest_0_), channel_id=1, source_target_pairs={{0,2},{1,5},{2,0},{3,7},{4,6},{5,1},{6,4},{7,3},{8,10},{9,13},{10,... | collective-permute-start | bytes 2359304 | tf_op jit(solution)/shard_map/own_second/ppermute | solution.py:23
  33.0 25.5 %collective-permute-start.7 = (bf16[128,1536]{1,0:T(8,128)(2,1)}, bf16[128,1536]{1,0:T(8,128)(2,1)S(1)}, u32[]{:S(2)}, u32[]{:S(2)}) collective-permute-start(bf16[128,1536]{1,0:T(8,128)(2,1)} %collective-permute-done.1), channel_id=1, source_target_pairs={{0,8},{1,9},{2,10},{3,11},{4,12},{5,13},{6,14},{7,15},{8,16},{9,17... | collective-permute-start | bytes 1179656 | tf_op jit(solution)/shard_map/plane_2/ppermute | solution.py:23
  33.0 25.5 %collective-permute-start.8 = (bf16[128,1536]{1,0:T(8,128)(2,1)}, bf16[128,1536]{1,0:T(8,128)(2,1)S(1)}, u32[]{:S(2)}, u32[]{:S(2)}) collective-permute-start(bf16[128,1536]{1,0:T(8,128)(2,1)} %param.7), channel_id=1, source_target_pairs={{0,24},{1,25},{2,26},{3,27},{4,28},{5,29},{6,30},{7,31},{8,0},{9,1... | collective-permute-start | bytes 1179656 | tf_op jit(solution)/shard_map/plane_3/ppermute | solution.py:23
  43.0 24.8 %collective-permute-start.13 = (bf16[2,128,1536]{2,1,0:T(8,128)(2,1)S(1)}, bf16[2,128,1536]{2,1,0:T(8,128)(2,1)S(1)}, u32[]{:S(2)}, u32[]{:S(2)}) collective-permute-start(bf16[2,128,1536]{2,1,0:T(8,128)(2,1)S(1)} %pad_maximum_fusion.2.rest_2_), channel_id=1, source_target_pairs={{0,2},{1,5},{2,0},{3,7},{4,6},{5,1},{6,4},{7,3},{8,10},{9,13},{10,... | collective-permute-start | bytes 2359304 | tf_op jit(solution)/shard_map/plane_1_second/ppermute | solution.py:23
  58.6 12.7 %collective-permute-start.11 = (bf16[2,128,1536]{2,1,0:T(8,128)(2,1)S(1)}, bf16[2,128,1536]{2,1,0:T(8,128)(2,1)S(1)}, u32[]{:S(2)}, u32[]{:S(2)}) collective-permute-start(bf16[2,128,1536]{2,1,0:T(8,128)(2,1)S(1)} %pad_maximum_fusion.3), channel_id=1, source_target_pairs={{0,4},{1,3},{2,6},{3,1},{4,0},{5,7},{6,2},{7,5},{8,12},{9,11},{10,... | collective-permute-start | bytes 2359304 | tf_op jit(solution)/shard_map/pair_first/ppermute | solution.py:23
  70.7 11.3 %collective-permute-start.17 = (bf16[512,1536]{1,0:T(8,128)(2,1)}, bf16[512,1536]{1,0:T(8,128)(2,1)S(1)}, u32[]{:S(2)}, u32[]{:S(2)}) collective-permute-start(bf16[512,1536]{1,0:T(8,128)(2,1)} %get-tuple-element.78.rest_0_), channel_id=1, source_target_pairs={{0,1},{1,0},{2,3},{3,2},{4,5},{5,4},{6,7},{7,6},{8,9},{9,8},{10,11... | collective-permute-start | bytes 4718600 | tf_op jit(solution)/shard_map/gradients_core/ppermute | solution.py:23
  70.8 11.2 %collective-permute-start.18 = (bf16[512,1536]{1,0:T(8,128)(2,1)}, bf16[512,1536]{1,0:T(8,128)(2,1)S(1)}, u32[]{:S(2)}, u32[]{:S(2)}) collective-permute-start(bf16[512,1536]{1,0:T(8,128)(2,1)} %get-tuple-element.79.rest_1_.rest_2_), channel_id=1, source_target_pairs={{0,1},{1,0},{2,3},{3,2},{4,5},{5,4},{6,7},{7,6},{8,9},{9,8},{10,11... | collective-permute-start | bytes 4718600 | tf_op jit(solution)/shard_map/gradients_core/ppermute | solution.py:23
  71.4 24.0 %collective-permute-start.16 = (bf16[2,256,1536]{2,1,0:T(8,128)(2,1)S(1)}, bf16[2,256,1536]{2,1,0:T(8,128)(2,1)S(1)}, u32[]{:S(2)}, u32[]{:S(2)}) collective-permute-start(bf16[2,256,1536]{2,1,0:T(8,128)(2,1)S(1)} %pad_maximum_fusion.rest_0_), channel_id=1, source_target_pairs={{0,2},{1,5},{2,0},{3,7},{4,6},{5,1},{6,4},{7,3},{8,10},{9,13},{10,... | collective-permute-start | bytes 4718600 | tf_op jit(solution)/shard_map/pair_second/ppermute | solution.py:23
  80.1 29.3 %collective-permute-start.15 = (bf16[2,256,1536]{2,1,0:T(8,128)(2,1)S(1)}, bf16[2,256,1536]{2,1,0:T(8,128)(2,1)}, u32[]{:S(2)}, u32[]{:S(2)}) collective-permute-start(bf16[2,256,1536]{2,1,0:T(8,128)(2,1)S(1)} %get-tuple-element.88), channel_id=1, source_target_pairs={{0,2},{1,5},{2,0},{3,7},{4,6},{5,1},{6,4},{7,3},{8,10},{9,13},{10,... | collective-permute-start | bytes 4718600 | tf_op jit(solution)/shard_map/sum_1/ppermute | solution.py:23
  82.0 11.2 %copy-start.5 = (bf16[512,1536]{1,0:T(8,128)(2,1)}, bf16[512,1536]{1,0:T(8,128)(2,1)S(1)}, u32[]{:S(2)}) copy-start(bf16[512,1536]{1,0:T(8,128)(2,1)S(1)} %collective-permute-done.18.rest_3_.rest_2_) | copy-start | bytes 4718596
  95.4 2.8 %copy-start.1 = (bf16[1024,1024]{1,0:T(8,128)(2,1)S(1)}, bf16[1024,1024]{1,0:T(8,128)(2,1)}, u32[]{:S(2)}) copy-start(bf16[1024,1024]{1,0:T(8,128)(2,1)} %copy-done) | copy-start | bytes 6291460
  97.4 17.2 %collective-permute-start.19 = (bf16[512,1536]{1,0:T(8,128)(2,1)}, bf16[512,1536]{1,0:T(8,128)(2,1)}, u32[]{:S(2)}, u32[]{:S(2)}) collective-permute-start(bf16[512,1536]{1,0:T(8,128)(2,1)} %get-tuple-element.92.rest_1_.rest_0_), channel_id=1, source_target_pairs={{0,1},{1,0},{2,3},{3,2},{4,5},{5,4},{6,7},{7,6},{8,9},{9,8},{10,11... | collective-permute-start | bytes 4718600 | tf_op jit(solution)/shard_map/gradients_core/ppermute | solution.py:23
  97.5 17.1 %collective-permute-start.20 = (bf16[512,1536]{1,0:T(8,128)(2,1)}, bf16[512,1536]{1,0:T(8,128)(2,1)}, u32[]{:S(2)}, u32[]{:S(2)}) collective-permute-start(bf16[512,1536]{1,0:T(8,128)(2,1)} %get-tuple-element.93.rest_3_.rest_1_), channel_id=1, source_target_pairs={{0,1},{1,0},{2,3},{3,2},{4,5},{5,4},{6,7},{7,6},{8,9},{9,8},{10,11... | collective-permute-start | bytes 4718600 | tf_op jit(solution)/shard_map/gradients_core/ppermute | solution.py:23
  98.0 36.2 %collective-permute-start.14 = (bf16[2,256,1536]{2,1,0:T(8,128)(2,1)S(1)}, bf16[2,256,1536]{2,1,0:T(8,128)(2,1)}, u32[]{:S(2)}, u32[]{:S(2)}) collective-permute-start(bf16[2,256,1536]{2,1,0:T(8,128)(2,1)S(1)} %get-tuple-element.84), channel_id=1, source_target_pairs={{0,2},{1,5},{2,0},{3,7},{4,6},{5,1},{6,4},{7,3},{8,10},{9,13},{10,... | collective-permute-start | bytes 4718600 | tf_op jit(solution)/shard_map/sum_0/ppermute | solution.py:23
  112.6 25.6 %collective-permute-start.22 = (bf16[256,1536]{1,0:T(8,128)(2,1)}, bf16[256,1536]{1,0:T(8,128)(2,1)}, u32[]{:S(2)}, u32[]{:S(2)}) collective-permute-start(bf16[256,1536]{1,0:T(8,128)(2,1)} %get-tuple-element.97), channel_id=1, source_target_pairs={{0,4},{1,3},{2,6},{3,1},{4,0},{5,7},{6,2},{7,5},{8,12},{9,11},{10,... | collective-permute-start | bytes 2359304 | tf_op jit(solution)/shard_map/sum_1/ppermute | solution.py:23
  136.0 2.2 %copy-start.10 = (bf16[256,1536]{1,0:T(8,128)(2,1)S(1)}, bf16[256,1536]{1,0:T(8,128)(2,1)}, u32[]{:S(2)}) copy-start(bf16[256,1536]{1,0:T(8,128)(2,1)} %get-tuple-element.102) | copy-start | bytes 2359300
  136.0 7.5 %copy-start.6 = (bf16[512,1536]{1,0:T(8,128)(2,1)S(1)}, bf16[512,1536]{1,0:T(8,128)(2,1)}, u32[]{:S(2)}) copy-start(bf16[512,1536]{1,0:T(8,128)(2,1)} %copy-done.5) | copy-start | bytes 4718596
  136.1 7.4 %copy-start.2 = (bf16[1024,1024]{1,0:T(8,128)(2,1)S(1)}, bf16[1024,1024]{1,0:T(8,128)(2,1)}, u32[]{:S(2)}) copy-start(bf16[1024,1024]{1,0:T(8,128)(2,1)} %copy-done) | copy-start | bytes 6291460
  136.1 7.4 %copy-start.4 = (bf16[512,1536]{1,0:T(8,128)(2,1)S(1)}, bf16[512,1536]{1,0:T(8,128)(2,1)}, u32[]{:S(2)}) copy-start(bf16[512,1536]{1,0:T(8,128)(2,1)} %copy-done.3) | copy-start | bytes 4718596
  136.1 22.0 %collective-permute-start.21 = (bf16[256,1536]{1,0:T(8,128)(2,1)S(1)}, bf16[256,1536]{1,0:T(8,128)(2,1)S(1)}, u32[]{:S(2)}, u32[]{:S(2)}) collective-permute-start(bf16[256,1536]{1,0:T(8,128)(2,1)S(1)} %get-tuple-element.101), channel_id=1, source_target_pairs={{0,4},{1,3},{2,6},{3,1},{4,0},{5,7},{6,2},{7,5},{8,12},{9,11},{10,... | collective-permute-start | bytes 2359304 | tf_op jit(solution)/shard_map/sum_0/ppermute | solution.py:23
  139.6 20.8 %collective-permute-start.23 = (bf16[128,1536]{1,0:T(8,128)(2,1)S(1)}, bf16[128,1536]{1,0:T(8,128)(2,1)S(1)}, u32[]{:S(2)}, u32[]{:S(2)}) collective-permute-start(bf16[128,1536]{1,0:T(8,128)(2,1)S(1)} %get-tuple-element.113), channel_id=1, source_target_pairs={{0,8},{1,9},{2,10},{3,11},{4,12},{5,13},{6,14},{7,15},{8,16},{9,17... | collective-permute-start | bytes 1179656 | tf_op jit(solution)/shard_map/sum_3_z/ppermute | solution.py:23
  139.6 18.4 %collective-permute-start.24 = (bf16[128,1536]{1,0:T(8,128)(2,1)S(1)}, bf16[128,1536]{1,0:T(8,128)(2,1)S(1)}, u32[]{:S(2)}, u32[]{:S(2)}) collective-permute-start(bf16[128,1536]{1,0:T(8,128)(2,1)S(1)} %get-tuple-element.114), channel_id=1, source_target_pairs={{0,24},{1,25},{2,26},{3,27},{4,28},{5,29},{6,30},{7,31},{8,0},{9,1... | collective-permute-start | bytes 1179656 | tf_op jit(solution)/shard_map/sum_2_z/ppermute | solution.py:23
  158.3 9.3 %collective-permute-start.25 = (bf16[128,1536]{1,0:T(8,128)(2,1)S(1)}, bf16[128,1536]{1,0:T(8,128)(2,1)S(1)}, u32[]{:S(2)}, u32[]{:S(2)}) collective-permute-start(bf16[128,1536]{1,0:T(8,128)(2,1)S(1)} %slice_add_fusion), channel_id=1, source_target_pairs={{0,24},{1,25},{2,26},{3,27},{4,28},{5,29},{6,30},{7,31},{8,0},{9,1... | collective-permute-start | bytes 1179656 | tf_op jit(solution)/shard_map/sum_1_z/ppermute | solution.py:23
  (5 other events, 6.3 us)

commit v4 on v3

--- a/solution.py
+++ b/solution.py
@@ -349,16 +349,16 @@
             picked = jnp.dot(chosen, back, preferred_element_type=F32).astype(BF16)
             if last:
                 before = rest[sources]
-                place = table[steps + count + i] * capacity
+                place = table[steps // each + count + i] * capacity
                 out[pl.ds(pl.multiple_of(place, capacity), capacity), :] = picked
-                place = table[steps + i] * capacity
+                place = table[steps // each + i] * capacity
                 old = before[pl.ds(i * capacity, capacity), :]
                 out[pl.ds(pl.multiple_of(place, capacity), capacity), :] = old
             else:
                 out[pl.ds(i * capacity, capacity), :] = picked
 
 
-def hidden_gradient(gates, slots, grads, weight, quarters, capacity, shards=None, before=None):
+def hidden_gradient(gates, slots, grads, weight, table, capacity, before=None):
     tokens, width = grads[0].shape
     depth = weight.shape[0]
     tile = tile_of(width, 1536)
@@ -367,13 +367,10 @@
     last = before is not None
     number = slots.shape[0]
     height = capacity * number * (2 if last else 1)
-    table = jnp.repeat(quarters, per) if per > 1 else quarters
-    if last:
-        table = jnp.concatenate([table, shards])
     specs = [
         pl.BlockSpec(gates.shape, lambda s, t: (0, 0)),
         pl.BlockSpec(slots.shape, lambda s, t: (0, 0)),
-        pl.BlockSpec((depth, tile), lambda s, t: (0, t[s] * per + s % per)),
+        pl.BlockSpec((depth, tile), lambda s, t: (0, t[s // per] * per + s % per)),
     ]
     for i in range(len(grads)):
 
@@ -438,17 +435,28 @@
         with jax.named_scope(name):
             return at.far_z[k % nz].shift(block)
 
-    packed = jnp.concatenate([routing.astype(F32).T, gates.T])
-    packed = jnp.stack(gathered(at.ring_y, packed, "routes_y"))
+    shards = jnp.stack([(at.z - jz) % nz * ny + (at.y - jy) % ny for jz, jy in order])
+    shards = shards.astype(jnp.int32)
+    forward_tables = [jnp.concatenate([mine[jx : jx + 1], swapped]) for jx in range(nx)]
+    hidden_table = jnp.concatenate([quarters, shards])
     hiddens = both(hidden_rows, "hidden_core")
+    first = [gathered(at.ring_1, grad_out, "own_first")]
+    tables = jnp.concatenate([routing.astype(F32).T, gates.T])[None]
     plane = [grad_out]
-    first = [gathered(at.ring_1, grad_out, "own_first")]
-    tables = [packed] + [shifted(jz, packed, "routes_z") for jz in range(1, nz)]
-    plane.append(shifted(1, tie(grad_out, packed), "plane_1"))
+    while len(tables) < nz:
+        more = shifted(len(tables), tables[: nz - len(tables)], "routes_z")
+        tables = jnp.concatenate([tables, more])
+        if len(plane) == 1:
+            tables = tie(tables, first[0], forward_tables, hidden_table, mine, theirs)
+            plane.append(shifted(1, tie(grad_out, tables), "plane_1"))
+            weights = both(tie(weight, tables, hiddens), "weight_core")
     first[0] = jnp.stack(first[0])
-    weights = both(tie(weight, packed, hiddens), "weight_core")
     second = [gathered(at.ring_2, first[0], "own_second")]
-    packed = jnp.stack([tables[jz][jy] for jz, jy in order])
+    tables = tie(gathered(at.ring_y, tables, "routes_y"), plane[1])
+    plane.append(shifted(1, plane[1], "plane_2"))
+    first.append(gathered(at.ring_1, plane[1], "plane_1_first"))
+    backward_z = shifted(nz - 1, tie(grad_out, plane[1]), "plane_3")
+    packed = jnp.stack([tables[jy][jz] for jz, jy in order])
 
     expert = lax.axis_index("expert")
     ours = [expert, expert - at.core + 1 - at.core] if two else [expert]
@@ -458,33 +466,18 @@
     gate = jnp.where(hits, packed[None, :, top:], 0.0).sum(axis=2)
     earlier = (jnp.arange(rows)[:, None] < jnp.arange(rows)[None, :]).astype(BF16)
     place = jnp.dot(hit.astype(BF16), earlier, preferred_element_type=F32).astype(jnp.int32)
-    shards = jnp.stack([(at.z - jz) % nz * ny + (at.y - jy) % ny for jz, jy in order])
-    shards = shards.astype(jnp.int32)
     slot_of = jnp.where(hit > 0, place, -1)
-    rows_in, turned = token_rows(slot_of, gate, hiddens, shards)
+    rows_in, turned = token_rows(slot_of, gate, hiddens, tie(shards, first[0]))
     slot_of, gate = slot_of[0], gate[0]
-    plane[1], first[0] = tie((plane[1], first[0]), rows_in)
-    plane.append(shifted(1, plane[1], "plane_2"))
-    plane.append(shifted(nz - 1, tie(grad_out, plane[1]), "plane_3"))
-    first.append(gathered(at.ring_1, plane[1], "plane_1_first"))
-
-    calls = [(jx, 0, 1) for jx in range(nx - 1)] + [(nx - 1, 0, 2), (nx - 1, 1, 2)]
-    forward_tables = [jnp.concatenate([mine[jx : jx + 1], swapped]) for jx in range(nx)]
+
+    calls = [(0, 0, 2), (0, 1, 2)] + [(jx, 0, 1) for jx in range(1, nx)]
 
     def forward(call, placed, *after):
         jx, part, parts = call
         table = tie(forward_tables[jx], *after)
         return forward_placed(rows_in, weights, table, jx, part, parts, places, size, at, placed)
 
-    first[1] = jnp.stack(first[1])
-    second.append(gathered(at.ring_2, first[1], "plane_1_second"))
-    done = None
-    for call in calls[:-2]:
-        done = forward(call, done, plane[1], first[1])
-    pair = jnp.stack(tie(plane[2:], done))
-    first.append(gathered(at.ring_1, pair, "pair_first"))
-
-    def assembled(blocks, turn):
+    def assembled(blocks):
         plan = []
         for i in range(len(blocks) // nx):
             for j2 in range(nx):
@@ -493,12 +486,20 @@
                     plan.append((number, j1, (j1, j2), i * rows, size, blocks[number].shape[1]))
         return list(put_together(plan, blocks, swapped, nx, (half, width)))
 
-    done = forward(calls[-2], done, pair, first[1])
+    first[1] = jnp.stack(tie(first[1], rows_in))
+    second.append(gathered(at.ring_2, first[1], "plane_1_second"))
+    done = forward(calls[0], None, first[1], second[0])
+    plane[2], plane_3 = tie((plane[2], backward_z), done)
+    pair = jnp.stack([plane[2], plane_3])
+    first.append(gathered(at.ring_1, pair, "pair_first"))
+    done = forward(calls[1], done, pair)
     first[2] = jnp.stack(tie(first[2], done)).reshape(ny, size, width)
     second.append(gathered(at.ring_2, first[2], "pair_second"))
-    grads_1 = assembled(tie(second[0] + second[1], done), turns[0])
+    grads_1 = assembled(tie(second[0] + second[1], done))
     others_1 = [both(block, "gradients_core")[-1] for block in grads_1] if two else []
-    placed = forward(calls[-1], done, first[2], grads_1)
+    placed = done
+    for call in calls[2:]:
+        placed = forward(call, placed, first[2], grads_1)
 
     class Sum:
         def __init__(self, turn):
@@ -523,18 +524,28 @@
 
     near, far = Sum(0), Sum(1)
     far.start(at.ring_2)
-    ask = tie(quarters, far.sent)
+    ask = tie(hidden_table, far.sent)
     count = len(order) // 2
     back = hidden_gradient(gate[:count], slot_of[:count], grads_1 + others_1, weight, ask, capacity)
 
-    grads_2 = assembled(tie(second[2], back), turns[1])
+    grads_2 = assembled(tie(second[2], back))
     others_2 = [both(block, "gradients_core")[-1] for block in grads_2] if two else []
     ask = tie(mine, grads_2)
     grad_weight = weight_gradient(turned, list(zip(grads_1, grads_2)), ask, weight.shape, None)
     far.finish(grad_weight)
     far.second()
     near.start(at.ring_2)
-    ask = tie(quarters, far.sent, near.sent)
+    ask = tie(theirs, far.sent, near.sent)
+    if two:
+        grad_weight = weight_gradient(
+            turned, list(zip(others_1, others_2)), ask, weight.shape, grad_weight
+        )
+    far.finish(grad_weight)
+    near.finish(grad_weight)
+    near.second()
+    last = shifted(nz - 3, far.terms[rows:], "sum_3_z")
+    onward = shifted(nz - 1, far.terms[:rows], "sum_2_z")
+    ask = tie(hidden_table, far.terms, near.sent)
     grad_hidden = hidden_gradient(
         gate[count:],
         slot_of[count:],
@@ -542,21 +553,10 @@
         weight,
         ask,
         capacity,
-        shards,
         back,
     )
-    far.finish(grad_hidden)
     near.finish(grad_hidden)
-    near.second()
-    last = shifted(nz - 3, far.terms[rows:], "sum_3_z")
-    onward = shifted(nz - 1, far.terms[:rows], "sum_2_z")
-    ask = tie(theirs, far.terms, near.sent)
-    if two:
-        grad_weight = weight_gradient(
-            turned, list(zip(others_1, others_2)), ask, weight.shape, grad_weight
-        )
-    near.finish(grad_weight)
-    onward = tie(onward, grad_weight) + near.terms[rows:]
+    onward = tie(onward, grad_hidden) + near.terms[rows:]
     onward = shifted(nz - 1, onward, "sum_1_z")
     mixed_out = near.terms[:rows].astype(F32) + last.astype(F32) + onward.astype(F32)
     return (mixed_out.astype(BF16), grad_hidden[None], grad_weight[None])

time: 169 us -> 159 us (0.941)
  other arithmetic: 13 us -> 9.36 us
  local copies, waits for them, and re-layouts: 8.6 us -> 5.56 us
  starting transfers between devices: 32 us -> 30 us
    ppermute x26 -> x25, starting transfers between devices: 32 us -> 30 us  [shift(): return lax.ppermute(block, ALL, self.perm)]
    unnamed x28 -> x23, local copies, waits for them, and re-layouts: 6.33 us -> 4.51 us
    ppermute x26 -> x25, waiting for transfers between devices: 25.3 us -> 24.5 us  [shift(): return lax.ppermute(block, ALL, self.perm)]
  transfers between devices with their start and end apart: 26 -> 25, of which waited for: 7 -> 6; matrix products, arithmetic and copies ran while one was open for 9% -> 6% of each run, Pallas kernels for 53% -> 56%
where the time goes in v4:
time: 159 us; the launch traced here: 158 us
  Pallas kernels  88 us (55%)
  starting transfers between devices  30 us (19%)
  waiting for transfers between devices  24.5 us (15%)
  other arithmetic  9.36 us (6%)
  local copies, waits for them, and re-layouts  5.56 us (3%)
    pallas_call x3, Pallas kernels, forward_placed(): pl.pallas_call(functools.partial(place_kernel, jx, part * per, at.ny, pla...  30.2 us
    ppermute x25, starting transfers between devices, shift(): return lax.ppermute(block, ALL, self.perm)  30 us
    ppermute x25, waiting for transfers between devices, shift(): return lax.ppermute(block, ALL, self.perm)  24.5 us
    pallas_call x2, Pallas kernels, hidden_gradient(): pl.pallas_call(functools.partial(hidden_kernel, steps, per, number, last)...  23.2 us
    pallas_call x2, Pallas kernels, weight_gradient(): pl.pallas_call(kernel, grid_spec=pltpu.PrefetchScalarGridSpec(num_scalar_...  20.7 us
    pallas_call x1, Pallas kernels, token_rows(): pl.pallas_call(functools.partial(rows_kernel, size), grid_spec=pltpu.Pref...  7.59 us
    pallas_call x2, Pallas kernels, put_together(): pl.pallas_call(functools.partial(gather_kernel, plan, count), grid_spec=p...  6.37 us
    unnamed x23, local copies, waits for them, and re-layouts  4.51 us
  transfers between devices with their start and end apart: 25, of which 6 were waited for; matrix products, arithmetic and copies ran while one was open for 6% of the time, Pallas kernels for 56%

profile of v4, /device:TPU:0, one launch (start us, length us, event | category | flops | bytes accessed | tf_op | source)
XLA Modules:
  0.0 158.4 jit_solution(7090295366336153279)
XLA Ops:
  2.5 2.6 %collective-permute-start = (f32[1,4,128]{2,1,0:T(4,128)S(1)}, f32[1,4,128]{2,1,0:T(4,128)S(1)}, u32[]{:S(2)}, u32[]{:S(2)}) collective-permute-start(f32[1,4,128]{2,1,0:T(4,128)S(1)} %maximum_bitcast_fusion), channel_id=1, source_target_pairs={{0,8},{1,9},{2,10},{3,11},{4,12},{5,13},{6,14},{7,15},{8,16},{9,17... | collective-permute-start | bytes 6152 | tf_op jit(solution)/shard_map/routes_z/ppermute | solution.py:23
  5.2 1.5 collective-permute-start.1
  8.8 4.3 %collective-permute-done.1 = bf16[128,1536]{1,0:T(8,128)(2,1)S(1)} collective-permute-done((bf16[128,1536]{1,0:T(8,128)(2,1)}, bf16[128,1536]{1,0:T(8,128)(2,1)S(1)}, u32[]{:S(2)}, u32[]{:S(2)}) %collective-permute-start.1) | collective-permute-done | bytes 393248 | tf_op jit(solution)/shard_map/own_first/ppermute | solution.py:23
  13.3 2.6 %collective-permute-start.6 = (f32[2,4,128]{2,1,0:T(4,128)S(1)}, f32[2,4,128]{2,1,0:T(4,128)S(1)}, u32[]{:S(2)}, u32[]{:S(2)}) collective-permute-start(f32[2,4,128]{2,1,0:T(4,128)S(1)} %pad_maximum_fusion.5), channel_id=1, source_target_pairs={{0,16},{1,17},{2,18},{3,19},{4,20},{5,21},{6,22},{7,23},{8,24},{9,... | collective-permute-start | bytes 12296 | tf_op jit(solution)/shard_map/routes_z/ppermute | solution.py:23
  16.0 1.8 %collective-permute-done.6 = f32[2,4,128]{2,1,0:T(4,128)S(1)} collective-permute-done((f32[2,4,128]{2,1,0:T(4,128)S(1)}, f32[2,4,128]{2,1,0:T(4,128)S(1)}, u32[]{:S(2)}, u32[]{:S(2)}) %collective-permute-start.6) | collective-permute-done | bytes 4128 | tf_op jit(solution)/shard_map/routes_z/ppermute | solution.py:23
  17.8 1.5 collective-permute-start.7
  20.4 1.6 collective-permute-start.9
  22.0 7.2 %collective-permute-done.2 = bf16[128,1536]{1,0:T(8,128)(2,1)S(1)} collective-permute-done((bf16[128,1536]{1,0:T(8,128)(2,1)}, bf16[128,1536]{1,0:T(8,128)(2,1)S(1)}, u32[]{:S(2)}, u32[]{:S(2)}) %collective-permute-start.2) | collective-permute-done | bytes 393248 | tf_op jit(solution)/shard_map/plane_1/ppermute | solution.py:23
  29.3 1.6 %collective-permute-start.5 = (bf16[128,1536]{1,0:T(8,128)(2,1)S(1)}, bf16[128,1536]{1,0:T(8,128)(2,1)S(1)}, u32[]{:S(2)}, u32[]{:S(2)}) collective-permute-start(bf16[128,1536]{1,0:T(8,128)(2,1)S(1)} %collective-permute-done.2), channel_id=1, source_target_pairs={{0,4},{1,3},{2,6},{3,1},{4,0},{5,7},{6,2},{7,5},{8,12},{9,11},{10,... | collective-permute-start | bytes 1179656 | tf_op jit(solution)/shard_map/plane_1_first/ppermute | solution.py:23
  30.9 1.9 %collective-permute-start.3 = (bf16[128,1536]{1,0:T(8,128)(2,1)S(1)}, bf16[128,1536]{1,0:T(8,128)(2,1)S(1)}, u32[]{:S(2)}, u32[]{:S(2)}) collective-permute-start(bf16[128,1536]{1,0:T(8,128)(2,1)S(1)} %collective-permute-done.2), channel_id=1, source_target_pairs={{0,8},{1,9},{2,10},{3,11},{4,12},{5,13},{6,14},{7,15},{8,16},{9,17... | collective-permute-start | bytes 1179656 | tf_op jit(solution)/shard_map/plane_2/ppermute | solution.py:23
  33.0 1.6 %copy-done.4 = bf16[1,1024,1024]{2,1,0:T(8,128)(2,1)S(1)} copy-done((bf16[1,1024,1024]{2,1,0:T(8,128)(2,1)S(1)}, bf16[1,1024,1024]{2,1,0:T(8,128)(2,1)}, u32[]{:S(2)}) %copy-start.4) | copy-done | bytes 2097176
  34.6 7.6 %token_rows.1 = (bf16[2,1024,1024]{2,1,0:T(8,128)(2,1)}, bf16[1024,1024]{1,0:T(8,128)(2,1)S(1)}) custom-call(s32[8]{0:T(128)S(1)} %stack.84.shards, s32[2,8,128]{2,1,0:T(8,128)S(1)} %fusion.slots, f32[2,8,128]{2,1,0:T(8,128)S(1)} %get-tuple-element.117.gates, bf16[1024,1024]{1,0:T(8,128)(2,1)S(1)} %bitcast.48, bf16[1024,1024]{1,0:T(8,128)(2,1)} %collective-permute-done.8.rest_1_), custom_call_target="tpu_custom_call" | custom-call | flops 2147483648 | bytes 8388608 | tf_op jit(solution)/shard_map/token_rows/pallas_call | solution.py:111
  42.3 1.5 collective-permute-start.12
  43.9 8.3 %forward_placed.3 = (bf16[2,256,1536]{2,1,0:T(8,128)(2,1)S(1)}, bf16[2,256,1536]{2,1,0:T(8,128)(2,1)S(1)}, bf16[2,256,1536]{2,1,0:T(8,128)(2,1)S(1)}, bf16[2,256,1536]{2,1,0:T(8,128)(2,1)S(1)}) custom-call(s32[2]{0:T(128)S(1)} %pad_add_fusion.1.table, bf16[2,1024,1024]{2,1,0:T(8,128)(2,1)} %get-tuple-element.66.rows, bf16[1024,6144]{1,0:T(8,128)(2,1)} %bitcast.50, ...), custom_call_target="tpu_custom_call" | custom-call | flops 3221225472 | bytes 6291456 | tf_op jit(solution)/shard_map/forward_placed/pallas_call | solution.py:189
  52.9 8.3 %forward_placed.4 = (bf16[2,256,1536]{2,1,0:T(8,128)(2,1)S(1)}, bf16[2,256,1536]{2,1,0:T(8,128)(2,1)S(1)}, bf16[2,256,1536]{2,1,0:T(8,128)(2,1)S(1)}, bf16[2,256,1536]{2,1,0:T(8,128)(2,1)S(1)}) custom-call(s32[2]{0:T(128)S(1)} %pad_add_fusion.1.table, ...), custom_call_target="tpu_custom_call", output_to_operand_aliasing={{0}: (4, {}), {1}: (5, {}), {2}: (6, {}), {3}: (7, {})} | custom-call | flops 3221225472 | bytes 6291456 | tf_op jit(solution)/shard_map/forward_placed/pallas_call | solution.py:189
  61.2 3.4 %put_together.2 = (bf16[512,1536]{1,0:T(8,128)(2,1)S(1)}, bf16[512,1536]{1,0:T(8,128)(2,1)}) custom-call(s32[1]{0:T(128)} %bitcast.swapped, bf16[2,128,1536]{2,1,0:T(8,128)(2,1)S(1)} %pad_maximum_fusion.1.rest_0_, bf16[2,128,1536]{2,1,0:T(8,128)(2,1)S(1)} %collective-permute-done.9.rest_1_, bf16[2,128,1536]{2,1,0:T(8,128)(2,1)S(1)} %pad_maximum_fusion.2.rest_2_, ...), custom_call_target="tpu_custom_call" | custom-call | bytes 6291456 | tf_op jit(solution)/shard_map/put_together/pallas_call | solution.py:242
  66.3 13.6 %forward_placed.5 = (bf16[2,256,1536]{2,1,0:T(8,128)(2,1)S(1)}, bf16[2,256,1536]{2,1,0:T(8,128)(2,1)S(1)}, bf16[2,256,1536]{2,1,0:T(8,128)(2,1)S(1)}, bf16[2,256,1536]{2,1,0:T(8,128)(2,1)S(1)}) custom-call(s32[2]{0:T(128)S(1)} %pad_add_fusion.table, ...), custom_call_target="tpu_custom_call", output_to_operand_aliasing={{0}: (4, {}), {1}: (5, {}), {2}: (6, {}), {3}: (7, {})} | custom-call | flops 6442450944 | bytes 12582912 | tf_op jit(solution)/shard_map/forward_placed/pallas_call | solution.py:189
  79.8 1.6 collective-permute-start.14
  81.4 10.7 %hidden_gradient.2.rest_4_ = bf16[512,1024]{1,0:T(8,128)(2,1)S(1)} custom-call(s32[12]{0:T(128)S(1)} %concatenate.28.table, f32[4,128]{1,0:T(4,128)S(1)} %get-tuple-element.130.gates, s32[4,128]{1,0:T(4,128)S(1)} %get-tuple-element.128.slots, bf16[1024,6144]{1,0:T(8,128)(2,1)} %bitcast.53, bf16[512,1536]{1,0:T(8,128)(2,1)S(1)} %copy-done.6, ...), custom_call_target="tpu_custom_call" | custom-call | flops 6442450944 | bytes 18874368 | tf_op jit(solution)/shard_map/hidden_gradient/pallas_call | solution.py:385
  93.2 3.0 %put_together.3 = (bf16[512,1536]{1,0:T(8,128)(2,1)}, bf16[512,1536]{1,0:T(8,128)(2,1)}) custom-call(s32[1]{0:T(128)} %bitcast.swapped, bf16[2,256,1536]{2,1,0:T(8,128)(2,1)S(1)} %pad_maximum_fusion.rest_0_, bf16[2,256,1536]{2,1,0:T(8,128)(2,1)} %collective-permute-done.15.rest_1_), custom_call_target="tpu_custom_call" | custom-call | bytes 6291456 | tf_op jit(solution)/shard_map/put_together/pallas_call | solution.py:242
  98.7 10.8 %weight_gradient.2.rest_4_ = bf16[1024,6144]{1,0:T(8,128)(2,1)} custom-call(s32[2]{0:T(128)S(1)} %get-tuple-element.104.quarters, bf16[1024,1024]{1,0:T(8,128)(2,1)S(1)} %get-tuple-element.105.turned, bf16[512,1536]{1,0:T(8,128)(2,1)S(1)} %copy-done.7, bf16[512,1536]{1,0:T(8,128)(2,1)} %get-tuple-element.102.rest_1_.rest_0_, ...), custom_call_target="tpu_custom_call" | custom-call | flops 6442450944 | bytes 12582912 | tf_op jit(solution)/shard_map/weight_gradient/pallas_call | solution.py:304
  109.5 1.8 %add.137 = bf16[2,256,1536]{2,1,0:T(8,128)(2,1)S(1)} add(bf16[2,256,1536]{2,1,0:T(8,128)(2,1)S(1)} %get-tuple-element.97, bf16[2,256,1536]{2,1,0:T(8,128)(2,1)} %collective-permute-done.14) | non-fusion elementwise | flops 786432 | bytes 4718592 | tf_op jit(solution)/shard_map/add | solution.py:519
  111.4 1.6 %collective-permute-start.21 = (bf16[256,1536]{1,0:T(8,128)(2,1)S(1)}, bf16[256,1536]{1,0:T(8,128)(2,1)S(1)}, u32[]{:S(2)}, u32[]{:S(2)}) collective-permute-start(bf16[256,1536]{1,0:T(8,128)(2,1)S(1)} %get-tuple-element.107), channel_id=1, source_target_pairs={{0,4},{1,3},{2,6},{3,1},{4,0},{5,7},{6,2},{7,5},{8,12},{9,11},{10,... | collective-permute-start | bytes 2359304 | tf_op jit(solution)/shard_map/sum_1/ppermute | solution.py:23
  113.1 9.8 %weight_gradient.3 = bf16[1024,6144]{1,0:T(8,128)(2,1)} custom-call(s32[2]{0:T(128)S(1)} %get-tuple-element.108.quarters, bf16[1024,1024]{1,0:T(8,128)(2,1)S(1)} %get-tuple-element.105.turned, bf16[512,1536]{1,0:T(8,128)(2,1)S(1)} %collective-permute-done.16.rest_2_.rest_0_, ...), custom_call_target="tpu_custom_call", output_to_operand_aliasing={{}: (6, {})} | custom-call | flops 6442450944 | bytes 12582912 | tf_op jit(solution)/shard_map/weight_gradient/pallas_call | solution.py:304
  122.9 1.9 %collective-permute-done.13 = bf16[2,256,1536]{2,1,0:T(8,128)(2,1)} collective-permute-done((bf16[2,256,1536]{2,1,0:T(8,128)(2,1)S(1)}, bf16[2,256,1536]{2,1,0:T(8,128)(2,1)}, u32[]{:S(2)}, u32[]{:S(2)}) %collective-permute-start.13) | collective-permute-done | bytes 1572896 | tf_op jit(solution)/shard_map/sum_0/ppermute | solution.py:23
  124.8 1.8 %add.138 = bf16[2,256,1536]{2,1,0:T(8,128)(2,1)S(1)} add(bf16[2,256,1536]{2,1,0:T(8,128)(2,1)S(1)} %get-tuple-element.93, bf16[2,256,1536]{2,1,0:T(8,128)(2,1)} %collective-permute-done.13) | non-fusion elementwise | flops 786432 | bytes 4718592 | tf_op jit(solution)/shard_map/add | solution.py:519
  126.7 2.6 %collective-permute-start.20 = (bf16[256,1536]{1,0:T(8,128)(2,1)S(1)}, bf16[256,1536]{1,0:T(8,128)(2,1)S(1)}, u32[]{:S(2)}, u32[]{:S(2)}) collective-permute-start(bf16[256,1536]{1,0:T(8,128)(2,1)S(1)} %get-tuple-element.111), channel_id=1, source_target_pairs={{0,4},{1,3},{2,6},{3,1},{4,0},{5,7},{6,2},{7,5},{8,12},{9,11},{10,... | collective-permute-start | bytes 2359304 | tf_op jit(solution)/shard_map/sum_0/ppermute | solution.py:23
  129.7 3.8 %collective-permute-start.23 = (bf16[128,1536]{1,0:T(8,128)(2,1)S(1)}, bf16[128,1536]{1,0:T(8,128)(2,1)S(1)}, u32[]{:S(2)}, u32[]{:S(2)}) collective-permute-start(bf16[128,1536]{1,0:T(8,128)(2,1)S(1)} %get-tuple-element.124), channel_id=1, source_target_pairs={{0,24},{1,25},{2,26},{3,27},{4,28},{5,29},{6,30},{7,31},{8,0},{9,1... | collective-permute-start | bytes 1179656 | tf_op jit(solution)/shard_map/sum_2_z/ppermute | solution.py:23
  133.5 12.5 %hidden_gradient.3 = bf16[1024,1024]{1,0:T(8,128)(2,1)} custom-call(s32[12]{0:T(128)S(1)} %concatenate.28.table, f32[4,128]{1,0:T(4,128)S(1)} %get-tuple-element.129.gates, s32[4,128]{1,0:T(4,128)S(1)} %get-tuple-element.127.slots, bf16[1024,6144]{1,0:T(8,128)(2,1)} %bitcast.54, bf16[512,1536]{1,0:T(8,128)(2,1)} %get-tuple-element.102.rest_1_.rest_0_, ...), custom_call_target="tpu_custom_call" | custom-call | flops 6442450944 | bytes 18874368 | tf_op jit(solution)/shard_map/hidden_gradient/pallas_call | solution.py:385
  146.0 2.0 %collective-permute-done.23 = bf16[128,1536]{1,0:T(8,128)(2,1)S(1)} collective-permute-done((bf16[128,1536]{1,0:T(8,128)(2,1)S(1)}, bf16[128,1536]{1,0:T(8,128)(2,1)S(1)}, u32[]{:S(2)}, u32[]{:S(2)}) %collective-permute-start.23) | collective-permute-done | bytes 393248 | tf_op jit(solution)/shard_map/sum_2_z/ppermute | solution.py:23
  148.2 2.1 %collective-permute-start.24 = (bf16[128,1536]{1,0:T(8,128)(2,1)S(1)}, bf16[128,1536]{1,0:T(8,128)(2,1)S(1)}, u32[]{:S(2)}, u32[]{:S(2)}) collective-permute-start(bf16[128,1536]{1,0:T(8,128)(2,1)S(1)} %slice_add_fusion), channel_id=1, source_target_pairs={{0,24},{1,25},{2,26},{3,27},{4,28},{5,29},{6,30},{7,31},{8,0},{9,1... | collective-permute-start | bytes 1179656 | tf_op jit(solution)/shard_map/sum_1_z/ppermute | solution.py:23
  150.3 7.2 %collective-permute-done.24 = bf16[128,1536]{1,0:T(8,128)(2,1)S(1)} collective-permute-done((bf16[128,1536]{1,0:T(8,128)(2,1)S(1)}, bf16[128,1536]{1,0:T(8,128)(2,1)S(1)}, u32[]{:S(2)}, u32[]{:S(2)}) %collective-permute-start.24) | collective-permute-done | bytes 393248 | tf_op jit(solution)/shard_map/sum_1_z/ppermute | solution.py:23
  (85 shorter events, 13.4 us)
Async XLA Ops:
  0.6 28.6 %copy-start.10 = (bf16[128,1536]{1,0:T(8,128)(2,1)S(1)}, bf16[128,1536]{1,0:T(8,128)(2,1)}, u32[]{:S(2)}) copy-start(bf16[128,1536]{1,0:T(8,128)(2,1)} %param.7) | copy-start | bytes 1179652
  0.6 12.5 %collective-permute-start.8 = (bf16[1024,1024]{1,0:T(8,128)(2,1)}, bf16[1024,1024]{1,0:T(8,128)(2,1)}, u32[]{:S(2)}, u32[]{:S(2)}) collective-permute-start(bf16[1024,1024]{1,0:T(8,128)(2,1)} %bitcast.47), channel_id=1, source_target_pairs={{0,1},{1,0},{2,3},{3,2},{4,5},{5,4},{6,7},{7,6},{8,9},{9,8},{10,11... | collective-permute-start | bytes 6291464 | tf_op jit(solution)/shard_map/hidden_core/ppermute | solution.py:23
  2.5 6.3 %collective-permute-start = (f32[1,4,128]{2,1,0:T(4,128)S(1)}, f32[1,4,128]{2,1,0:T(4,128)S(1)}, u32[]{:S(2)}, u32[]{:S(2)}) collective-permute-start(f32[1,4,128]{2,1,0:T(4,128)S(1)} %maximum_bitcast_fusion), channel_id=1, source_target_pairs={{0,8},{1,9},{2,10},{3,11},{4,12},{5,13},{6,14},{7,15},{8,16},{9,17... | collective-permute-start | bytes 6152 | tf_op jit(solution)/shard_map/routes_z/ppermute | solution.py:23
  5.2 8.0 %collective-permute-start.1 = (bf16[128,1536]{1,0:T(8,128)(2,1)}, bf16[128,1536]{1,0:T(8,128)(2,1)S(1)}, u32[]{:S(2)}, u32[]{:S(2)}) collective-permute-start(bf16[128,1536]{1,0:T(8,128)(2,1)} %param.7), channel_id=1, source_target_pairs={{0,4},{1,3},{2,6},{3,1},{4,0},{5,7},{6,2},{7,5},{8,12},{9,11},{10,... | collective-permute-start | bytes 1179656 | tf_op jit(solution)/shard_map/own_first/ppermute | solution.py:23
  13.1 30.7 %collective-permute-start.10 = (bf16[1024,6144]{1,0:T(8,128)(2,1)}, bf16[1024,6144]{1,0:T(8,128)(2,1)}, u32[]{:S(2)}, u32[]{:S(2)}) collective-permute-start(bf16[1024,6144]{1,0:T(8,128)(2,1)} %bitcast.49), channel_id=1, source_target_pairs={{0,1},{1,0},{2,3},{3,2},{4,5},{5,4},{6,7},{7,6},{8,9},{9,8},{10,11... | collective-permute-start | bytes 37748744 | tf_op jit(solution)/shard_map/weight_core/ppermute | solution.py:23
  13.3 4.5 %collective-permute-start.6 = (f32[2,4,128]{2,1,0:T(4,128)S(1)}, f32[2,4,128]{2,1,0:T(4,128)S(1)}, u32[]{:S(2)}, u32[]{:S(2)}) collective-permute-start(f32[2,4,128]{2,1,0:T(4,128)S(1)} %pad_maximum_fusion.5), channel_id=1, source_target_pairs={{0,16},{1,17},{2,18},{3,19},{4,20},{5,21},{6,22},{7,23},{8,24},{9,... | collective-permute-start | bytes 12296 | tf_op jit(solution)/shard_map/routes_z/ppermute | solution.py:23
  15.9 13.3 %collective-permute-start.2 = (bf16[128,1536]{1,0:T(8,128)(2,1)}, bf16[128,1536]{1,0:T(8,128)(2,1)S(1)}, u32[]{:S(2)}, u32[]{:S(2)}) collective-permute-start(bf16[128,1536]{1,0:T(8,128)(2,1)} %param.7), channel_id=1, source_target_pairs={{0,8},{1,9},{2,10},{3,11},{4,12},{5,13},{6,14},{7,15},{8,16},{9,17... | collective-permute-start | bytes 1179656 | tf_op jit(solution)/shard_map/plane_1/ppermute | solution.py:23
  17.8 4.2 %collective-permute-start.7 = (f32[4,4,128]{2,1,0:T(4,128)S(1)}, f32[4,4,128]{2,1,0:T(4,128)S(1)}, u32[]{:S(2)}, u32[]{:S(2)}) collective-permute-start(f32[4,4,128]{2,1,0:T(4,128)S(1)} %constant_dynamic-update-slice_fusion), channel_id=1, source_target_pairs={{0,4},{1,5},{2,6},{3,7},{4,0},{5,1},{6,2},{7,3},{8,12},{9,13},{10,... | collective-permute-start | bytes 24584 | tf_op jit(solution)/shard_map/routes_y/ppermute | solution.py:23
  20.4 23.4 %collective-permute-start.9 = (bf16[2,128,1536]{2,1,0:T(8,128)(2,1)S(1)}, bf16[2,128,1536]{2,1,0:T(8,128)(2,1)S(1)}, u32[]{:S(2)}, u32[]{:S(2)}) collective-permute-start(bf16[2,128,1536]{2,1,0:T(8,128)(2,1)S(1)} %pad_maximum_fusion.1.rest_0_), channel_id=1, source_target_pairs={{0,2},{1,5},{2,0},{3,7},{4,6},{5,1},{6,4},{7,3},{8,10},{9,13},{10,... | collective-permute-start | bytes 2359304 | tf_op jit(solution)/shard_map/own_second/ppermute | solution.py:23
  29.2 23.0 %collective-permute-start.4 = (bf16[128,1536]{1,0:T(8,128)(2,1)S(1)}, bf16[128,1536]{1,0:T(8,128)(2,1)S(1)}, u32[]{:S(2)}, u32[]{:S(2)}) collective-permute-start(bf16[128,1536]{1,0:T(8,128)(2,1)S(1)} %copy-done.10), channel_id=1, source_target_pairs={{0,24},{1,25},{2,26},{3,27},{4,28},{5,29},{6,30},{7,31},{8,0},{9,1... | collective-permute-start | bytes 1179656 | tf_op jit(solution)/shard_map/plane_3/ppermute | solution.py:23
  29.3 12.9 %collective-permute-start.5 = (bf16[128,1536]{1,0:T(8,128)(2,1)S(1)}, bf16[128,1536]{1,0:T(8,128)(2,1)S(1)}, u32[]{:S(2)}, u32[]{:S(2)}) collective-permute-start(bf16[128,1536]{1,0:T(8,128)(2,1)S(1)} %collective-permute-done.2), channel_id=1, source_target_pairs={{0,4},{1,3},{2,6},{3,1},{4,0},{5,7},{6,2},{7,5},{8,12},{9,11},{10,... | collective-permute-start | bytes 1179656 | tf_op jit(solution)/shard_map/plane_1_first/ppermute | solution.py:23
  30.9 21.3 %collective-permute-start.3 = (bf16[128,1536]{1,0:T(8,128)(2,1)S(1)}, bf16[128,1536]{1,0:T(8,128)(2,1)S(1)}, u32[]{:S(2)}, u32[]{:S(2)}) collective-permute-start(bf16[128,1536]{1,0:T(8,128)(2,1)S(1)} %collective-permute-done.2), channel_id=1, source_target_pairs={{0,8},{1,9},{2,10},{3,11},{4,12},{5,13},{6,14},{7,15},{8,16},{9,17... | collective-permute-start | bytes 1179656 | tf_op jit(solution)/shard_map/plane_2/ppermute | solution.py:23
  42.3 18.9 %collective-permute-start.12 = (bf16[2,128,1536]{2,1,0:T(8,128)(2,1)S(1)}, bf16[2,128,1536]{2,1,0:T(8,128)(2,1)S(1)}, u32[]{:S(2)}, u32[]{:S(2)}) collective-permute-start(bf16[2,128,1536]{2,1,0:T(8,128)(2,1)S(1)} %pad_maximum_fusion.2.rest_2_), channel_id=1, source_target_pairs={{0,2},{1,5},{2,0},{3,7},{4,6},{5,1},{6,4},{7,3},{8,10},{9,13},{10,... | collective-permute-start | bytes 2359304 | tf_op jit(solution)/shard_map/plane_1_second/ppermute | solution.py:23
  52.3 12.9 %collective-permute-start.11 = (bf16[2,128,1536]{2,1,0:T(8,128)(2,1)S(1)}, bf16[2,128,1536]{2,1,0:T(8,128)(2,1)S(1)}, u32[]{:S(2)}, u32[]{:S(2)}) collective-permute-start(bf16[2,128,1536]{2,1,0:T(8,128)(2,1)S(1)} %pad_maximum_fusion.3), channel_id=1, source_target_pairs={{0,4},{1,3},{2,6},{3,1},{4,0},{5,7},{6,2},{7,5},{8,12},{9,11},{10,... | collective-permute-start | bytes 2359304 | tf_op jit(solution)/shard_map/pair_first/ppermute | solution.py:23
  64.6 16.8 %collective-permute-start.16 = (bf16[512,1536]{1,0:T(8,128)(2,1)S(1)}, bf16[512,1536]{1,0:T(8,128)(2,1)S(1)}, u32[]{:S(2)}, u32[]{:S(2)}) collective-permute-start(bf16[512,1536]{1,0:T(8,128)(2,1)S(1)} %get-tuple-element.88.rest_0_), channel_id=1, source_target_pairs={{0,1},{1,0},{2,3},{3,2},{4,5},{5,4},{6,7},{7,6},{8,9},{9,8},{10,11... | collective-permute-start | bytes 4718600 | tf_op jit(solution)/shard_map/gradients_core/ppermute | solution.py:23
  64.6 16.7 %collective-permute-start.17 = (bf16[512,1536]{1,0:T(8,128)(2,1)}, bf16[512,1536]{1,0:T(8,128)(2,1)S(1)}, u32[]{:S(2)}, u32[]{:S(2)}) collective-permute-start(bf16[512,1536]{1,0:T(8,128)(2,1)} %get-tuple-element.89.rest_1_.rest_2_), channel_id=1, source_target_pairs={{0,1},{1,0},{2,3},{3,2},{4,5},{5,4},{6,7},{7,6},{8,9},{9,8},{10,11... | collective-permute-start | bytes 4718600 | tf_op jit(solution)/shard_map/gradients_core/ppermute | solution.py:23
  65.7 27.4 %collective-permute-start.15 = (bf16[2,256,1536]{2,1,0:T(8,128)(2,1)S(1)}, bf16[2,256,1536]{2,1,0:T(8,128)(2,1)}, u32[]{:S(2)}, u32[]{:S(2)}) collective-permute-start(bf16[2,256,1536]{2,1,0:T(8,128)(2,1)S(1)} %pad_maximum_fusion.rest_0_), channel_id=1, source_target_pairs={{0,2},{1,5},{2,0},{3,7},{4,6},{5,1},{6,4},{7,3},{8,10},{9,13},{10,... | collective-permute-start | bytes 4718600 | tf_op jit(solution)/shard_map/pair_second/ppermute | solution.py:23
  66.2 15.1 %copy-start.6 = (bf16[512,1536]{1,0:T(8,128)(2,1)S(1)}, bf16[512,1536]{1,0:T(8,128)(2,1)}, u32[]{:S(2)}) copy-start(bf16[512,1536]{1,0:T(8,128)(2,1)} %copy-done.5) | copy-start | bytes 4718596
  79.8 29.7 %collective-permute-start.14 = (bf16[2,256,1536]{2,1,0:T(8,128)(2,1)S(1)}, bf16[2,256,1536]{2,1,0:T(8,128)(2,1)}, u32[]{:S(2)}, u32[]{:S(2)}) collective-permute-start(bf16[2,256,1536]{2,1,0:T(8,128)(2,1)S(1)} %get-tuple-element.98), channel_id=1, source_target_pairs={{0,2},{1,5},{2,0},{3,7},{4,6},{5,1},{6,4},{7,3},{8,10},{9,13},{10,... | collective-permute-start | bytes 4718600 | tf_op jit(solution)/shard_map/sum_1/ppermute | solution.py:23
  81.4 10.7 %copy-start = (bf16[512,1536]{1,0:T(8,128)(2,1)}, bf16[512,1536]{1,0:T(8,128)(2,1)S(1)}, u32[]{:S(2)}) copy-start(bf16[512,1536]{1,0:T(8,128)(2,1)S(1)} %collective-permute-done.17.rest_3_.rest_2_) | copy-start | bytes 4718596
  96.2 16.9 %collective-permute-start.18 = (bf16[512,1536]{1,0:T(8,128)(2,1)}, bf16[512,1536]{1,0:T(8,128)(2,1)S(1)}, u32[]{:S(2)}, u32[]{:S(2)}) collective-permute-start(bf16[512,1536]{1,0:T(8,128)(2,1)} %get-tuple-element.102.rest_1_.rest_0_), channel_id=1, source_target_pairs={{0,1},{1,0},{2,3},{3,2},{4,5},{5,4},{6,7},{7,6},{8,9},{9,8},{10,11... | collective-permute-start | bytes 4718600 | tf_op jit(solution)/shard_map/gradients_core/ppermute | solution.py:23
  96.3 16.8 %collective-permute-start.19 = (bf16[512,1536]{1,0:T(8,128)(2,1)}, bf16[512,1536]{1,0:T(8,128)(2,1)S(1)}, u32[]{:S(2)}, u32[]{:S(2)}) collective-permute-start(bf16[512,1536]{1,0:T(8,128)(2,1)} %get-tuple-element.103.rest_3_.rest_1_), channel_id=1, source_target_pairs={{0,1},{1,0},{2,3},{3,2},{4,5},{5,4},{6,7},{7,6},{8,9},{9,8},{10,11... | collective-permute-start | bytes 4718600 | tf_op jit(solution)/shard_map/gradients_core/ppermute | solution.py:23
  96.8 28.1 %collective-permute-start.13 = (bf16[2,256,1536]{2,1,0:T(8,128)(2,1)S(1)}, bf16[2,256,1536]{2,1,0:T(8,128)(2,1)}, u32[]{:S(2)}, u32[]{:S(2)}) collective-permute-start(bf16[2,256,1536]{2,1,0:T(8,128)(2,1)S(1)} %get-tuple-element.94), channel_id=1, source_target_pairs={{0,2},{1,5},{2,0},{3,7},{4,6},{5,1},{6,4},{7,3},{8,10},{9,13},{10,... | collective-permute-start | bytes 4718600 | tf_op jit(solution)/shard_map/sum_0/ppermute | solution.py:23
  111.3 1.7 %copy-start.1 = (bf16[512,1536]{1,0:T(8,128)(2,1)S(1)}, bf16[512,1536]{1,0:T(8,128)(2,1)}, u32[]{:S(2)}) copy-start(bf16[512,1536]{1,0:T(8,128)(2,1)} %copy-done) | copy-start | bytes 4718596
  111.4 17.9 %collective-permute-start.21 = (bf16[256,1536]{1,0:T(8,128)(2,1)S(1)}, bf16[256,1536]{1,0:T(8,128)(2,1)S(1)}, u32[]{:S(2)}, u32[]{:S(2)}) collective-permute-start(bf16[256,1536]{1,0:T(8,128)(2,1)S(1)} %get-tuple-element.107), channel_id=1, source_target_pairs={{0,4},{1,3},{2,6},{3,1},{4,0},{5,7},{6,2},{7,5},{8,12},{9,11},{10,... | collective-permute-start | bytes 2359304 | tf_op jit(solution)/shard_map/sum_1/ppermute | solution.py:23
  113.1 9.8 %copy-start.2 = (bf16[512,1536]{1,0:T(8,128)(2,1)}, bf16[512,1536]{1,0:T(8,128)(2,1)S(1)}, u32[]{:S(2)}) copy-start(bf16[512,1536]{1,0:T(8,128)(2,1)S(1)} %collective-permute-done.19.rest_3_) | copy-start | bytes 4718596
  126.7 6.8 %copy-start.3 = (bf16[512,1536]{1,0:T(8,128)(2,1)S(1)}, bf16[512,1536]{1,0:T(8,128)(2,1)}, u32[]{:S(2)}) copy-start(bf16[512,1536]{1,0:T(8,128)(2,1)} %copy-done.2) | copy-start | bytes 4718596
  126.7 6.8 %copy-start.9 = (bf16[512,1024]{1,0:T(8,128)(2,1)S(1)}, bf16[512,1024]{1,0:T(8,128)(2,1)}, u32[]{:S(2)}) copy-start(bf16[512,1024]{1,0:T(8,128)(2,1)} %copy-done.8) | copy-start | bytes 3145732
  126.7 21.2 %collective-permute-start.20 = (bf16[256,1536]{1,0:T(8,128)(2,1)S(1)}, bf16[256,1536]{1,0:T(8,128)(2,1)S(1)}, u32[]{:S(2)}, u32[]{:S(2)}) collective-permute-start(bf16[256,1536]{1,0:T(8,128)(2,1)S(1)} %get-tuple-element.111), channel_id=1, source_target_pairs={{0,4},{1,3},{2,6},{3,1},{4,0},{5,7},{6,2},{7,5},{8,12},{9,11},{10,... | collective-permute-start | bytes 2359304 | tf_op jit(solution)/shard_map/sum_0/ppermute | solution.py:23
  129.6 20.7 %collective-permute-start.22 = (bf16[128,1536]{1,0:T(8,128)(2,1)S(1)}, bf16[128,1536]{1,0:T(8,128)(2,1)S(1)}, u32[]{:S(2)}, u32[]{:S(2)}) collective-permute-start(bf16[128,1536]{1,0:T(8,128)(2,1)S(1)} %get-tuple-element.123), channel_id=1, source_target_pairs={{0,8},{1,9},{2,10},{3,11},{4,12},{5,13},{6,14},{7,15},{8,16},{9,17... | collective-permute-start | bytes 1179656 | tf_op jit(solution)/shard_map/sum_3_z/ppermute | solution.py:23
  129.7 18.2 %collective-permute-start.23 = (bf16[128,1536]{1,0:T(8,128)(2,1)S(1)}, bf16[128,1536]{1,0:T(8,128)(2,1)S(1)}, u32[]{:S(2)}, u32[]{:S(2)}) collective-permute-start(bf16[128,1536]{1,0:T(8,128)(2,1)S(1)} %get-tuple-element.124), channel_id=1, source_target_pairs={{0,24},{1,25},{2,26},{3,27},{4,28},{5,29},{6,30},{7,31},{8,0},{9,1... | collective-permute-start | bytes 1179656 | tf_op jit(solution)/shard_map/sum_2_z/ppermute | solution.py:23
  148.2 9.3 %collective-permute-start.24 = (bf16[128,1536]{1,0:T(8,128)(2,1)S(1)}, bf16[128,1536]{1,0:T(8,128)(2,1)S(1)}, u32[]{:S(2)}, u32[]{:S(2)}) collective-permute-start(bf16[128,1536]{1,0:T(8,128)(2,1)S(1)} %slice_add_fusion), channel_id=1, source_target_pairs={{0,24},{1,25},{2,26},{3,27},{4,28},{5,29},{6,30},{7,31},{8,0},{9,1... | collective-permute-start | bytes 1179656 | tf_op jit(solution)/shard_map/sum_1_z/ppermute | solution.py:23
  (4 other events, 5.2 us)

commit v5 on v4

--- a/solution.py
+++ b/solution.py
@@ -169,13 +169,13 @@
             copies(at, lambda copy: copy.wait())
 
 
-def forward_placed(rows, weights, table, jx, part, parts, places, size, at, before):
+def forward_placed(rows, weights, table, jx, part, parts, places, at, before):
     experts, tokens, depth = rows.shape
     width = weights[0].shape[1] // at.owners
     tile = tile_of(width // parts, 384)
     per = width // parts // tile
     plan, shapes = [], []
-    for first, stride in places:
+    for first, stride, size in places:
         plan.append((first, stride, size, [len(shapes) + k for k in range(at.nx)]))
         shapes += [jax.ShapeDtypeStruct((at.ny, size, width), BF16)] * at.nx
     block = pl.BlockSpec((depth, tile), lambda j, t: (0, (t[0] * parts + part) * per + j))
@@ -415,7 +415,7 @@
     order = [(jz, jy) for turn in turns for jy in range(ny) for jz in turn]
     size = len(turns[0]) * rows
     half = ny * size
-    places = [(0, size), (half, size)]
+    places = [(i * rows, size, rows) for i in range(len(turns[0]))] + [(half, size, size)]
     swapped = ((at.core == 1) if at.mixed else (at.core < 0)).astype(jnp.int32)[None]
     back_x = (at.x - jnp.arange(nx)) % nx * at.nc
     mine = (back_x + at.core).astype(jnp.int32)
@@ -452,10 +452,7 @@
             weights = both(tie(weight, tables, hiddens), "weight_core")
     first[0] = jnp.stack(first[0])
     second = [gathered(at.ring_2, first[0], "own_second")]
-    tables = tie(gathered(at.ring_y, tables, "routes_y"), plane[1])
-    plane.append(shifted(1, plane[1], "plane_2"))
-    first.append(gathered(at.ring_1, plane[1], "plane_1_first"))
-    backward_z = shifted(nz - 1, tie(grad_out, plane[1]), "plane_3")
+    tables = gathered(at.ring_y, tables, "routes_y")
     packed = jnp.stack([tables[jy][jz] for jz, jy in order])
 
     expert = lax.axis_index("expert")
@@ -470,12 +467,12 @@
     rows_in, turned = token_rows(slot_of, gate, hiddens, tie(shards, first[0]))
     slot_of, gate = slot_of[0], gate[0]
 
-    calls = [(0, 0, 2), (0, 1, 2)] + [(jx, 0, 1) for jx in range(1, nx)]
+    calls = [(jx, part, 2) for jx in range(nx) for part in range(2)]
 
     def forward(call, placed, *after):
         jx, part, parts = call
         table = tie(forward_tables[jx], *after)
-        return forward_placed(rows_in, weights, table, jx, part, parts, places, size, at, placed)
+        return forward_placed(rows_in, weights, table, jx, part, parts, places, at, placed)
 
     def assembled(blocks):
         plan = []
@@ -486,20 +483,23 @@
                     plan.append((number, j1, (j1, j2), i * rows, size, blocks[number].shape[1]))
         return list(put_together(plan, blocks, swapped, nx, (half, width)))
 
-    first[1] = jnp.stack(tie(first[1], rows_in))
+    plane[1] = tie(plane[1], rows_in)
+    plane.append(shifted(1, plane[1], "plane_2"))
+    plane.append(shifted(nz - 1, tie(grad_out, plane[1]), "plane_3"))
+    first.append(gathered(at.ring_1, plane[1], "plane_1_first"))
+    done = forward(calls[0], None, plane[1])
+    first[1] = jnp.stack(tie(first[1], done))
     second.append(gathered(at.ring_2, first[1], "plane_1_second"))
-    done = forward(calls[0], None, first[1], second[0])
-    plane[2], plane_3 = tie((plane[2], backward_z), done)
-    pair = jnp.stack([plane[2], plane_3])
+    done = forward(calls[1], done, first[1], second[0])
+    pair = jnp.stack(tie(plane[2:], done))
     first.append(gathered(at.ring_1, pair, "pair_first"))
-    done = forward(calls[1], done, pair)
+    for call in calls[2:-1]:
+        done = forward(call, done, pair)
     first[2] = jnp.stack(tie(first[2], done)).reshape(ny, size, width)
     second.append(gathered(at.ring_2, first[2], "pair_second"))
     grads_1 = assembled(tie(second[0] + second[1], done))
     others_1 = [both(block, "gradients_core")[-1] for block in grads_1] if two else []
-    placed = done
-    for call in calls[2:]:
-        placed = forward(call, placed, first[2], grads_1)
+    placed = forward(calls[-1], done, first[2], grads_1)
 
     class Sum:
         def __init__(self, turn):
@@ -522,7 +522,7 @@
             self.terms = [self.terms[j] for j in range(ny)]
             self.start(at.ring_1)
 
-    near, far = Sum(0), Sum(1)
+    own_sum, next_sum, far = [Sum(i) for i in range(len(places))]
     far.start(at.ring_2)
     ask = tie(hidden_table, far.sent)
     count = len(order) // 2
@@ -530,22 +530,23 @@
 
     grads_2 = assembled(tie(second[2], back))
     others_2 = [both(block, "gradients_core")[-1] for block in grads_2] if two else []
-    ask = tie(mine, grads_2)
-    grad_weight = weight_gradient(turned, list(zip(grads_1, grads_2)), ask, weight.shape, None)
+    next_sum.start(at.ring_2, back)
+    pairs = list(zip(grads_1, grads_2))
+    ask = tie(mine, grads_2, next_sum.sent)
+    grad_weight = weight_gradient(turned, pairs, ask, weight.shape, None)
     far.finish(grad_weight)
     far.second()
-    near.start(at.ring_2)
-    ask = tie(theirs, far.sent, near.sent)
     if two:
-        grad_weight = weight_gradient(
-            turned, list(zip(others_1, others_2)), ask, weight.shape, grad_weight
-        )
-    far.finish(grad_weight)
-    near.finish(grad_weight)
-    near.second()
+        pairs = list(zip(others_1, others_2))
+        ask = tie(theirs, far.sent)
+        grad_weight = weight_gradient(turned, pairs, ask, weight.shape, grad_weight)
+    own_sum.start(at.ring_2, grad_weight)
+    next_sum.finish(grad_weight)
+    far.finish((grad_weight, next_sum.terms))
+    next_sum.second()
     last = shifted(nz - 3, far.terms[rows:], "sum_3_z")
     onward = shifted(nz - 1, far.terms[:rows], "sum_2_z")
-    ask = tie(hidden_table, far.terms, near.sent)
+    ask = tie(hidden_table, own_sum.sent, next_sum.sent, far.terms)
     grad_hidden = hidden_gradient(
         gate[count:],
         slot_of[count:],
@@ -555,10 +556,14 @@
         capacity,
         back,
     )
-    near.finish(grad_hidden)
-    onward = tie(onward, grad_hidden) + near.terms[rows:]
+    own_sum.finish(grad_hidden)
+    own_sum.second()
+    next_sum.finish(grad_hidden)
+    onward, last = tie((onward, last), grad_hidden)
+    onward = tie(onward, last) + next_sum.terms
     onward = shifted(nz - 1, onward, "sum_1_z")
-    mixed_out = near.terms[:rows].astype(F32) + last.astype(F32) + onward.astype(F32)
+    own_sum.finish(grad_hidden)
+    mixed_out = own_sum.terms.astype(F32) + last.astype(F32) + onward.astype(F32)
     return (mixed_out.astype(BF16), grad_hidden[None], grad_weight[None])
 
 

time: 159 us -> 155 us (0.975)
  waiting for transfers between devices: 24.5 us -> 15.3 us
  Pallas kernels: 88 us -> 92.9 us
  starting transfers between devices: 30 us -> 33 us
  other arithmetic: 9.36 us -> 6.4 us
    ppermute x25 -> x27, waiting for transfers between devices: 24.5 us -> 15.3 us  [shift(): return lax.ppermute(block, ALL, self.perm)]
    pallas_call x3 -> x4, Pallas kernels: 30.2 us -> 33.7 us  [forward_placed(): pl.pallas_call(functools.partial(place_kernel, jx, part * per, at.ny, pla...]
    ppermute x25 -> x27, starting transfers between devices: 30 us -> 33 us  [shift(): return lax.ppermute(block, ALL, self.perm)]
    add x4, other arithmetic: 4.06 us -> 1.01 us  [finish(): self.terms = self.terms[0] + tie(self.got, after)]
    unnamed x23 -> x22, local copies, waits for them, and re-layouts: 4.51 us -> 4.52 us
  transfers between devices with their start and end apart: 25 -> 27, of which waited for: 6 -> 5; matrix products, arithmetic and copies ran while one was open for 6% -> 4% of each run, Pallas kernels for 56% -> 60%
where the time goes in v5:
time: 155 us; the launch traced here: 154 us
  Pallas kernels  92.9 us (60%)
  starting transfers between devices  33 us (21%)
  waiting for transfers between devices  15.3 us (10%)
  other arithmetic  6.4 us (4%)
  local copies, waits for them, and re-layouts  5.56 us (4%)
    pallas_call x4, Pallas kernels, forward_placed(): pl.pallas_call(functools.partial(place_kernel, jx, part * per, at.ny, pla...  33.7 us
    ppermute x27, starting transfers between devices, shift(): return lax.ppermute(block, ALL, self.perm)  33 us
    pallas_call x2, Pallas kernels, hidden_gradient(): pl.pallas_call(functools.partial(hidden_kernel, steps, per, number, last)...  23.7 us
    pallas_call x2, Pallas kernels, weight_gradient(): pl.pallas_call(kernel, grid_spec=pltpu.PrefetchScalarGridSpec(num_scalar_...  21.5 us
    ppermute x27, waiting for transfers between devices, shift(): return lax.ppermute(block, ALL, self.perm)  15.3 us
    pallas_call x1, Pallas kernels, token_rows(): pl.pallas_call(functools.partial(rows_kernel, size), grid_spec=pltpu.Pref...  7.59 us
    pallas_call x2, Pallas kernels, put_together(): pl.pallas_call(functools.partial(gather_kernel, plan, count), grid_spec=p...  6.36 us
    unnamed x22, local copies, waits for them, and re-layouts  4.52 us
  transfers between devices with their start and end apart: 27, of which 5 were waited for; matrix products, arithmetic and copies ran while one was open for 4% of the time, Pallas kernels for 60%

profile of v5, /device:TPU:0, one launch (start us, length us, event | category | flops | bytes accessed | tf_op | source)
XLA Modules:
  0.0 154.2 jit_solution(2295227417960395896)
XLA Ops:
  2.5 2.6 %collective-permute-start = (f32[1,4,128]{2,1,0:T(4,128)S(1)}, f32[1,4,128]{2,1,0:T(4,128)S(1)}, u32[]{:S(2)}, u32[]{:S(2)}) collective-permute-start(f32[1,4,128]{2,1,0:T(4,128)S(1)} %maximum_bitcast_fusion), channel_id=1, source_target_pairs={{0,8},{1,9},{2,10},{3,11},{4,12},{5,13},{6,14},{7,15},{8,16},{9,17... | collective-permute-start | bytes 6152 | tf_op jit(solution)/shard_map/routes_z/ppermute | solution.py:23
  5.1 1.5 collective-permute-start.1
  8.8 4.3 %collective-permute-done.1 = bf16[128,1536]{1,0:T(8,128)(2,1)S(1)} collective-permute-done((bf16[128,1536]{1,0:T(8,128)(2,1)}, bf16[128,1536]{1,0:T(8,128)(2,1)S(1)}, u32[]{:S(2)}, u32[]{:S(2)}) %collective-permute-start.1) | collective-permute-done | bytes 393248 | tf_op jit(solution)/shard_map/own_first/ppermute | solution.py:23
  13.1 2.6 %collective-permute-start.3 = (f32[2,4,128]{2,1,0:T(4,128)S(1)}, f32[2,4,128]{2,1,0:T(4,128)S(1)}, u32[]{:S(2)}, u32[]{:S(2)}) collective-permute-start(f32[2,4,128]{2,1,0:T(4,128)S(1)} %pad_maximum_fusion.6), channel_id=1, source_target_pairs={{0,16},{1,17},{2,18},{3,19},{4,20},{5,21},{6,22},{7,23},{8,24},{9,... | collective-permute-start | bytes 12296 | tf_op jit(solution)/shard_map/routes_z/ppermute | solution.py:23
  15.9 1.7 %collective-permute-done.3 = f32[2,4,128]{2,1,0:T(4,128)S(1)} collective-permute-done((f32[2,4,128]{2,1,0:T(4,128)S(1)}, f32[2,4,128]{2,1,0:T(4,128)S(1)}, u32[]{:S(2)}, u32[]{:S(2)}) %collective-permute-start.3) | collective-permute-done | bytes 4128 | tf_op jit(solution)/shard_map/routes_z/ppermute | solution.py:23
  17.6 1.5 collective-permute-start.4
  20.2 1.6 %collective-permute-start.10 = (bf16[2,128,1536]{2,1,0:T(8,128)(2,1)S(1)}, bf16[2,128,1536]{2,1,0:T(8,128)(2,1)S(1)}, u32[]{:S(2)}, u32[]{:S(2)}) collective-permute-start(bf16[2,128,1536]{2,1,0:T(8,128)(2,1)S(1)} %pad_maximum_fusion.1.rest_0_), channel_id=1, source_target_pairs={{0,2},{1,5},{2,0},{3,7},{4,6},{5,1},{6,4},{7,3},{8,10},{9,13},{10,... | collective-permute-start | bytes 2359304 | tf_op jit(solution)/shard_map/own_second/ppermute | solution.py:23
  22.0 1.6 %copy-done.4 = bf16[1,1024,1024]{2,1,0:T(8,128)(2,1)S(1)} copy-done((bf16[1,1024,1024]{2,1,0:T(8,128)(2,1)S(1)}, bf16[1,1024,1024]{2,1,0:T(8,128)(2,1)}, u32[]{:S(2)}) %copy-start.4) | copy-done | bytes 2097176
  23.6 7.6 %token_rows.1 = (bf16[2,1024,1024]{2,1,0:T(8,128)(2,1)}, bf16[1024,1024]{1,0:T(8,128)(2,1)S(1)}) custom-call(s32[8]{0:T(128)S(1)} %stack.84.shards, s32[2,8,128]{2,1,0:T(8,128)S(1)} %fusion.slots, f32[2,8,128]{2,1,0:T(8,128)S(1)} %get-tuple-element.157.gates, bf16[1024,1024]{1,0:T(8,128)(2,1)S(1)} %bitcast.52, bf16[1024,1024]{1,0:T(8,128)(2,1)} %collective-permute-done.5.rest_1_), custom_call_target="tpu_custom_call" | custom-call | flops 2147483648 | bytes 8388608 | tf_op jit(solution)/shard_map/token_rows/pallas_call | solution.py:111
  32.3 1.6 %collective-permute-start.6 = (bf16[128,1536]{1,0:T(8,128)(2,1)S(1)}, bf16[128,1536]{1,0:T(8,128)(2,1)S(1)}, u32[]{:S(2)}, u32[]{:S(2)}) collective-permute-start(bf16[128,1536]{1,0:T(8,128)(2,1)S(1)} %collective-permute-done.2), channel_id=1, source_target_pairs={{0,8},{1,9},{2,10},{3,11},{4,12},{5,13},{6,14},{7,15},{8,16},{9,17... | collective-permute-start | bytes 1179656 | tf_op jit(solution)/shard_map/plane_2/ppermute | solution.py:23
  33.9 2.3 %collective-permute-start.7 = (bf16[128,1536]{1,0:T(8,128)(2,1)S(1)}, bf16[128,1536]{1,0:T(8,128)(2,1)S(1)}, u32[]{:S(2)}, u32[]{:S(2)}) collective-permute-start(bf16[128,1536]{1,0:T(8,128)(2,1)S(1)} %copy-done.10), channel_id=1, source_target_pairs={{0,24},{1,25},{2,26},{3,27},{4,28},{5,29},{6,30},{7,31},{8,0},{9,1... | collective-permute-start | bytes 1179656 | tf_op jit(solution)/shard_map/plane_3/ppermute | solution.py:23
  36.2 8.4 %forward_placed.4 = (bf16[2,128,1536]{2,1,0:T(8,128)(2,1)S(1)}, bf16[2,128,1536]{2,1,0:T(8,128)(2,1)S(1)}, bf16[2,128,1536]{2,1,0:T(8,128)(2,1)S(1)}, bf16[2,128...) custom-call(s32[2]{0:T(128)S(1)} %pad_add_fusion.1.table, ...), custom_call_target="tpu_custom_call" | custom-call | flops 3221225472 | bytes 6291456 | tf_op jit(solution)/shard_map/forward_placed/pallas_call | solution.py:189
  44.7 1.6 %collective-permute-start.12 = (bf16[2,128,1536]{2,1,0:T(8,128)(2,1)S(1)}, bf16[2,128,1536]{2,1,0:T(8,128)(2,1)S(1)}, u32[]{:S(2)}, u32[]{:S(2)}) collective-permute-start(bf16[2,128,1536]{2,1,0:T(8,128)(2,1)S(1)} %pad_maximum_fusion.2.rest_2_), channel_id=1, source_target_pairs={{0,2},{1,5},{2,0},{3,7},{4,6},{5,1},{6,4},{7,3},{8,10},{9,13},{10,... | collective-permute-start | bytes 2359304 | tf_op jit(solution)/shard_map/plane_1_second/ppermute | solution.py:23
  46.3 8.4 %forward_placed.5 = (bf16[2,128,1536]{2,1,0:T(8,128)(2,1)S(1)}, bf16[2,128,1536]{2,1,0:T(8,128)(2,1)S(1)}, bf16[2,128,1536]{2,1,0:T(8,128)(2,1)S(1)}, bf16[2,128...) custom-call(s32[2]{0:T(128)S(1)} %pad_add_fusion.1.table, ...), custom_call_target="tpu_custom_call", output_to_operand_aliasing={{0}: (4, {}), {1}: (5, {}), {2}: (6, {}), {3}: (7, {}), {4}... | custom-call | flops 3221225472 | bytes 6291456 | tf_op jit(solution)/shard_map/forward_placed/pallas_call | solution.py:189
  55.3 8.4 %forward_placed.6 = (bf16[2,128,1536]{2,1,0:T(8,128)(2,1)S(1)}, bf16[2,128,1536]{2,1,0:T(8,128)(2,1)S(1)}, bf16[2,128,1536]{2,1,0:T(8,128)(2,1)S(1)}, bf16[2,128...) custom-call(s32[2]{0:T(128)S(1)} %pad_add_fusion.table, ...), custom_call_target="tpu_custom_call", output_to_operand_aliasing={{0}: (4, {}), {1}: (5, {}), {2}: (6, {}), {3}: (7, {}), {4}... | custom-call | flops 3221225472 | bytes 6291456 | tf_op jit(solution)/shard_map/forward_placed/pallas_call | solution.py:189
  63.7 3.4 %put_together.2 = (bf16[512,1536]{1,0:T(8,128)(2,1)S(1)}, bf16[512,1536]{1,0:T(8,128)(2,1)}) custom-call(s32[1]{0:T(128)} %bitcast.swapped, bf16[2,128,1536]{2,1,0:T(8,128)(2,1)S(1)} %pad_maximum_fusion.1.rest_0_, bf16[2,128,1536]{2,1,0:T(8,128)(2,1)S(1)} %collective-permute-done.10.rest_1_, bf16[2,128,1536]{2,1,0:T(8,128)(2,1)S(1)} %pad_maximum_fusion.2.rest_2_, ...), custom_call_target="tpu_custom_call" | custom-call | bytes 6291456 | tf_op jit(solution)/shard_map/put_together/pallas_call | solution.py:242
  69.3 8.4 %forward_placed.7 = (bf16[2,128,1536]{2,1,0:T(8,128)(2,1)S(1)}, bf16[2,128,1536]{2,1,0:T(8,128)(2,1)S(1)}, bf16[2,128,1536]{2,1,0:T(8,128)(2,1)S(1)}, bf16[2,128...) custom-call(s32[2]{0:T(128)S(1)} %pad_add_fusion.table, ...), custom_call_target="tpu_custom_call", output_to_operand_aliasing={{0}: (4, {}), {1}: (5, {}), {2}: (6, {}), {3}: (7, {}), {4}... | custom-call | flops 3221225472 | bytes 6291456 | tf_op jit(solution)/shard_map/forward_placed/pallas_call | solution.py:189
  78.8 10.7 %hidden_gradient.2.rest_4_ = bf16[512,1024]{1,0:T(8,128)(2,1)S(1)} custom-call(s32[12]{0:T(128)S(1)} %concatenate.28.table, f32[4,128]{1,0:T(4,128)S(1)} %get-tuple-element.172.gates, s32[4,128]{1,0:T(4,128)S(1)} %get-tuple-element.170.slots, bf16[1024,6144]{1,0:T(8,128)(2,1)} %bitcast.58, bf16[512,1536]{1,0:T(8,128)(2,1)S(1)} %copy-done.6, ...), custom_call_target="tpu_custom_call" | custom-call | flops 6442450944 | bytes 18874368 | tf_op jit(solution)/shard_map/hidden_gradient/pallas_call | solution.py:385
  90.5 3.0 %put_together.3 = (bf16[512,1536]{1,0:T(8,128)(2,1)}, bf16[512,1536]{1,0:T(8,128)(2,1)}) custom-call(s32[1]{0:T(128)} %bitcast.swapped, bf16[2,256,1536]{2,1,0:T(8,128)(2,1)S(1)} %pad_maximum_fusion.rest_0_, bf16[2,256,1536]{2,1,0:T(8,128)(2,1)} %collective-permute-done.14.rest_1_), custom_call_target="tpu_custom_call" | custom-call | bytes 6291456 | tf_op jit(solution)/shard_map/put_together/pallas_call | solution.py:242
  95.1 1.4 copy-done.7
  96.5 10.8 %weight_gradient.2.rest_4_ = bf16[1024,6144]{1,0:T(8,128)(2,1)} custom-call(s32[2]{0:T(128)S(1)} %get-tuple-element.135.quarters, bf16[1024,1024]{1,0:T(8,128)(2,1)S(1)} %get-tuple-element.136.turned, bf16[512,1536]{1,0:T(8,128)(2,1)S(1)} %copy-done.7, bf16[512,1536]{1,0:T(8,128)(2,1)} %get-tuple-element.130.rest_1_.rest_0_, ...), custom_call_target="tpu_custom_call" | custom-call | flops 6442450944 | bytes 12582912 | tf_op jit(solution)/shard_map/weight_gradient/pallas_call | solution.py:304
  107.9 1.2 collective-permute-start.21
  109.2 10.7 %weight_gradient.3 = bf16[1024,6144]{1,0:T(8,128)(2,1)} custom-call(s32[2]{0:T(128)S(1)} %get-tuple-element.139.quarters, bf16[1024,1024]{1,0:T(8,128)(2,1)S(1)} %get-tuple-element.136.turned, bf16[512,1536]{1,0:T(8,128)(2,1)S(1)} %collective-permute-done.15.rest_2_.rest_0_, ...), custom_call_target="tpu_custom_call", output_to_operand_aliasing={{}: (6, {})} | custom-call | flops 6442450944 | bytes 12582912 | tf_op jit(solution)/shard_map/weight_gradient/pallas_call | solution.py:304
  120.2 1.2 collective-permute-start.25
  121.3 1.5 collective-permute-start.19
  123.2 3.8 %collective-permute-start.23 = (bf16[128,1536]{1,0:T(8,128)(2,1)S(1)}, bf16[128,1536]{1,0:T(8,128)(2,1)S(1)}, u32[]{:S(2)}, u32[]{:S(2)}) collective-permute-start(bf16[128,1536]{1,0:T(8,128)(2,1)S(1)} %get-tuple-element.166), channel_id=1, source_target_pairs={{0,24},{1,25},{2,26},{3,27},{4,28},{5,29},{6,30},{7,31},{8,0},{9,1... | collective-permute-start | bytes 1179656 | tf_op jit(solution)/shard_map/sum_2_z/ppermute | solution.py:23
  127.0 13.0 %hidden_gradient.3 = bf16[1024,1024]{1,0:T(8,128)(2,1)} custom-call(s32[12]{0:T(128)S(1)} %concatenate.28.table, f32[4,128]{1,0:T(4,128)S(1)} %get-tuple-element.171.gates, s32[4,128]{1,0:T(4,128)S(1)} %get-tuple-element.169.slots, bf16[1024,6144]{1,0:T(8,128)(2,1)} %bitcast.59, bf16[512,1536]{1,0:T(8,128)(2,1)} %get-tuple-element.130.rest_1_.rest_0_, ...), custom_call_target="tpu_custom_call" | custom-call | flops 6442450944 | bytes 18874368 | tf_op jit(solution)/shard_map/hidden_gradient/pallas_call | solution.py:385
  140.0 2.0 %collective-permute-done.23 = bf16[128,1536]{1,0:T(8,128)(2,1)S(1)} collective-permute-done((bf16[128,1536]{1,0:T(8,128)(2,1)S(1)}, bf16[128,1536]{1,0:T(8,128)(2,1)S(1)}, u32[]{:S(2)}, u32[]{:S(2)}) %collective-permute-start.23) | collective-permute-done | bytes 393248 | tf_op jit(solution)/shard_map/sum_2_z/ppermute | solution.py:23
  142.3 1.7 %collective-permute-start.22 = (bf16[128,1536]{1,0:T(8,128)(2,1)S(1)}, bf16[128,1536]{1,0:T(8,128)(2,1)S(1)}, u32[]{:S(2)}, u32[]{:S(2)}) collective-permute-start(bf16[128,1536]{1,0:T(8,128)(2,1)S(1)} %get-tuple-element.150), channel_id=1, source_target_pairs={{0,4},{1,3},{2,6},{3,1},{4,0},{5,7},{6,2},{7,5},{8,12},{9,11},{10,... | collective-permute-start | bytes 1179656 | tf_op jit(solution)/shard_map/sum_0/ppermute | solution.py:23
  144.1 2.1 %collective-permute-start.26 = (bf16[128,1536]{1,0:T(8,128)(2,1)S(1)}, bf16[128,1536]{1,0:T(8,128)(2,1)S(1)}, u32[]{:S(2)}, u32[]{:S(2)}) collective-permute-start(bf16[128,1536]{1,0:T(8,128)(2,1)S(1)} %add_add_fusion), channel_id=1, source_target_pairs={{0,24},{1,25},{2,26},{3,27},{4,28},{5,29},{6,30},{7,31},{8,0},{9,1... | collective-permute-start | bytes 1179656 | tf_op jit(solution)/shard_map/sum_1_z/ppermute | solution.py:23
  146.1 4.0 %collective-permute-done.22 = bf16[128,1536]{1,0:T(8,128)(2,1)S(1)} collective-permute-done((bf16[128,1536]{1,0:T(8,128)(2,1)S(1)}, bf16[128,1536]{1,0:T(8,128)(2,1)S(1)}, u32[]{:S(2)}, u32[]{:S(2)}) %collective-permute-start.22) | collective-permute-done | bytes 393248 | tf_op jit(solution)/shard_map/sum_0/ppermute | solution.py:23
  150.2 3.1 %collective-permute-done.26 = bf16[128,1536]{1,0:T(8,128)(2,1)S(1)} collective-permute-done((bf16[128,1536]{1,0:T(8,128)(2,1)S(1)}, bf16[128,1536]{1,0:T(8,128)(2,1)S(1)}, u32[]{:S(2)}, u32[]{:S(2)}) %collective-permute-start.26) | collective-permute-done | bytes 393248 | tf_op jit(solution)/shard_map/sum_1_z/ppermute | solution.py:23
  (89 shorter events, 15.7 us)
Async XLA Ops:
  0.6 12.5 %collective-permute-start.5 = (bf16[1024,1024]{1,0:T(8,128)(2,1)}, bf16[1024,1024]{1,0:T(8,128)(2,1)}, u32[]{:S(2)}, u32[]{:S(2)}) collective-permute-start(bf16[1024,1024]{1,0:T(8,128)(2,1)} %bitcast.51), channel_id=1, source_target_pairs={{0,1},{1,0},{2,3},{3,2},{4,5},{5,4},{6,7},{7,6},{8,9},{9,8},{10,11... | collective-permute-start | bytes 6291464 | tf_op jit(solution)/shard_map/hidden_core/ppermute | solution.py:23
  2.5 6.2 %collective-permute-start = (f32[1,4,128]{2,1,0:T(4,128)S(1)}, f32[1,4,128]{2,1,0:T(4,128)S(1)}, u32[]{:S(2)}, u32[]{:S(2)}) collective-permute-start(f32[1,4,128]{2,1,0:T(4,128)S(1)} %maximum_bitcast_fusion), channel_id=1, source_target_pairs={{0,8},{1,9},{2,10},{3,11},{4,12},{5,13},{6,14},{7,15},{8,16},{9,17... | collective-permute-start | bytes 6152 | tf_op jit(solution)/shard_map/routes_z/ppermute | solution.py:23
  5.1 8.0 %collective-permute-start.1 = (bf16[128,1536]{1,0:T(8,128)(2,1)}, bf16[128,1536]{1,0:T(8,128)(2,1)S(1)}, u32[]{:S(2)}, u32[]{:S(2)}) collective-permute-start(bf16[128,1536]{1,0:T(8,128)(2,1)} %param.7), channel_id=1, source_target_pairs={{0,4},{1,3},{2,6},{3,1},{4,0},{5,7},{6,2},{7,5},{8,12},{9,11},{10,... | collective-permute-start | bytes 1179656 | tf_op jit(solution)/shard_map/own_first/ppermute | solution.py:23
  13.1 23.1 %collective-permute-start.9 = (bf16[1024,6144]{1,0:T(8,128)(2,1)}, bf16[1024,6144]{1,0:T(8,128)(2,1)}, u32[]{:S(2)}, u32[]{:S(2)}) collective-permute-start(bf16[1024,6144]{1,0:T(8,128)(2,1)} %bitcast.53), channel_id=1, source_target_pairs={{0,1},{1,0},{2,3},{3,2},{4,5},{5,4},{6,7},{7,6},{8,9},{9,8},{10,11... | collective-permute-start | bytes 37748744 | tf_op jit(solution)/shard_map/weight_core/ppermute | solution.py:23
  13.1 4.5 %collective-permute-start.3 = (f32[2,4,128]{2,1,0:T(4,128)S(1)}, f32[2,4,128]{2,1,0:T(4,128)S(1)}, u32[]{:S(2)}, u32[]{:S(2)}) collective-permute-start(f32[2,4,128]{2,1,0:T(4,128)S(1)} %pad_maximum_fusion.6), channel_id=1, source_target_pairs={{0,16},{1,17},{2,18},{3,19},{4,20},{5,21},{6,22},{7,23},{8,24},{9,... | collective-permute-start | bytes 12296 | tf_op jit(solution)/shard_map/routes_z/ppermute | solution.py:23
  15.9 15.4 %collective-permute-start.2 = (bf16[128,1536]{1,0:T(8,128)(2,1)}, bf16[128,1536]{1,0:T(8,128)(2,1)S(1)}, u32[]{:S(2)}, u32[]{:S(2)}) collective-permute-start(bf16[128,1536]{1,0:T(8,128)(2,1)} %param.7), channel_id=1, source_target_pairs={{0,8},{1,9},{2,10},{3,11},{4,12},{5,13},{6,14},{7,15},{8,16},{9,17... | collective-permute-start | bytes 1179656 | tf_op jit(solution)/shard_map/plane_1/ppermute | solution.py:23
  17.6 4.2 %collective-permute-start.4 = (f32[4,4,128]{2,1,0:T(4,128)S(1)}, f32[4,4,128]{2,1,0:T(4,128)S(1)}, u32[]{:S(2)}, u32[]{:S(2)}) collective-permute-start(f32[4,4,128]{2,1,0:T(4,128)S(1)} %pad_maximum_fusion.5), channel_id=1, source_target_pairs={{0,4},{1,5},{2,6},{3,7},{4,0},{5,1},{6,2},{7,3},{8,12},{9,13},{10,... | collective-permute-start | bytes 24584 | tf_op jit(solution)/shard_map/routes_y/ppermute | solution.py:23
  20.2 26.0 %collective-permute-start.10 = (bf16[2,128,1536]{2,1,0:T(8,128)(2,1)S(1)}, bf16[2,128,1536]{2,1,0:T(8,128)(2,1)S(1)}, u32[]{:S(2)}, u32[]{:S(2)}) collective-permute-start(bf16[2,128,1536]{2,1,0:T(8,128)(2,1)S(1)} %pad_maximum_fusion.1.rest_0_), channel_id=1, source_target_pairs={{0,2},{1,5},{2,0},{3,7},{4,6},{5,1},{6,4},{7,3},{8,10},{9,13},{10,... | collective-permute-start | bytes 2359304 | tf_op jit(solution)/shard_map/own_second/ppermute | solution.py:23
  23.6 10.3 %copy-start.10 = (bf16[128,1536]{1,0:T(8,128)(2,1)S(1)}, bf16[128,1536]{1,0:T(8,128)(2,1)}, u32[]{:S(2)}) copy-start(bf16[128,1536]{1,0:T(8,128)(2,1)} %param.7) | copy-start | bytes 1179652
  31.2 13.4 %collective-permute-start.8 = (bf16[128,1536]{1,0:T(8,128)(2,1)S(1)}, bf16[128,1536]{1,0:T(8,128)(2,1)S(1)}, u32[]{:S(2)}, u32[]{:S(2)}) collective-permute-start(bf16[128,1536]{1,0:T(8,128)(2,1)S(1)} %collective-permute-done.2), channel_id=1, source_target_pairs={{0,4},{1,3},{2,6},{3,1},{4,0},{5,7},{6,2},{7,5},{8,12},{9,11},{10,... | collective-permute-start | bytes 1179656 | tf_op jit(solution)/shard_map/plane_1_first/ppermute | solution.py:23
  32.3 22.4 %collective-permute-start.6 = (bf16[128,1536]{1,0:T(8,128)(2,1)S(1)}, bf16[128,1536]{1,0:T(8,128)(2,1)S(1)}, u32[]{:S(2)}, u32[]{:S(2)}) collective-permute-start(bf16[128,1536]{1,0:T(8,128)(2,1)S(1)} %collective-permute-done.2), channel_id=1, source_target_pairs={{0,8},{1,9},{2,10},{3,11},{4,12},{5,13},{6,14},{7,15},{8,16},{9,17... | collective-permute-start | bytes 1179656 | tf_op jit(solution)/shard_map/plane_2/ppermute | solution.py:23
  33.9 20.8 %collective-permute-start.7 = (bf16[128,1536]{1,0:T(8,128)(2,1)S(1)}, bf16[128,1536]{1,0:T(8,128)(2,1)S(1)}, u32[]{:S(2)}, u32[]{:S(2)}) collective-permute-start(bf16[128,1536]{1,0:T(8,128)(2,1)S(1)} %copy-done.10), channel_id=1, source_target_pairs={{0,24},{1,25},{2,26},{3,27},{4,28},{5,29},{6,30},{7,31},{8,0},{9,1... | collective-permute-start | bytes 1179656 | tf_op jit(solution)/shard_map/plane_3/ppermute | solution.py:23
  44.7 19.0 %collective-permute-start.12 = (bf16[2,128,1536]{2,1,0:T(8,128)(2,1)S(1)}, bf16[2,128,1536]{2,1,0:T(8,128)(2,1)S(1)}, u32[]{:S(2)}, u32[]{:S(2)}) collective-permute-start(bf16[2,128,1536]{2,1,0:T(8,128)(2,1)S(1)} %pad_maximum_fusion.2.rest_2_), channel_id=1, source_target_pairs={{0,2},{1,5},{2,0},{3,7},{4,6},{5,1},{6,4},{7,3},{8,10},{9,13},{10,... | collective-permute-start | bytes 2359304 | tf_op jit(solution)/shard_map/plane_1_second/ppermute | solution.py:23
  54.8 12.9 %collective-permute-start.11 = (bf16[2,128,1536]{2,1,0:T(8,128)(2,1)S(1)}, bf16[2,128,1536]{2,1,0:T(8,128)(2,1)S(1)}, u32[]{:S(2)}, u32[]{:S(2)}) collective-permute-start(bf16[2,128,1536]{2,1,0:T(8,128)(2,1)S(1)} %pad_maximum_fusion.3), channel_id=1, source_target_pairs={{0,4},{1,3},{2,6},{3,1},{4,0},{5,7},{6,2},{7,5},{8,12},{9,11},{10,... | collective-permute-start | bytes 2359304 | tf_op jit(solution)/shard_map/pair_first/ppermute | solution.py:23
  67.1 11.7 %collective-permute-start.15 = (bf16[512,1536]{1,0:T(8,128)(2,1)S(1)}, bf16[512,1536]{1,0:T(8,128)(2,1)S(1)}, u32[]{:S(2)}, u32[]{:S(2)}) collective-permute-start(bf16[512,1536]{1,0:T(8,128)(2,1)S(1)} %get-tuple-element.118.rest_0_), channel_id=1, source_target_pairs={{0,1},{1,0},{2,3},{3,2},{4,5},{5,4},{6,7},{7,6},{8,9},{9,8},{10,11... | collective-permute-start | bytes 4718600 | tf_op jit(solution)/shard_map/gradients_core/ppermute | solution.py:23
  67.2 11.6 %collective-permute-start.16 = (bf16[512,1536]{1,0:T(8,128)(2,1)}, bf16[512,1536]{1,0:T(8,128)(2,1)S(1)}, u32[]{:S(2)}, u32[]{:S(2)}) collective-permute-start(bf16[512,1536]{1,0:T(8,128)(2,1)} %get-tuple-element.119.rest_1_.rest_2_), channel_id=1, source_target_pairs={{0,1},{1,0},{2,3},{3,2},{4,5},{5,4},{6,7},{7,6},{8,9},{9,8},{10,11... | collective-permute-start | bytes 4718600 | tf_op jit(solution)/shard_map/gradients_core/ppermute | solution.py:23
  68.2 22.3 %collective-permute-start.14 = (bf16[2,256,1536]{2,1,0:T(8,128)(2,1)S(1)}, bf16[2,256,1536]{2,1,0:T(8,128)(2,1)}, u32[]{:S(2)}, u32[]{:S(2)}) collective-permute-start(bf16[2,256,1536]{2,1,0:T(8,128)(2,1)S(1)} %pad_maximum_fusion.rest_0_), channel_id=1, source_target_pairs={{0,2},{1,5},{2,0},{3,7},{4,6},{5,1},{6,4},{7,3},{8,10},{9,13},{10,... | collective-permute-start | bytes 4718600 | tf_op jit(solution)/shard_map/pair_second/ppermute | solution.py:23
  69.3 9.5 %copy-start.6 = (bf16[512,1536]{1,0:T(8,128)(2,1)S(1)}, bf16[512,1536]{1,0:T(8,128)(2,1)}, u32[]{:S(2)}) copy-start(bf16[512,1536]{1,0:T(8,128)(2,1)} %copy-done.5) | copy-start | bytes 4718596
  77.7 29.6 %collective-permute-start.13 = (bf16[2,256,1536]{2,1,0:T(8,128)(2,1)S(1)}, bf16[2,256,1536]{2,1,0:T(8,128)(2,1)S(1)}, u32[]{:S(2)}, u32[]{:S(2)}) collective-permute-start(bf16[2,256,1536]{2,1,0:T(8,128)(2,1)S(1)} %get-tuple-element.126), channel_id=1, source_target_pairs={{0,2},{1,5},{2,0},{3,7},{4,6},{5,1},{6,4},{7,3},{8,10},{9,13},{10,... | collective-permute-start | bytes 4718600 | tf_op jit(solution)/shard_map/sum_2/ppermute | solution.py:23
  78.8 10.7 %copy-start = (bf16[512,1536]{1,0:T(8,128)(2,1)}, bf16[512,1536]{1,0:T(8,128)(2,1)S(1)}, u32[]{:S(2)}) copy-start(bf16[512,1536]{1,0:T(8,128)(2,1)S(1)} %collective-permute-done.16.rest_3_.rest_2_) | copy-start | bytes 4718596
  93.5 15.6 %collective-permute-start.17 = (bf16[512,1536]{1,0:T(8,128)(2,1)}, bf16[512,1536]{1,0:T(8,128)(2,1)S(1)}, u32[]{:S(2)}, u32[]{:S(2)}) collective-permute-start(bf16[512,1536]{1,0:T(8,128)(2,1)} %get-tuple-element.130.rest_1_.rest_0_), channel_id=1, source_target_pairs={{0,1},{1,0},{2,3},{3,2},{4,5},{5,4},{6,7},{7,6},{8,9},{9,8},{10,11... | collective-permute-start | bytes 4718600 | tf_op jit(solution)/shard_map/gradients_core/ppermute | solution.py:23
  93.6 15.5 %collective-permute-start.18 = (bf16[512,1536]{1,0:T(8,128)(2,1)}, bf16[512,1536]{1,0:T(8,128)(2,1)}, u32[]{:S(2)}, u32[]{:S(2)}) collective-permute-start(bf16[512,1536]{1,0:T(8,128)(2,1)} %get-tuple-element.131.rest_3_.rest_1_), channel_id=1, source_target_pairs={{0,1},{1,0},{2,3},{3,2},{4,5},{5,4},{6,7},{7,6},{8,9},{9,8},{10,11... | collective-permute-start | bytes 4718600 | tf_op jit(solution)/shard_map/gradients_core/ppermute | solution.py:23
  94.1 25.8 %collective-permute-start.20 = (bf16[2,128,1536]{2,1,0:T(8,128)(2,1)S(1)}, bf16[2,128,1536]{2,1,0:T(8,128)(2,1)S(1)}, u32[]{:S(2)}, u32[]{:S(2)}) collective-permute-start(bf16[2,128,1536]{2,1,0:T(8,128)(2,1)S(1)} %get-tuple-element.134), channel_id=1, source_target_pairs={{0,2},{1,5},{2,0},{3,7},{4,6},{5,1},{6,4},{7,3},{8,10},{9,13},{10,... | collective-permute-start | bytes 2359304 | tf_op jit(solution)/shard_map/sum_1/ppermute | solution.py:23
  107.9 14.9 %collective-permute-start.21 = (bf16[256,1536]{1,0:T(8,128)(2,1)S(1)}, bf16[256,1536]{1,0:T(8,128)(2,1)S(1)}, u32[]{:S(2)}, u32[]{:S(2)}) collective-permute-start(bf16[256,1536]{1,0:T(8,128)(2,1)S(1)} %get-tuple-element.138), channel_id=1, source_target_pairs={{0,4},{1,3},{2,6},{3,1},{4,0},{5,7},{6,2},{7,5},{8,12},{9,11},{10,... | collective-permute-start | bytes 2359304 | tf_op jit(solution)/shard_map/sum_2/ppermute | solution.py:23
  109.1 10.8 %copy-start.2 = (bf16[512,1536]{1,0:T(8,128)(2,1)}, bf16[512,1536]{1,0:T(8,128)(2,1)S(1)}, u32[]{:S(2)}) copy-start(bf16[512,1536]{1,0:T(8,128)(2,1)S(1)} %collective-permute-done.17.rest_1_.rest_2_) | copy-start | bytes 4718596
  120.1 6.8 %copy-start.3 = (bf16[512,1536]{1,0:T(8,128)(2,1)S(1)}, bf16[512,1536]{1,0:T(8,128)(2,1)}, u32[]{:S(2)}) copy-start(bf16[512,1536]{1,0:T(8,128)(2,1)} %copy-done.2) | copy-start | bytes 4718596
  120.2 19.8 %collective-permute-start.25 = (bf16[128,1536]{1,0:T(8,128)(2,1)S(1)}, bf16[128,1536]{1,0:T(8,128)(2,1)S(1)}, u32[]{:S(2)}, u32[]{:S(2)}) collective-permute-start(bf16[128,1536]{1,0:T(8,128)(2,1)S(1)} %get-tuple-element.144), channel_id=1, source_target_pairs={{0,4},{1,3},{2,6},{3,1},{4,0},{5,7},{6,2},{7,5},{8,12},{9,11},{10,... | collective-permute-start | bytes 1179656 | tf_op jit(solution)/shard_map/sum_1/ppermute | solution.py:23
  121.3 20.7 %collective-permute-start.19 = (bf16[2,128,1536]{2,1,0:T(8,128)(2,1)S(1)}, bf16[2,128,1536]{2,1,0:T(8,128)(2,1)S(1)}, u32[]{:S(2)}, u32[]{:S(2)}) collective-permute-start(bf16[2,128,1536]{2,1,0:T(8,128)(2,1)S(1)} %get-tuple-element.141), channel_id=1, source_target_pairs={{0,2},{1,5},{2,0},{3,7},{4,6},{5,1},{6,4},{7,3},{8,10},{9,13},{10,... | collective-permute-start | bytes 2359304 | tf_op jit(solution)/shard_map/sum_0/ppermute | solution.py:23
  123.1 16.9 %collective-permute-start.24 = (bf16[128,1536]{1,0:T(8,128)(2,1)S(1)}, bf16[128,1536]{1,0:T(8,128)(2,1)S(1)}, u32[]{:S(2)}, u32[]{:S(2)}) collective-permute-start(bf16[128,1536]{1,0:T(8,128)(2,1)S(1)} %get-tuple-element.165), channel_id=1, source_target_pairs={{0,8},{1,9},{2,10},{3,11},{4,12},{5,13},{6,14},{7,15},{8,16},{9,17... | collective-permute-start | bytes 1179656 | tf_op jit(solution)/shard_map/sum_3_z/ppermute | solution.py:23
  123.2 18.9 %collective-permute-start.23 = (bf16[128,1536]{1,0:T(8,128)(2,1)S(1)}, bf16[128,1536]{1,0:T(8,128)(2,1)S(1)}, u32[]{:S(2)}, u32[]{:S(2)}) collective-permute-start(bf16[128,1536]{1,0:T(8,128)(2,1)S(1)} %get-tuple-element.166), channel_id=1, source_target_pairs={{0,24},{1,25},{2,26},{3,27},{4,28},{5,29},{6,30},{7,31},{8,0},{9,1... | collective-permute-start | bytes 1179656 | tf_op jit(solution)/shard_map/sum_2_z/ppermute | solution.py:23
  142.3 7.8 %collective-permute-start.22 = (bf16[128,1536]{1,0:T(8,128)(2,1)S(1)}, bf16[128,1536]{1,0:T(8,128)(2,1)S(1)}, u32[]{:S(2)}, u32[]{:S(2)}) collective-permute-start(bf16[128,1536]{1,0:T(8,128)(2,1)S(1)} %get-tuple-element.150), channel_id=1, source_target_pairs={{0,4},{1,3},{2,6},{3,1},{4,0},{5,7},{6,2},{7,5},{8,12},{9,11},{10,... | collective-permute-start | bytes 1179656 | tf_op jit(solution)/shard_map/sum_0/ppermute | solution.py:23
  144.1 9.2 %collective-permute-start.26 = (bf16[128,1536]{1,0:T(8,128)(2,1)S(1)}, bf16[128,1536]{1,0:T(8,128)(2,1)S(1)}, u32[]{:S(2)}, u32[]{:S(2)}) collective-permute-start(bf16[128,1536]{1,0:T(8,128)(2,1)S(1)} %add_add_fusion), channel_id=1, source_target_pairs={{0,24},{1,25},{2,26},{3,27},{4,28},{5,29},{6,30},{7,31},{8,0},{9,1... | collective-permute-start | bytes 1179656 | tf_op jit(solution)/shard_map/sum_1_z/ppermute | solution.py:23
  (6 other events, 13.4 us)

commit v6 on v5

--- a/solution.py
+++ b/solution.py
@@ -8,7 +8,7 @@
 
 BF16, F32 = jnp.bfloat16, jnp.float32
 ALL = ("dp", "expert")
-VMEM = 44 * 2**20
+VMEM = 36 * 2**20
 
 
 def cost(flops, moved):

time: 155 us -> 150 us (0.968)
  waiting for transfers between devices: 15.3 us -> 28.9 us
  Pallas kernels: 92.9 us -> 80.1 us
  local copies, waits for them, and re-layouts: 5.56 us -> 2.64 us
  starting transfers between devices: 33 us -> 30.9 us
    ppermute x27, waiting for transfers between devices: 15.3 us -> 28.9 us  [shift(): return lax.ppermute(block, ALL, self.perm)]
    pallas_call x4, Pallas kernels: 33.7 us -> 28.4 us  [forward_placed(): pl.pallas_call(functools.partial(place_kernel, jx, part * per, at.ny, pla...]
    unnamed x22 -> x4, local copies, waits for them, and re-layouts: 4.52 us -> 1.6 us
    pallas_call x2, Pallas kernels: 21.5 us -> 19.2 us  [weight_gradient(): pl.pallas_call(kernel, grid_spec=pltpu.PrefetchScalarGridSpec(num_scalar_...]
    ppermute x27, starting transfers between devices: 33 us -> 30.9 us  [shift(): return lax.ppermute(block, ALL, self.perm)]
    pallas_call x2, Pallas kernels: 6.36 us -> 4.18 us  [put_together(): pl.pallas_call(functools.partial(gather_kernel, plan, count), grid_spec=p...]
    pallas_call x2, Pallas kernels: 23.7 us -> 21.7 us  [hidden_gradient(): pl.pallas_call(functools.partial(hidden_kernel, steps, per, number, last)...]
  transfers between devices with their start and end apart: 27 -> 27, of which waited for: 5 -> 10; matrix products, arithmetic and copies ran while one was open for 4% -> 4% of each run, Pallas kernels for 60% -> 53%
where the time goes in v6:
time: 150 us
  Pallas kernels  80.1 us (53%)
  starting transfers between devices  30.9 us (21%)
  waiting for transfers between devices  28.9 us (19%)
  other arithmetic  6.31 us (4%)
  local copies, waits for them, and re-layouts  2.64 us (2%)
    ppermute x27, starting transfers between devices, shift(): return lax.ppermute(block, ALL, self.perm)  30.9 us
    ppermute x27, waiting for transfers between devices, shift(): return lax.ppermute(block, ALL, self.perm)  28.9 us
    pallas_call x4, Pallas kernels, forward_placed(): pl.pallas_call(functools.partial(place_kernel, jx, part * per, at.ny, pla...  28.4 us
    pallas_call x2, Pallas kernels, hidden_gradient(): pl.pallas_call(functools.partial(hidden_kernel, steps, per, number, last)...  21.7 us
    pallas_call x2, Pallas kernels, weight_gradient(): pl.pallas_call(kernel, grid_spec=pltpu.PrefetchScalarGridSpec(num_scalar_...  19.2 us
    pallas_call x1, Pallas kernels, token_rows(): pl.pallas_call(functools.partial(rows_kernel, size), grid_spec=pltpu.Pref...  6.59 us
    pallas_call x2, Pallas kernels, put_together(): pl.pallas_call(functools.partial(gather_kernel, plan, count), grid_spec=p...  4.18 us
  transfers between devices with their start and end apart: 27, of which 10 were waited for; matrix products, arithmetic and copies ran while one was open for 4% of the time, Pallas kernels for 53%

profile of v6, /device:TPU:0, one launch (start us, length us, event | category | flops | bytes accessed | tf_op | source)
XLA Modules:
  0.0 149.8 jit_solution(763708324980893679)
XLA Ops:
  2.5 2.6 %collective-permute-start = (f32[1,4,128]{2,1,0:T(4,128)S(1)}, f32[1,4,128]{2,1,0:T(4,128)S(1)}, u32[]{:S(2)}, u32[]{:S(2)}) collective-permute-start(f32[1,4,128]{2,1,0:T(4,128)S(1)} %maximum_bitcast_fusion), channel_id=1, source_target_pairs={{0,8},{1,9},{2,10},{3,11},{4,12},{5,13},{6,14},{7,15},{8,16},{9,17... | collective-permute-start | bytes 6152 | tf_op jit(solution)/shard_map/routes_z/ppermute | solution.py:23
  5.1 1.5 %collective-permute-start.1 = (bf16[128,1536]{1,0:T(8,128)(2,1)}, bf16[128,1536]{1,0:T(8,128)(2,1)S(1)}, u32[]{:S(2)}, u32[]{:S(2)}) collective-permute-start(bf16[128,1536]{1,0:T(8,128)(2,1)} %param.7), channel_id=1, source_target_pairs={{0,4},{1,3},{2,6},{3,1},{4,0},{5,7},{6,2},{7,5},{8,12},{9,11},{10,... | collective-permute-start | bytes 1179656 | tf_op jit(solution)/shard_map/own_first/ppermute | solution.py:23
  8.8 4.3 %collective-permute-done.1 = bf16[128,1536]{1,0:T(8,128)(2,1)S(1)} collective-permute-done((bf16[128,1536]{1,0:T(8,128)(2,1)}, bf16[128,1536]{1,0:T(8,128)(2,1)S(1)}, u32[]{:S(2)}, u32[]{:S(2)}) %collective-permute-start.1) | collective-permute-done | bytes 393248 | tf_op jit(solution)/shard_map/own_first/ppermute | solution.py:23
  13.1 2.6 %collective-permute-start.3 = (f32[2,4,128]{2,1,0:T(4,128)S(1)}, f32[2,4,128]{2,1,0:T(4,128)S(1)}, u32[]{:S(2)}, u32[]{:S(2)}) collective-permute-start(f32[2,4,128]{2,1,0:T(4,128)S(1)} %pad_maximum_fusion.6), channel_id=1, source_target_pairs={{0,16},{1,17},{2,18},{3,19},{4,20},{5,21},{6,22},{7,23},{8,24},{9,... | collective-permute-start | bytes 12296 | tf_op jit(solution)/shard_map/routes_z/ppermute | solution.py:23
  15.9 1.7 %collective-permute-done.3 = f32[2,4,128]{2,1,0:T(4,128)S(1)} collective-permute-done((f32[2,4,128]{2,1,0:T(4,128)S(1)}, f32[2,4,128]{2,1,0:T(4,128)S(1)}, u32[]{:S(2)}, u32[]{:S(2)}) %collective-permute-start.3) | collective-permute-done | bytes 4128 | tf_op jit(solution)/shard_map/routes_z/ppermute | solution.py:23
  17.6 1.5 %collective-permute-start.4 = (f32[4,4,128]{2,1,0:T(4,128)S(1)}, f32[4,4,128]{2,1,0:T(4,128)S(1)}, u32[]{:S(2)}, u32[]{:S(2)}) collective-permute-start(f32[4,4,128]{2,1,0:T(4,128)S(1)} %pad_maximum_fusion.5), channel_id=1, source_target_pairs={{0,4},{1,5},{2,6},{3,7},{4,0},{5,1},{6,2},{7,3},{8,12},{9,13},{10,... | collective-permute-start | bytes 24584 | tf_op jit(solution)/shard_map/routes_y/ppermute | solution.py:23
  20.2 1.6 %collective-permute-start.10 = (bf16[2,128,1536]{2,1,0:T(8,128)(2,1)S(1)}, bf16[2,128,1536]{2,1,0:T(8,128)(2,1)S(1)}, u32[]{:S(2)}, u32[]{:S(2)}) collective-permute-start(bf16[2,128,1536]{2,1,0:T(8,128)(2,1)S(1)} %pad_maximum_fusion.1.rest_0_), channel_id=1, source_target_pairs={{0,2},{1,5},{2,0},{3,7},{4,6},{5,1},{6,4},{7,3},{8,10},{9,13},{10,... | collective-permute-start | bytes 2359304 | tf_op jit(solution)/shard_map/own_second/ppermute | solution.py:23
  22.0 1.6 %copy-done = bf16[1,1024,1024]{2,1,0:T(8,128)(2,1)S(1)} copy-done((bf16[1,1024,1024]{2,1,0:T(8,128)(2,1)S(1)}, bf16[1,1024,1024]{2,1,0:T(8,128)(2,1)}, u32[]{:S(2)}) %copy-start) | copy-done | bytes 2097176
  23.6 6.6 %token_rows.1 = (bf16[2,1024,1024]{2,1,0:T(8,128)(2,1)S(1)}, bf16[1024,1024]{1,0:T(8,128)(2,1)S(1)}) custom-call(s32[8]{0:T(128)S(1)} %stack.84.shards, s32[2,8,128]{2,1,0:T(8,128)S(1)} %fusion.slots, f32[2,8,128]{2,1,0:T(8,128)S(1)} %get-tuple-element.157.gates, bf16[1024,1024]{1,0:T(8,128)(2,1)S(1)} %bitcast.52, ...), custom_call_target="tpu_custom_call" | custom-call | flops 2147483648 | bytes 8388608 | tf_op jit(solution)/shard_map/token_rows/pallas_call | solution.py:111
  30.2 1.2 collective-permute-start.8
  31.4 1.6 %collective-permute-start.6 = (bf16[128,1536]{1,0:T(8,128)(2,1)S(1)}, bf16[128,1536]{1,0:T(8,128)(2,1)S(1)}, u32[]{:S(2)}, u32[]{:S(2)}) collective-permute-start(bf16[128,1536]{1,0:T(8,128)(2,1)S(1)} %collective-permute-done.2), channel_id=1, source_target_pairs={{0,8},{1,9},{2,10},{3,11},{4,12},{5,13},{6,14},{7,15},{8,16},{9,17... | collective-permute-start | bytes 1179656 | tf_op jit(solution)/shard_map/plane_2/ppermute | solution.py:23
  33.0 2.2 %collective-permute-start.7 = (bf16[128,1536]{1,0:T(8,128)(2,1)S(1)}, bf16[128,1536]{1,0:T(8,128)(2,1)S(1)}, u32[]{:S(2)}, u32[]{:S(2)}) collective-permute-start(bf16[128,1536]{1,0:T(8,128)(2,1)S(1)} %copy-done.1), channel_id=1, source_target_pairs={{0,24},{1,25},{2,26},{3,27},{4,28},{5,29},{6,30},{7,31},{8,0},{9,1... | collective-permute-start | bytes 1179656 | tf_op jit(solution)/shard_map/plane_3/ppermute | solution.py:23
  35.2 7.1 %forward_placed.4 = (bf16[2,128,1536]{2,1,0:T(8,128)(2,1)S(1)}, bf16[2,128,1536]{2,1,0:T(8,128)(2,1)S(1)}, bf16[2,128,1536]{2,1,0:T(8,128)(2,1)S(1)}, bf16[2,128...) custom-call(s32[2]{0:T(128)S(1)} %pad_add_fusion.1.table, ...), custom_call_target="tpu_custom_call" | custom-call | flops 3221225472 | bytes 6291456 | tf_op jit(solution)/shard_map/forward_placed/pallas_call | solution.py:189
  42.4 1.6 %collective-permute-start.12 = (bf16[2,128,1536]{2,1,0:T(8,128)(2,1)S(1)}, bf16[2,128,1536]{2,1,0:T(8,128)(2,1)S(1)}, u32[]{:S(2)}, u32[]{:S(2)}) collective-permute-start(bf16[2,128,1536]{2,1,0:T(8,128)(2,1)S(1)} %pad_maximum_fusion.2.rest_2_), channel_id=1, source_target_pairs={{0,2},{1,5},{2,0},{3,7},{4,6},{5,1},{6,4},{7,3},{8,10},{9,13},{10,... | collective-permute-start | bytes 2359304 | tf_op jit(solution)/shard_map/plane_1_second/ppermute | solution.py:23
  44.0 7.1 %forward_placed.5 = (bf16[2,128,1536]{2,1,0:T(8,128)(2,1)S(1)}, bf16[2,128,1536]{2,1,0:T(8,128)(2,1)S(1)}, bf16[2,128,1536]{2,1,0:T(8,128)(2,1)S(1)}, bf16[2,128...) custom-call(s32[2]{0:T(128)S(1)} %pad_add_fusion.1.table, ...), custom_call_target="tpu_custom_call", output_to_operand_aliasing={{0}: (4, {}), {1}: (5, {}), {2}: (6, {}), {3}: (7, {}), {4}... | custom-call | flops 3221225472 | bytes 6291456 | tf_op jit(solution)/shard_map/forward_placed/pallas_call | solution.py:189
  51.9 7.1 %forward_placed.6 = (bf16[2,128,1536]{2,1,0:T(8,128)(2,1)S(1)}, bf16[2,128,1536]{2,1,0:T(8,128)(2,1)S(1)}, bf16[2,128,1536]{2,1,0:T(8,128)(2,1)S(1)}, bf16[2,128...) custom-call(s32[2]{0:T(128)S(1)} %pad_add_fusion.table, ...), custom_call_target="tpu_custom_call", output_to_operand_aliasing={{0}: (4, {}), {1}: (5, {}), {2}: (6, {}), {3}: (7, {}), {4}... | custom-call | flops 3221225472 | bytes 6291456 | tf_op jit(solution)/shard_map/forward_placed/pallas_call | solution.py:189
  59.0 3.4 %put_together.2 = (bf16[512,1536]{1,0:T(8,128)(2,1)S(1)}, bf16[512,1536]{1,0:T(8,128)(2,1)S(1)}) custom-call(s32[1]{0:T(128)} %bitcast.swapped, bf16[2,128,1536]{2,1,0:T(8,128)(2,1)S(1)} %pad_maximum_fusion.1.rest_0_, bf16[2,128,1536]{2,1,0:T(8,128)(2,1)S(1)} %collective-permute-done.10.rest_1_, bf16[2,128,1536]{2,1,0:T(8,128)(2,1)S(1)} %pad_maximum_fusion.2.rest_2_, ...), custom_call_target="tpu_custom_call" | custom-call | bytes 6291456 | tf_op jit(solution)/shard_map/put_together/pallas_call | solution.py:242
  64.1 7.1 %forward_placed.7 = (bf16[2,128,1536]{2,1,0:T(8,128)(2,1)S(1)}, bf16[2,128,1536]{2,1,0:T(8,128)(2,1)S(1)}, bf16[2,128,1536]{2,1,0:T(8,128)(2,1)S(1)}, bf16[2,128...) custom-call(s32[2]{0:T(128)S(1)} %pad_add_fusion.table, ...), custom_call_target="tpu_custom_call", output_to_operand_aliasing={{0}: (4, {}), {1}: (5, {}), {2}: (6, {}), {3}: (7, {}), {4}... | custom-call | flops 3221225472 | bytes 6291456 | tf_op jit(solution)/shard_map/forward_placed/pallas_call | solution.py:189
  71.2 1.5 %collective-permute-start.13 = (bf16[2,256,1536]{2,1,0:T(8,128)(2,1)S(1)}, bf16[2,256,1536]{2,1,0:T(8,128)(2,1)S(1)}, u32[]{:S(2)}, u32[]{:S(2)}) collective-permute-start(bf16[2,256,1536]{2,1,0:T(8,128)(2,1)S(1)} %get-tuple-element.126), channel_id=1, source_target_pairs={{0,2},{1,5},{2,0},{3,7},{4,6},{5,1},{6,4},{7,3},{8,10},{9,13},{10,... | collective-permute-start | bytes 4718600 | tf_op jit(solution)/shard_map/sum_2/ppermute | solution.py:23
  72.7 10.2 %hidden_gradient.2.rest_4_ = bf16[512,1024]{1,0:T(8,128)(2,1)S(1)} custom-call(s32[12]{0:T(128)S(1)} %concatenate.28.table, f32[4,128]{1,0:T(4,128)S(1)} %get-tuple-element.172.gates, s32[4,128]{1,0:T(4,128)S(1)} %get-tuple-element.170.slots, bf16[1024,6144]{1,0:T(8,128)(2,1)} %bitcast.58, bf16[512,1536]{1,0:T(8,128)(2,1)S(1)} %get-tuple-element.118.rest_0_, ...), custom_call_target="tpu_custom_call" | custom-call | flops 6442450944 | bytes 18874368 | tf_op jit(solution)/shard_map/hidden_gradient/pallas_call | solution.py:385
  85.8 9.6 %weight_gradient.2.rest_4_ = bf16[1024,6144]{1,0:T(8,128)(2,1)} custom-call(s32[2]{0:T(128)S(1)} %get-tuple-element.135.quarters, bf16[1024,1024]{1,0:T(8,128)(2,1)S(1)} %get-tuple-element.136.turned, bf16[512,1536]{1,0:T(8,128)(2,1)S(1)} %get-tuple-element.118.rest_0_, bf16[512,1536]{1,0:T(8,128)(2,1)S(1)} %get-tuple-element.130.rest_1_.rest_0_, ...), custom_call_target="tpu_custom_call" | custom-call | flops 6442450944 | bytes 12582912 | tf_op jit(solution)/shard_map/weight_gradient/pallas_call | solution.py:304
  95.4 5.3 %collective-permute-done.13 = bf16[2,256,1536]{2,1,0:T(8,128)(2,1)S(1)} collective-permute-done((bf16[2,256,1536]{2,1,0:T(8,128)(2,1)S(1)}, bf16[2,256,1536]{2,1,0:T(8,128)(2,1)S(1)}, u32[]{:S(2)}, u32[]{:S(2)}) %collective-permute-start.13) | collective-permute-done | bytes 1572896 | tf_op jit(solution)/shard_map/sum_2/ppermute | solution.py:23
  101.3 1.2 collective-permute-start.21
  102.5 9.6 %weight_gradient.3 = bf16[1024,6144]{1,0:T(8,128)(2,1)} custom-call(s32[2]{0:T(128)S(1)} %get-tuple-element.139.quarters, bf16[1024,1024]{1,0:T(8,128)(2,1)S(1)} %get-tuple-element.136.turned, bf16[512,1536]{1,0:T(8,128)(2,1)S(1)} %collective-permute-done.15.rest_2_.rest_0_, ...), custom_call_target="tpu_custom_call", output_to_operand_aliasing={{}: (6, {})} | custom-call | flops 6442450944 | bytes 12582912 | tf_op jit(solution)/shard_map/weight_gradient/pallas_call | solution.py:304
  112.1 3.3 %collective-permute-done.20 = bf16[2,128,1536]{2,1,0:T(8,128)(2,1)S(1)} collective-permute-done((bf16[2,128,1536]{2,1,0:T(8,128)(2,1)S(1)}, bf16[2,128,1536]{2,1,0:T(8,128)(2,1)S(1)}, u32[]{:S(2)}, u32[]{:S(2)}) %collective-permute-start.20) | collective-permute-done | bytes 786464 | tf_op jit(solution)/shard_map/sum_1/ppermute | solution.py:23
  117.6 2.2 %collective-permute-start.24 = (bf16[128,1536]{1,0:T(8,128)(2,1)S(1)}, bf16[128,1536]{1,0:T(8,128)(2,1)S(1)}, u32[]{:S(2)}, u32[]{:S(2)}) collective-permute-start(bf16[128,1536]{1,0:T(8,128)(2,1)S(1)} %get-tuple-element.165), channel_id=1, source_target_pairs={{0,8},{1,9},{2,10},{3,11},{4,12},{5,13},{6,14},{7,15},{8,16},{9,17... | collective-permute-start | bytes 1179656 | tf_op jit(solution)/shard_map/sum_3_z/ppermute | solution.py:23
  119.8 1.6 %collective-permute-start.23 = (bf16[128,1536]{1,0:T(8,128)(2,1)S(1)}, bf16[128,1536]{1,0:T(8,128)(2,1)S(1)}, u32[]{:S(2)}, u32[]{:S(2)}) collective-permute-start(bf16[128,1536]{1,0:T(8,128)(2,1)S(1)} %get-tuple-element.166), channel_id=1, source_target_pairs={{0,24},{1,25},{2,26},{3,27},{4,28},{5,29},{6,30},{7,31},{8,0},{9,1... | collective-permute-start | bytes 1179656 | tf_op jit(solution)/shard_map/sum_2_z/ppermute | solution.py:23
  121.5 11.5 %hidden_gradient.3 = bf16[1024,1024]{1,0:T(8,128)(2,1)} custom-call(s32[12]{0:T(128)S(1)} %concatenate.28.table, f32[4,128]{1,0:T(4,128)S(1)} %get-tuple-element.171.gates, s32[4,128]{1,0:T(4,128)S(1)} %get-tuple-element.169.slots, bf16[1024,6144]{1,0:T(8,128)(2,1)} %bitcast.59, bf16[512,1536]{1,0:T(8,128)(2,1)S(1)} %get-tuple-element.130.rest_1_.rest_0_, ...), custom_call_target="tpu_custom_call" | custom-call | flops 6442450944 | bytes 18874368 | tf_op jit(solution)/shard_map/hidden_gradient/pallas_call | solution.py:385
  133.0 5.3 %collective-permute-done.23 = bf16[128,1536]{1,0:T(8,128)(2,1)S(1)} collective-permute-done((bf16[128,1536]{1,0:T(8,128)(2,1)S(1)}, bf16[128,1536]{1,0:T(8,128)(2,1)S(1)}, u32[]{:S(2)}, u32[]{:S(2)}) %collective-permute-start.23) | collective-permute-done | bytes 393248 | tf_op jit(solution)/shard_map/sum_2_z/ppermute | solution.py:23
  139.4 2.0 %collective-permute-start.26 = (bf16[128,1536]{1,0:T(8,128)(2,1)S(1)}, bf16[128,1536]{1,0:T(8,128)(2,1)S(1)}, u32[]{:S(2)}, u32[]{:S(2)}) collective-permute-start(bf16[128,1536]{1,0:T(8,128)(2,1)S(1)} %add_add_fusion), channel_id=1, source_target_pairs={{0,24},{1,25},{2,26},{3,27},{4,28},{5,29},{6,30},{7,31},{8,0},{9,1... | collective-permute-start | bytes 1179656 | tf_op jit(solution)/shard_map/sum_1_z/ppermute | solution.py:23
  141.3 5.0 %collective-permute-done.22 = bf16[128,1536]{1,0:T(8,128)(2,1)S(1)} collective-permute-done((bf16[128,1536]{1,0:T(8,128)(2,1)S(1)}, bf16[128,1536]{1,0:T(8,128)(2,1)S(1)}, u32[]{:S(2)}, u32[]{:S(2)}) %collective-permute-start.22) | collective-permute-done | bytes 393248 | tf_op jit(solution)/shard_map/sum_0/ppermute | solution.py:23
  146.4 2.5 %collective-permute-done.26 = bf16[128,1536]{1,0:T(8,128)(2,1)S(1)} collective-permute-done((bf16[128,1536]{1,0:T(8,128)(2,1)S(1)}, bf16[128,1536]{1,0:T(8,128)(2,1)S(1)}, u32[]{:S(2)}, u32[]{:S(2)}) %collective-permute-start.26) | collective-permute-done | bytes 393248 | tf_op jit(solution)/shard_map/sum_1_z/ppermute | solution.py:23
  (71 shorter events, 15.6 us)
Async XLA Ops:
  0.6 12.5 %collective-permute-start.5 = (bf16[1024,1024]{1,0:T(8,128)(2,1)}, bf16[1024,1024]{1,0:T(8,128)(2,1)}, u32[]{:S(2)}, u32[]{:S(2)}) collective-permute-start(bf16[1024,1024]{1,0:T(8,128)(2,1)} %bitcast.51), channel_id=1, source_target_pairs={{0,1},{1,0},{2,3},{3,2},{4,5},{5,4},{6,7},{7,6},{8,9},{9,8},{10,11... | collective-permute-start | bytes 6291464 | tf_op jit(solution)/shard_map/hidden_core/ppermute | solution.py:23
  2.5 6.2 %collective-permute-start = (f32[1,4,128]{2,1,0:T(4,128)S(1)}, f32[1,4,128]{2,1,0:T(4,128)S(1)}, u32[]{:S(2)}, u32[]{:S(2)}) collective-permute-start(f32[1,4,128]{2,1,0:T(4,128)S(1)} %maximum_bitcast_fusion), channel_id=1, source_target_pairs={{0,8},{1,9},{2,10},{3,11},{4,12},{5,13},{6,14},{7,15},{8,16},{9,17... | collective-permute-start | bytes 6152 | tf_op jit(solution)/shard_map/routes_z/ppermute | solution.py:23
  5.1 8.0 %collective-permute-start.1 = (bf16[128,1536]{1,0:T(8,128)(2,1)}, bf16[128,1536]{1,0:T(8,128)(2,1)S(1)}, u32[]{:S(2)}, u32[]{:S(2)}) collective-permute-start(bf16[128,1536]{1,0:T(8,128)(2,1)} %param.7), channel_id=1, source_target_pairs={{0,4},{1,3},{2,6},{3,1},{4,0},{5,7},{6,2},{7,5},{8,12},{9,11},{10,... | collective-permute-start | bytes 1179656 | tf_op jit(solution)/shard_map/own_first/ppermute | solution.py:23
  13.1 22.1 %collective-permute-start.9 = (bf16[1024,6144]{1,0:T(8,128)(2,1)}, bf16[1024,6144]{1,0:T(8,128)(2,1)}, u32[]{:S(2)}, u32[]{:S(2)}) collective-permute-start(bf16[1024,6144]{1,0:T(8,128)(2,1)} %bitcast.53), channel_id=1, source_target_pairs={{0,1},{1,0},{2,3},{3,2},{4,5},{5,4},{6,7},{7,6},{8,9},{9,8},{10,11... | collective-permute-start | bytes 37748744 | tf_op jit(solution)/shard_map/weight_core/ppermute | solution.py:23
  13.1 4.5 %collective-permute-start.3 = (f32[2,4,128]{2,1,0:T(4,128)S(1)}, f32[2,4,128]{2,1,0:T(4,128)S(1)}, u32[]{:S(2)}, u32[]{:S(2)}) collective-permute-start(f32[2,4,128]{2,1,0:T(4,128)S(1)} %pad_maximum_fusion.6), channel_id=1, source_target_pairs={{0,16},{1,17},{2,18},{3,19},{4,20},{5,21},{6,22},{7,23},{8,24},{9,... | collective-permute-start | bytes 12296 | tf_op jit(solution)/shard_map/routes_z/ppermute | solution.py:23
  15.9 14.4 %collective-permute-start.2 = (bf16[128,1536]{1,0:T(8,128)(2,1)}, bf16[128,1536]{1,0:T(8,128)(2,1)S(1)}, u32[]{:S(2)}, u32[]{:S(2)}) collective-permute-start(bf16[128,1536]{1,0:T(8,128)(2,1)} %param.7), channel_id=1, source_target_pairs={{0,8},{1,9},{2,10},{3,11},{4,12},{5,13},{6,14},{7,15},{8,16},{9,17... | collective-permute-start | bytes 1179656 | tf_op jit(solution)/shard_map/plane_1/ppermute | solution.py:23
  17.6 4.2 %collective-permute-start.4 = (f32[4,4,128]{2,1,0:T(4,128)S(1)}, f32[4,4,128]{2,1,0:T(4,128)S(1)}, u32[]{:S(2)}, u32[]{:S(2)}) collective-permute-start(f32[4,4,128]{2,1,0:T(4,128)S(1)} %pad_maximum_fusion.5), channel_id=1, source_target_pairs={{0,4},{1,5},{2,6},{3,7},{4,0},{5,1},{6,2},{7,3},{8,12},{9,13},{10,... | collective-permute-start | bytes 24584 | tf_op jit(solution)/shard_map/routes_y/ppermute | solution.py:23
  20.2 23.8 %collective-permute-start.10 = (bf16[2,128,1536]{2,1,0:T(8,128)(2,1)S(1)}, bf16[2,128,1536]{2,1,0:T(8,128)(2,1)S(1)}, u32[]{:S(2)}, u32[]{:S(2)}) collective-permute-start(bf16[2,128,1536]{2,1,0:T(8,128)(2,1)S(1)} %pad_maximum_fusion.1.rest_0_), channel_id=1, source_target_pairs={{0,2},{1,5},{2,0},{3,7},{4,6},{5,1},{6,4},{7,3},{8,10},{9,13},{10,... | collective-permute-start | bytes 2359304 | tf_op jit(solution)/shard_map/own_second/ppermute | solution.py:23
  22.0 1.6 %copy-start = (bf16[1,1024,1024]{2,1,0:T(8,128)(2,1)S(1)}, bf16[1,1024,1024]{2,1,0:T(8,128)(2,1)}, u32[]{:S(2)}) copy-start(bf16[1,1024,1024]{2,1,0:T(8,128)(2,1)} %param.5) | copy-start | bytes 6291460
  23.6 9.4 %copy-start.1 = (bf16[128,1536]{1,0:T(8,128)(2,1)S(1)}, bf16[128,1536]{1,0:T(8,128)(2,1)}, u32[]{:S(2)}) copy-start(bf16[128,1536]{1,0:T(8,128)(2,1)} %param.7) | copy-start | bytes 1179652
  30.2 12.1 %collective-permute-start.8 = (bf16[128,1536]{1,0:T(8,128)(2,1)S(1)}, bf16[128,1536]{1,0:T(8,128)(2,1)S(1)}, u32[]{:S(2)}, u32[]{:S(2)}) collective-permute-start(bf16[128,1536]{1,0:T(8,128)(2,1)S(1)} %collective-permute-done.2), channel_id=1, source_target_pairs={{0,4},{1,3},{2,6},{3,1},{4,0},{5,7},{6,2},{7,5},{8,12},{9,11},{10,... | collective-permute-start | bytes 1179656 | tf_op jit(solution)/shard_map/plane_1_first/ppermute | solution.py:23
  31.4 19.7 %collective-permute-start.6 = (bf16[128,1536]{1,0:T(8,128)(2,1)S(1)}, bf16[128,1536]{1,0:T(8,128)(2,1)S(1)}, u32[]{:S(2)}, u32[]{:S(2)}) collective-permute-start(bf16[128,1536]{1,0:T(8,128)(2,1)S(1)} %collective-permute-done.2), channel_id=1, source_target_pairs={{0,8},{1,9},{2,10},{3,11},{4,12},{5,13},{6,14},{7,15},{8,16},{9,17... | collective-permute-start | bytes 1179656 | tf_op jit(solution)/shard_map/plane_2/ppermute | solution.py:23
  33.0 18.1 %collective-permute-start.7 = (bf16[128,1536]{1,0:T(8,128)(2,1)S(1)}, bf16[128,1536]{1,0:T(8,128)(2,1)S(1)}, u32[]{:S(2)}, u32[]{:S(2)}) collective-permute-start(bf16[128,1536]{1,0:T(8,128)(2,1)S(1)} %copy-done.1), channel_id=1, source_target_pairs={{0,24},{1,25},{2,26},{3,27},{4,28},{5,29},{6,30},{7,31},{8,0},{9,1... | collective-permute-start | bytes 1179656 | tf_op jit(solution)/shard_map/plane_3/ppermute | solution.py:23
  42.4 16.6 %collective-permute-start.12 = (bf16[2,128,1536]{2,1,0:T(8,128)(2,1)S(1)}, bf16[2,128,1536]{2,1,0:T(8,128)(2,1)S(1)}, u32[]{:S(2)}, u32[]{:S(2)}) collective-permute-start(bf16[2,128,1536]{2,1,0:T(8,128)(2,1)S(1)} %pad_maximum_fusion.2.rest_2_), channel_id=1, source_target_pairs={{0,2},{1,5},{2,0},{3,7},{4,6},{5,1},{6,4},{7,3},{8,10},{9,13},{10,... | collective-permute-start | bytes 2359304 | tf_op jit(solution)/shard_map/plane_1_second/ppermute | solution.py:23
  51.2 12.1 %collective-permute-start.11 = (bf16[2,128,1536]{2,1,0:T(8,128)(2,1)S(1)}, bf16[2,128,1536]{2,1,0:T(8,128)(2,1)S(1)}, u32[]{:S(2)}, u32[]{:S(2)}) collective-permute-start(bf16[2,128,1536]{2,1,0:T(8,128)(2,1)S(1)} %pad_maximum_fusion.3), channel_id=1, source_target_pairs={{0,4},{1,3},{2,6},{3,1},{4,0},{5,7},{6,2},{7,5},{8,12},{9,11},{10,... | collective-permute-start | bytes 2359304 | tf_op jit(solution)/shard_map/pair_first/ppermute | solution.py:23
  62.5 10.3 %collective-permute-start.15 = (bf16[512,1536]{1,0:T(8,128)(2,1)S(1)}, bf16[512,1536]{1,0:T(8,128)(2,1)S(1)}, u32[]{:S(2)}, u32[]{:S(2)}) collective-permute-start(bf16[512,1536]{1,0:T(8,128)(2,1)S(1)} %get-tuple-element.118.rest_0_), channel_id=1, source_target_pairs={{0,1},{1,0},{2,3},{3,2},{4,5},{5,4},{6,7},{7,6},{8,9},{9,8},{10,11... | collective-permute-start | bytes 4718600 | tf_op jit(solution)/shard_map/gradients_core/ppermute | solution.py:23
  62.5 10.2 %collective-permute-start.16 = (bf16[512,1536]{1,0:T(8,128)(2,1)S(1)}, bf16[512,1536]{1,0:T(8,128)(2,1)S(1)}, u32[]{:S(2)}, u32[]{:S(2)}) collective-permute-start(bf16[512,1536]{1,0:T(8,128)(2,1)S(1)} %get-tuple-element.119.rest_1_.rest_2_), channel_id=1, source_target_pairs={{0,1},{1,0},{2,3},{3,2},{4,5},{5,4},{6,7},{7,6},{8,9},{9,8},{10,11... | collective-permute-start | bytes 4718600 | tf_op jit(solution)/shard_map/gradients_core/ppermute | solution.py:23
  63.4 20.5 %collective-permute-start.14 = (bf16[2,256,1536]{2,1,0:T(8,128)(2,1)S(1)}, bf16[2,256,1536]{2,1,0:T(8,128)(2,1)S(1)}, u32[]{:S(2)}, u32[]{:S(2)}) collective-permute-start(bf16[2,256,1536]{2,1,0:T(8,128)(2,1)S(1)} %pad_maximum_fusion.rest_0_), channel_id=1, source_target_pairs={{0,2},{1,5},{2,0},{3,7},{4,6},{5,1},{6,4},{7,3},{8,10},{9,13},{10,... | collective-permute-start | bytes 4718600 | tf_op jit(solution)/shard_map/pair_second/ppermute | solution.py:23
  71.2 29.6 %collective-permute-start.13 = (bf16[2,256,1536]{2,1,0:T(8,128)(2,1)S(1)}, bf16[2,256,1536]{2,1,0:T(8,128)(2,1)S(1)}, u32[]{:S(2)}, u32[]{:S(2)}) collective-permute-start(bf16[2,256,1536]{2,1,0:T(8,128)(2,1)S(1)} %get-tuple-element.126), channel_id=1, source_target_pairs={{0,2},{1,5},{2,0},{3,7},{4,6},{5,1},{6,4},{7,3},{8,10},{9,13},{10,... | collective-permute-start | bytes 4718600 | tf_op jit(solution)/shard_map/sum_2/ppermute | solution.py:23
  84.7 17.8 %collective-permute-start.17 = (bf16[512,1536]{1,0:T(8,128)(2,1)S(1)}, bf16[512,1536]{1,0:T(8,128)(2,1)S(1)}, u32[]{:S(2)}, u32[]{:S(2)}) collective-permute-start(bf16[512,1536]{1,0:T(8,128)(2,1)S(1)} %get-tuple-element.130.rest_1_.rest_0_), channel_id=1, source_target_pairs={{0,1},{1,0},{2,3},{3,2},{4,5},{5,4},{6,7},{7,6},{8,9},{9,8},{10,11... | collective-permute-start | bytes 4718600 | tf_op jit(solution)/shard_map/gradients_core/ppermute | solution.py:23
  84.8 17.7 %collective-permute-start.18 = (bf16[512,1536]{1,0:T(8,128)(2,1)S(1)}, bf16[512,1536]{1,0:T(8,128)(2,1)S(1)}, u32[]{:S(2)}, u32[]{:S(2)}) collective-permute-start(bf16[512,1536]{1,0:T(8,128)(2,1)S(1)} %get-tuple-element.131.rest_3_.rest_1_), channel_id=1, source_target_pairs={{0,1},{1,0},{2,3},{3,2},{4,5},{5,4},{6,7},{7,6},{8,9},{9,8},{10,11... | collective-permute-start | bytes 4718600 | tf_op jit(solution)/shard_map/gradients_core/ppermute | solution.py:23
  85.3 30.1 %collective-permute-start.20 = (bf16[2,128,1536]{2,1,0:T(8,128)(2,1)S(1)}, bf16[2,128,1536]{2,1,0:T(8,128)(2,1)S(1)}, u32[]{:S(2)}, u32[]{:S(2)}) collective-permute-start(bf16[2,128,1536]{2,1,0:T(8,128)(2,1)S(1)} %get-tuple-element.134), channel_id=1, source_target_pairs={{0,2},{1,5},{2,0},{3,7},{4,6},{5,1},{6,4},{7,3},{8,10},{9,13},{10,... | collective-permute-start | bytes 2359304 | tf_op jit(solution)/shard_map/sum_1/ppermute | solution.py:23
  101.3 16.1 %collective-permute-start.21 = (bf16[256,1536]{1,0:T(8,128)(2,1)S(1)}, bf16[256,1536]{1,0:T(8,128)(2,1)S(1)}, u32[]{:S(2)}, u32[]{:S(2)}) collective-permute-start(bf16[256,1536]{1,0:T(8,128)(2,1)S(1)} %get-tuple-element.138), channel_id=1, source_target_pairs={{0,4},{1,3},{2,6},{3,1},{4,0},{5,7},{6,2},{7,5},{8,12},{9,11},{10,... | collective-permute-start | bytes 2359304 | tf_op jit(solution)/shard_map/sum_2/ppermute | solution.py:23
  115.7 17.3 %collective-permute-start.25 = (bf16[128,1536]{1,0:T(8,128)(2,1)S(1)}, bf16[128,1536]{1,0:T(8,128)(2,1)S(1)}, u32[]{:S(2)}, u32[]{:S(2)}) collective-permute-start(bf16[128,1536]{1,0:T(8,128)(2,1)S(1)} %get-tuple-element.144), channel_id=1, source_target_pairs={{0,4},{1,3},{2,6},{3,1},{4,0},{5,7},{6,2},{7,5},{8,12},{9,11},{10,... | collective-permute-start | bytes 1179656 | tf_op jit(solution)/shard_map/sum_1/ppermute | solution.py:23
  116.6 21.6 %collective-permute-start.19 = (bf16[2,128,1536]{2,1,0:T(8,128)(2,1)S(1)}, bf16[2,128,1536]{2,1,0:T(8,128)(2,1)S(1)}, u32[]{:S(2)}, u32[]{:S(2)}) collective-permute-start(bf16[2,128,1536]{2,1,0:T(8,128)(2,1)S(1)} %get-tuple-element.141), channel_id=1, source_target_pairs={{0,2},{1,5},{2,0},{3,7},{4,6},{5,1},{6,4},{7,3},{8,10},{9,13},{10,... | collective-permute-start | bytes 2359304 | tf_op jit(solution)/shard_map/sum_0/ppermute | solution.py:23
  117.6 15.4 %collective-permute-start.24 = (bf16[128,1536]{1,0:T(8,128)(2,1)S(1)}, bf16[128,1536]{1,0:T(8,128)(2,1)S(1)}, u32[]{:S(2)}, u32[]{:S(2)}) collective-permute-start(bf16[128,1536]{1,0:T(8,128)(2,1)S(1)} %get-tuple-element.165), channel_id=1, source_target_pairs={{0,8},{1,9},{2,10},{3,11},{4,12},{5,13},{6,14},{7,15},{8,16},{9,17... | collective-permute-start | bytes 1179656 | tf_op jit(solution)/shard_map/sum_3_z/ppermute | solution.py:23
  119.8 18.4 %collective-permute-start.23 = (bf16[128,1536]{1,0:T(8,128)(2,1)S(1)}, bf16[128,1536]{1,0:T(8,128)(2,1)S(1)}, u32[]{:S(2)}, u32[]{:S(2)}) collective-permute-start(bf16[128,1536]{1,0:T(8,128)(2,1)S(1)} %get-tuple-element.166), channel_id=1, source_target_pairs={{0,24},{1,25},{2,26},{3,27},{4,28},{5,29},{6,30},{7,31},{8,0},{9,1... | collective-permute-start | bytes 1179656 | tf_op jit(solution)/shard_map/sum_2_z/ppermute | solution.py:23
  138.5 7.8 %collective-permute-start.22 = (bf16[128,1536]{1,0:T(8,128)(2,1)S(1)}, bf16[128,1536]{1,0:T(8,128)(2,1)S(1)}, u32[]{:S(2)}, u32[]{:S(2)}) collective-permute-start(bf16[128,1536]{1,0:T(8,128)(2,1)S(1)} %get-tuple-element.150), channel_id=1, source_target_pairs={{0,4},{1,3},{2,6},{3,1},{4,0},{5,7},{6,2},{7,5},{8,12},{9,11},{10,... | collective-permute-start | bytes 1179656 | tf_op jit(solution)/shard_map/sum_0/ppermute | solution.py:23
  139.4 9.5 %collective-permute-start.26 = (bf16[128,1536]{1,0:T(8,128)(2,1)S(1)}, bf16[128,1536]{1,0:T(8,128)(2,1)S(1)}, u32[]{:S(2)}, u32[]{:S(2)}) collective-permute-start(bf16[128,1536]{1,0:T(8,128)(2,1)S(1)} %add_add_fusion), channel_id=1, source_target_pairs={{0,24},{1,25},{2,26},{3,27},{4,28},{5,29},{6,30},{7,31},{8,0},{9,1... | collective-permute-start | bytes 1179656 | tf_op jit(solution)/shard_map/sum_1_z/ppermute | solution.py:23
